TPU v7x, 32 devices: a whole 2x2x4 slice. The times are simulated.
32 devices in a mesh: wide: 16 (over z, y, core), pair: 2 (over x).
Axes of the slice: x: 2, y: 2, z: 4, core: 2. Of those that a mesh axis runs over, the one named last changes fastest.
Arguments:
- queries: bfloat16 [2, 16, 2, 8192], P('pair', 'wide'), may hold values from -200 to 200
- cache: bfloat16 [2, 16, 512, 2, 1024], P('pair', 'wide'), may hold values from -10 to 10
- fresh_key_value: bfloat16 [2, 16, 2, 2, 1024], P('pair', 'wide'), may hold values from -15 to 15
- lengths: int32 [2, 16], P('pair', 'wide'), may hold values from 64 to 510, as said below
- residual: bfloat16 [2, 16, 2, 8192], P('pair', 'wide'), may hold values from -10 to 10
- norm_gain: float32 [8192], replicated, may hold values from 0.5 to 1.5
- vocab_weight: bfloat16 [8192, 4096], P('pair', 'wide'), may hold values from -0.5 to 0.5
- guidance: float32 [16], replicated, may hold values from 2 to 5
- allowed_blocks: int32 [2, 16, 128], P(None, 'pair', 'wide'), may hold values from 0 to 1, as said below
- sampled: int32 [2, 16], P(None, 'pair'), may hold values from 0 to 4095
Outputs:
- guided_logprobs: float32 [2, 16, 4096], P(None, 'pair', 'wide')
- token_logprobs: float32 [2, 16], P(None, 'pair')
Inputs may be any that keep to these rules, and one draw needn't show every extreme that they name: `lengths`: the longest row holds exactly 510 live slots. `allowed_blocks`: the block of each sampled id is allowed.
All inputs are finite; a program needn't handle non-finite values.
Results may differ from a plain program's by a relative error of at most 0.0022.
Values may be sent and summed in bfloat16 or wider, within the bound.
No kernel may reach another device: no remote copies, remote signals or barrier semaphores. Data moves between devices by JAX's collectives and lax.ppermute only.
A program may use at most 64 MiB of HBM per device.

v0:
```python
import math

import jax
import jax.numpy as jnp
from jax import lax
from jax.sharding import PartitionSpec as P

QUERY_HEADS = 64
KEY_VALUE_HEADS = 8
HEAD_SIZE = 128
BLK = 32
DECODE_STEPS = 2


NEG_FILL = -1e30


def attend_local(queries, cache, fresh_key_value, lengths):
    query_group = QUERY_HEADS // KEY_VALUE_HEADS
    factor = 1.0 / math.sqrt(HEAD_SIZE)
    slot_positions = cache.shape[2]
    key_rows = cache[0, 0, :, 0].reshape(slot_positions, KEY_VALUE_HEADS, HEAD_SIZE)
    value_rows = cache[0, 0, :, 1].reshape(slot_positions, KEY_VALUE_HEADS, HEAD_SIZE)
    appended_keys = fresh_key_value[0, 0, :, 0].reshape(DECODE_STEPS, KEY_VALUE_HEADS, HEAD_SIZE)
    appended_values = fresh_key_value[0, 0, :, 1].reshape(DECODE_STEPS, KEY_VALUE_HEADS, HEAD_SIZE)
    live = jnp.arange(slot_positions) < lengths[0, 0]
    outputs = []
    for index_of_step in range(DECODE_STEPS):
        query_vector = queries[0, 0, index_of_step].reshape(KEY_VALUE_HEADS, query_group, HEAD_SIZE)
        old = (
            jnp.einsum("kgd,ckd->kgc", query_vector, key_rows, preferred_element_type=jnp.float32)
            * factor
        )
        old = jnp.where(live[None, None, :], old, -jnp.inf)
        new = (
            jnp.einsum(
                "kgd,skd->kgs",
                query_vector,
                appended_keys[: index_of_step + 1],
                preferred_element_type=jnp.float32,
            )
            * factor
        )
        top = jnp.maximum(jnp.max(old, axis=-1), jnp.max(new, axis=-1))
        old_weight = jnp.exp(old - top[..., None])
        new_weight = jnp.exp(new - top[..., None])
        total = jnp.sum(old_weight, axis=-1) + jnp.sum(new_weight, axis=-1)
        old_weight = (old_weight / total[..., None]).astype(jnp.bfloat16)
        new_weight = (new_weight / total[..., None]).astype(jnp.bfloat16)
        mixed = jnp.einsum(
            "kgc,ckd->kgd", old_weight, value_rows, preferred_element_type=jnp.float32
        )
        mixed = mixed + jnp.einsum(
            "kgs,skd->kgd",
            new_weight,
            appended_values[: index_of_step + 1],
            preferred_element_type=jnp.float32,
        )
        outputs.append(mixed.reshape(QUERY_HEADS * HEAD_SIZE))
    return jnp.stack(outputs)


def shards(
    queries,
    cache,
    fresh_key_value,
    lengths,
    residual,
    norm_gain,
    vocab_weight,
    guidance,
    allowed_blocks,
    sampled,
):
    attended = attend_local(queries, cache, fresh_key_value, lengths)
    hidden = residual[0, 0].astype(jnp.float32) + attended
    power = jnp.mean(hidden * hidden, axis=-1, keepdims=True)
    normed = (hidden * lax.rsqrt(power + 1e-05) * norm_gain).astype(jnp.bfloat16)[:, None, :]
    half_pairs = allowed_blocks.shape[1]
    vocab_width = vocab_weight.shape[1]
    columns = lax.axis_index("wide") * vocab_width + jnp.arange(vocab_width)

    def finish(row_block, first, count):
        swapped = lax.all_to_all(row_block, "pair", split_axis=2, concat_axis=1, tiled=True)
        spread = swapped[:, :, None, :]
        masks = allowed_blocks[first : first + count]
        chosen = sampled[first : first + count]
        both_logits = jnp.einsum(
            "sbnd,dv->sbnv",
            lax.all_gather(spread, "wide", axis=2, tiled=True),
            vocab_weight,
            preferred_element_type=jnp.float32,
        )
        summed = lax.psum_scatter(both_logits, "pair", scatter_dimension=2, tiled=True)
        scale_mine = lax.dynamic_slice_in_dim(
            guidance, lax.axis_index("pair") * half_pairs, half_pairs, 0
        )
        guided = summed[:, 1] + scale_mine[None, :, None] * (summed[:, 0] - summed[:, 1])
        allowed = jnp.broadcast_to(masks[..., None] > 0, masks.shape + (BLK,)).reshape(
            count, half_pairs, vocab_width
        )
        local_top = jnp.max(jnp.where(allowed, guided, NEG_FILL), axis=-1)
        hit = columns[None, None, :] == chosen[..., None]
        picked_local = jnp.sum(jnp.where(hit, guided, 0.0), axis=-1)
        top = lax.pmax(local_top, "wide")
        local_total = jnp.sum(jnp.where(allowed, jnp.exp(guided - top[..., None]), 0.0), axis=-1)
        total, picked = lax.psum((local_total, picked_local), "wide")
        normalizer = top + jnp.log(total)
        logprob = jnp.where(allowed, guided - normalizer[..., None], 0.0)
        return (logprob, picked - normalizer)

    results = [
        finish(normed[index_of_step : index_of_step + 1], index_of_step, 1)
        for index_of_step in range(DECODE_STEPS)
    ]
    guided_logprobs = jnp.concatenate([entry[0] for entry in results], axis=0)
    token_logprobs = jnp.concatenate([entry[1] for entry in results], axis=0)
    return (guided_logprobs, token_logprobs)


def solution(mesh):
    placed = (
        P("pair", "wide", None, None),
        P("pair", "wide", None, None, None),
        P("pair", "wide", None, None, None),
        P("pair", "wide"),
        P("pair", "wide", None, None),
        P(),
        P("pair", "wide"),
        P(),
        P(None, "pair", "wide"),
        P(None, "pair"),
    )
    return jax.shard_map(
        shards,
        mesh=mesh,
        in_specs=placed,
        out_specs=(P(None, "pair", "wide"), P(None, "pair")),
        check_vma=False,
    )
```

profile of v0, /device:TPU:0, one launch (start us, length us, event | category | flops | bytes accessed | tf_op | source)
XLA Modules:
  0.0 440.1 jit_solution(13261988004522768820)
XLA Ops:
  7.2 0.9 slice_reduce_fusion.2
  8.8 7.0 %fusion.47 = (bf16[1,1,512,1,1024]{4,3,2,1,0:T(2,128)(2,1)}, bf16[1,1,512,1,1024]{4,3,2,1,0:T(2,128)(2,1)}) fusion(bf16[1,1,512,2,1024]{4,3,2,1,0:T(2,128)(2,1)} %param.11), kind=kLoop, calls=%fused_computation.90 | loop fusion | bytes 4194304 | tf_op jit(solution)/shard_map/slice | solution.py:22
  15.8 4.6 %copy.52 = bf16[1,1,512,1,1024]{2,4,3,1,0:T(8,128)(2,1)S(1)} copy(bf16[1,1,512,1,1024]{4,3,2,1,0:T(2,128)(2,1)} %get-tuple-element.18) | data formatting | bytes 2097152
  22.4 4.6 %copy.53 = bf16[1,1,512,1,1024]{2,4,3,1,0:T(8,128)(2,1)S(1)} copy(bf16[1,1,512,1,1024]{4,3,2,1,0:T(2,128)(2,1)} %get-tuple-element.19) | data formatting | bytes 2097152
  28.6 6.8 %copy.40 = bf16[1,1,8192]{1,0,2:T(2,128)(2,1)} copy(bf16[1,1,8192]{2,1,0:T(2,128)(2,1)S(1)} %get-tuple-element.21) | data formatting | bytes 32768 | tf_op jit(solution)/shard_map/slice | solution.py:113
  35.9 62.6 %reduce.26 = bf16[8192]{0:T(1024)(128)(2,1)S(1)} reduce(bf16[8192,1,1]{2,1,0:T(2,128)(2,1)} %bitcast.130, bf16[]{:T(256)} %broadcast.372), dimensions={1,2}, to_apply=%bitcast.111.reduce_sub_computation | reduce | bytes 32770
  99.2 4.2 all-to-all-start
  104.0 6.8 %copy.43 = bf16[1,1,8192]{1,0,2:T(2,128)(2,1)} copy(bf16[1,1,8192]{2,1,0:T(2,128)(2,1)S(1)} %get-tuple-element.20) | data formatting | bytes 32768 | tf_op jit(solution)/shard_map/slice | solution.py:113
  110.7 62.6 %reduce.27 = bf16[8192]{0:T(1024)(128)(2,1)S(1)} reduce(bf16[8192,1,1]{2,1,0:T(2,128)(2,1)} %bitcast.131, bf16[]{:T(256)} %broadcast.372), dimensions={1,2}, to_apply=%bitcast.113.reduce_sub_computation | reduce | bytes 32770
  174.0 3.4 all-to-all-start.1
  177.6 6.1 %reshape.622 = bf16[8192,1,1]{2,1,0:T(2,128)(2,1)} reshape(bf16[2,2,2048]{2,1,0:T(2,128)(2,1)S(1)} %all-to-all-done) | data formatting | bytes 32768
  183.7 62.0 %bitcast_reduce_fusion.1 = bf16[8192]{0:T(1024)(128)(2,1)S(1)} fusion(bf16[8192,1,1]{2,1,0:T(2,128)(2,1)} %reshape.622), kind=kLoop, calls=%fused_computation.95 | loop fusion | bytes 32768 | tf_op jit(solution)/shard_map/all_to_all | solution.py:84
  245.6 23.0 %all_gather.6 = bf16[1,2,16,4096]{3,1,0,2:T(2,128)(2,1)S(1)} all-gather(bf16[1,2,1,4096]{3,1,0,2:T(2,128)(2,1)S(1)} %bitcast.140), channel_id=1, replica_groups=mesh['wide'=16,'pair'=2] {'wide'}, dimensions={2}, use_global_device_ids=true | all-gather | bytes 278528 | tf_op jit(solution)/shard_map/all_gather | solution.py:90
  268.7 1.1 fusion.6
  270.1 6.1 %reshape.624 = bf16[8192,1,1]{2,1,0:T(2,128)(2,1)} reshape(bf16[2,2,2048]{2,1,0:T(2,128)(2,1)S(1)} %all-to-all-done.1) | data formatting | bytes 32768
  276.3 62.0 %bitcast_reduce_fusion = bf16[8192]{0:T(1024)(128)(2,1)S(1)} fusion(bf16[8192,1,1]{2,1,0:T(2,128)(2,1)} %reshape.624), kind=kLoop, calls=%fused_computation.94 | loop fusion | bytes 32768 | tf_op jit(solution)/shard_map/all_to_all | solution.py:84
  338.2 18.1 %all_gather.7 = bf16[1,2,16,4096]{3,1,0,2:T(2,128)(2,1)S(1)} all-gather(bf16[1,2,1,4096]{3,1,0,2:T(2,128)(2,1)S(1)} %bitcast.141), channel_id=1, replica_groups=mesh['wide'=16,'pair'=2] {'wide'}, dimensions={2}, use_global_device_ids=true | all-gather | bytes 278528 | tf_op jit(solution)/shard_map/all_gather | solution.py:90
  356.4 1.1 fusion.9
  357.6 8.6 %reduce-scatter.5.cloned.1.call-done = f32[1,2,8,256]{3,2,1,0:T(8,128)} async-done(((f32[1,2,16,256]{3,2,1,0:T(8,128)}), f32[1,2,8,256]{3,2,1,0:T(8,128)}) %reduce-scatter.5.cloned.1.call-update) | async-done | bytes 16400 | tf_op jit(solution)/shard_map/reduce_scatter | solution.py:94
  366.2 1.0 select_reduce_fusion.5
  367.1 32.7 %all-reduce.1 = (f32[1,8]{1,0:T(1,128)S(1)}, f32[1,8]{1,0:T(1,128)S(1)}) all-reduce(f32[1,8]{1,0:T(1,128)S(1)} %bitcast.152, f32[1,8]{1,0:T(1,128)S(1)} %bitcast.151), channel_id=1, replica_groups=mesh['wide'=16,'pair'=2] {'wide'}, use_global_device_ids=true, to_apply=%region_14.15 | all-reduce | flops 16 | bytes 128 | tf_op jit(solution)/shard_map/pmax | solution.py:105
  399.9 1.0 select_reduce_fusion.4
  400.8 1.0 select_reduce_fusion.1
  401.8 29.5 %all-reduce = (f32[1,8]{1,0:T(1,128)S(1)}, f32[1,8]{1,0:T(1,128)S(1)}, f32[1,8]{1,0:T(1,128)S(1)}, f32[1,8]{1,0:T(1,128)S(1)}) all-reduce(f32[1,8]{1,0:T(1,128)S(1)} %bitcast.148, f32[1,8]{1,0:T(1,128)S(1)} %bitcast.147, f32[1,8]{1,0:T(1,128)S(1)} %bitcast.150, f32[1,8]{1,0:T(1,128)S(1)} %bitcast.149), channel_id=1, replica_groups=mesh['wide'=16,'pair'=2] {'wide'}, use_global_device_ids=true, to_apply=%region_16.17 | all-reduce | flops 32 | bytes 256 | tf_op jit(solution)/shard_map/psum | solution.py:107
  (63 shorter events, 8.5 us)
Async XLA Ops:
  7.2 261.5 %copy-start = (bf16[4096,256]{1,0:T(8,128)(2,1)S(1)}, bf16[4096,256]{1,0:T(8,128)(2,1)}, u32[]{:S(2)}) copy-start(bf16[4096,256]{1,0:T(8,128)(2,1)} %param.16) | copy-start | bytes 6291460
  15.8 4.6 %copy-start.2 = (bf16[1,1,2,8192]{3,2,1,0:T(2,128)(2,1)S(1)}, bf16[1,1,2,8192]{3,2,1,0:T(2,128)(2,1)}, u32[]{:S(2)}) copy-start(bf16[1,1,2,8192]{3,2,1,0:T(2,128)(2,1)} %param.10) | copy-start | bytes 98308
  15.8 5.4 %copy-start.3 = (bf16[1,1,2,2,1024]{4,3,2,1,0:T(2,128)(2,1)S(1)}, bf16[1,1,2,2,1024]{4,3,2,1,0:T(2,128)(2,1)}, u32[]{:S(2)}) copy-start(bf16[1,1,2,2,1024]{4,3,2,1,0:T(2,128)(2,1)} %param.12) | copy-start | bytes 24580
  26.9 1.3 copy-start.1
  26.9 1.5 copy-start.4
  35.9 67.5 %copy-start.5 = (s32[2,8,8]{2,1,0:T(8,128)S(1)}, s32[2,8,8]{2,1,0:T(8,128)}, u32[]{:S(2)}) copy-start(s32[2,8,8]{2,1,0:T(8,128)} %param.18) | copy-start | bytes 1540
  35.9 67.5 %copy-start.6 = (s32[2,8]{1,0:T(2,128)S(1)}, s32[2,8]{1,0:T(2,128)}, u32[]{:S(2)}) copy-start(s32[2,8]{1,0:T(2,128)} %param.19) | copy-start | bytes 196
  99.2 74.8 %all-to-all-start = ((bf16[2,2,2048]{2,1,0:T(2,128)(2,1)}), bf16[2,2,2048]{2,1,0:T(2,128)(2,1)S(1)}, u32[]{:S(2)}, u32[]{:S(2)}) async-start(bf16[2,2,2048]{2,1,0:T(2,128)(2,1)} %reshape.621), calls=%async_computation | async-start | bytes 32768 | tf_op jit(solution)/shard_map/all_to_all | solution.py:84
  110.7 63.3 %copy-start.7 = (f32[16]{0:T(128)S(1)}, f32[16]{0:T(128)}, u32[]{:S(2)}) copy-start(f32[16]{0:T(128)} %param.17) | copy-start | bytes 196
  174.0 96.1 %all-to-all-start.1 = ((bf16[2,2,2048]{2,1,0:T(2,128)(2,1)}), bf16[2,2,2048]{2,1,0:T(2,128)(2,1)S(1)}, u32[]{:S(2)}, u32[]{:S(2)}) async-start(bf16[2,2,2048]{2,1,0:T(2,128)(2,1)} %reshape.623), calls=%async_computation.2 | async-start | bytes 32768 | tf_op jit(solution)/shard_map/all_to_all | solution.py:84
  177.5 180.1 %reduce-scatter.3.cloned.1.call-start = ((), (), s32[]{:S(2)}) async-start(), calls=%async_computation.4 | async-start | bytes 49152 | tf_op jit(solution)/shard_map/reduce_scatter | solution.py:94
  269.8 96.4 %reduce-scatter.5.cloned.1.call-start = ((), (), s32[]{:S(2)}) async-start(), calls=%async_computation.5 | async-start | bytes 49152 | tf_op jit(solution)/shard_map/reduce_scatter | solution.py:94
Sparse Core Ops, SparseCore 0:
  269.9 7.3 reduce-scatter.2
  357.7 8.4 reduce-scatter.4
where the time goes:
time: 441 us; the launch traced here: 440 us
  local copies, waits for them, and re-layouts  169 us (38%)
  other arithmetic  132 us (30%)
  blocking collectives  103 us (23%)
  between operations  14.9 us (3%)
  waiting for transfers between devices  8.67 us (2%)
  starting transfers between devices  8.01 us (2%)
    unnamed x2, other arithmetic  125 us
    all_to_all x2, local copies, waits for them, and re-layouts, finish(): lax.all_to_all(row_block, 'pair', split_axis=2, concat_axis=1, tiled=True)  124 us
    all_gather x2, blocking collectives, finish(): lax.all_gather(spread, 'wide', axis=2, tiled=True)  41.2 us
    pmax x1, blocking collectives, finish(): top = lax.pmax(local_top, 'wide')  32.7 us
    psum x1, blocking collectives, finish(): total, picked = lax.psum((local_total, picked_local), 'wide')  29.5 us
    unnamed x23, local copies, waits for them, and re-layouts  23.1 us
    slice x3, local copies, waits for them, and re-layouts, shards(): normed[index_of_step:index_of_step + 1]  13.6 us
  transfers between devices with their start and end apart: 4, of which 1 were waited for; matrix products, arithmetic and copies ran while one was open for 47% of the time, Pallas kernels for 0%

commit v1 on v0

v1 whole, which is shorter than its diff:
```python
import functools
import math

import jax
import jax.numpy as jnp
from jax import lax
from jax.experimental import pallas as pl
from jax.experimental.pallas import tpu as pltpu
from jax.sharding import PartitionSpec as P

QUERY_HEADS = 64
KEY_VALUE_HEADS = 8
HEAD_SIZE = 128
BLK = 32
DECODE_STEPS = 2
HEAD_ROWS = DECODE_STEPS * (QUERY_HEADS // KEY_VALUE_HEADS)
NEG_FILL = -1e30
BLOCKS = 4


def in_vmem():
    return pl.BlockSpec(memory_space=pltpu.VMEM)


def in_smem():
    return pl.BlockSpec(memory_space=pltpu.SMEM)


def call(kernel, out_shape, in_specs, scratch=(), limit=16 << 20, cost=None):
    return pl.pallas_call(
        kernel,
        out_shape=out_shape,
        in_specs=in_specs,
        out_specs=jax.tree.map(lambda _: in_vmem(), out_shape),
        scratch_shapes=list(scratch),
        compiler_params=pltpu.CompilerParams(vmem_limit_bytes=limit),
        cost_estimate=cost,
    )


def attend_kernel(
    lengths, queries_in, cache, fresh_in, residual_in, gain_in, mine, theirs,
    slots, gain_rows, queries, residual, gain, arrived,
):
    count = cache.shape[0]
    first_fresh = count - DECODE_STEPS
    small = [
        pltpu.make_async_copy(source, target, arrived.at[index])
        for index, (source, target) in enumerate(((queries_in, queries), (residual_in, residual), (gain_in, gain)))
    ]
    block = count // BLOCKS
    pieces = [
        [
            pltpu.make_async_copy(
                cache.at[pl.ds(part * block, size), head],
                slots.at[head, pl.ds(part * block, size)],
                arrived.at[len(small) + part * KEY_VALUE_HEADS + head],
            )
            for head in range(KEY_VALUE_HEADS)
        ]
        for part, size in enumerate([block] * (BLOCKS - 1) + [block - DECODE_STEPS])
    ]
    pieces[-1] += [
        pltpu.make_async_copy(
            fresh_in.at[:, head],
            slots.at[head, pl.ds(first_fresh, DECODE_STEPS)],
            arrived.at[len(small) + BLOCKS * KEY_VALUE_HEADS + head],
        )
        for head in range(KEY_VALUE_HEADS)
    ]
    small[0].start()
    for part in pieces:
        for copy in part:
            copy.start()
    small[1].start()
    small[2].start()
    small[0].wait()

    query_rows = queries.shape[0]
    head_of_row = lax.broadcasted_iota(jnp.int32, queries.shape, 0) // HEAD_ROWS
    wide_queries = queries[...].astype(jnp.float32)
    of_head = [
        jnp.where(head_of_row == head, wide_queries, 0.0).astype(jnp.bfloat16) for head in range(KEY_VALUE_HEADS)
    ]
    of_two = [jnp.concatenate(of_head[head : head + 2], axis=1) for head in range(0, KEY_VALUE_HEADS, 2)]
    interleaved = [slots.at[head].reshape(2 * count, HEAD_SIZE) for head in range(KEY_VALUE_HEADS)]
    parts = []
    for part, copies in enumerate(pieces):
        for copy in copies:
            copy.wait()
        rows = pl.ds(part * 2 * block, 2 * block)
        total = jnp.zeros((2 * block, query_rows), jnp.float32)
        for two, heads in enumerate(of_two):
            keys = jnp.concatenate([interleaved[2 * two][rows, :], interleaved[2 * two + 1][rows, :]], axis=1)
            total = total + lax.dot_general(
                keys, heads, (((1,), (1,)), ((), ())), preferred_element_type=jnp.float32
            )
        parts.append(total)
    score = jnp.concatenate(parts, axis=0)
    row = lax.broadcasted_iota(jnp.int32, score.shape, 0)
    step_of_query = lax.rem(lax.broadcasted_iota(jnp.int32, score.shape, 1), DECODE_STEPS)
    live = (row < 2 * lengths[0, 0]) | ((row >= 2 * first_fresh) & (row - 2 * first_fresh <= 2 * step_of_query))
    live = live & (lax.rem(row, 2) == 0)
    score = jnp.where(live, score * (1.0 / math.sqrt(HEAD_SIZE)), NEG_FILL)
    weight = jnp.exp(score - jnp.max(score, axis=0, keepdims=True))
    weight = weight * (1.0 / jnp.sum(weight, axis=0, keepdims=True))
    weight = pltpu.roll(weight, 1, 0).T.astype(jnp.bfloat16)
    mixed = [
        jnp.dot(
            weight[head * HEAD_ROWS : (head + 1) * HEAD_ROWS],
            interleaved[head][...],
            preferred_element_type=jnp.float32,
        )
        for head in range(KEY_VALUE_HEADS)
    ]
    for copy in small[1:]:
        copy.wait()
    gain_rows[pl.ds(0, QUERY_HEADS, stride=2), :] = gain[...]
    gain_rows[pl.ds(1, QUERY_HEADS, stride=2), :] = gain[...]
    hidden = jnp.concatenate(mixed, axis=0) + residual[...].astype(jnp.float32)
    row_power = jnp.sum(hidden * hidden, axis=1, keepdims=True)
    step_of_row = lax.rem(lax.broadcasted_iota(jnp.int32, row_power.shape, 0), DECODE_STEPS)
    scale = jnp.zeros_like(row_power)
    for step in range(DECODE_STEPS):
        power = jnp.sum(jnp.where(step_of_row == step, row_power, 0.0), axis=0, keepdims=True)
        power = power / (QUERY_HEADS * HEAD_SIZE)
        scale = jnp.where(step_of_row == step, lax.rsqrt(power + 1e-05), scale)
    normed = (hidden * scale * gain_rows[...]).astype(jnp.bfloat16)
    half = normed.shape[0] // 2
    first = lax.axis_index("pair") == 0
    mine[...] = jnp.where(first, normed[:half], normed[half:])
    theirs[...] = jnp.where(first, normed[half:], normed[:half])


def branch_factor(scale, branch):
    guidance = scale[lax.axis_index("wide")]
    return jnp.where(branch == 0, guidance, 1.0 - guidance)


def own_part_kernel(scale, mine, out, factor):
    branch = lax.axis_index("pair")
    out[...] = branch_factor(scale, branch) * mine[...].astype(jnp.float32)
    factor[...] = jnp.full(factor.shape, branch_factor(scale, 1 - branch), jnp.float32)


def combine_kernel(factor, own_part, received, spread):
    other_part = factor[0:1, :] * received[...].astype(jnp.float32)
    guided = (own_part[...] + other_part).astype(jnp.bfloat16)
    spread[...] = jnp.broadcast_to(guided[None], spread.shape)


def project_kernel(rows, weight, mine, theirs, wide_rows):
    pairs, per_pair, lanes = rows.shape
    half = pairs // 2
    for pair in range(pairs):
        wide_rows[pl.ds(pair * per_pair, per_pair), :] = rows[pair].astype(jnp.float32)

    def head_rows(head):
        steps = [
            wide_rows[pl.ds(head * DECODE_STEPS + step, pairs, stride=per_pair), :]
            for step in range(DECODE_STEPS)
        ]
        return jnp.concatenate(
            [rows_of_step[part * half : (part + 1) * half] for part in range(2) for rows_of_step in steps], axis=0
        ).astype(jnp.bfloat16)

    total = jnp.zeros((DECODE_STEPS * pairs, mine.shape[1]), jnp.float32)
    for two in range(per_pair // DECODE_STEPS // 2):
        left = jnp.concatenate([head_rows(2 * two), head_rows(2 * two + 1)], axis=1)
        total = total + jnp.dot(
            left, weight[pl.ds(two * 2 * lanes, 2 * lanes), :], preferred_element_type=jnp.float32
        )
    first = lax.axis_index("pair") == 0
    low, high = total[: mine.shape[0]], total[mine.shape[0] :]
    mine[...] = jnp.where(first, low, high)
    theirs[...] = jnp.where(first, high, low)


def to_lanes(column):
    size = column.shape[0]
    eye = lax.broadcasted_iota(jnp.int32, (size, size), 0) == lax.broadcasted_iota(jnp.int32, (size, size), 1)
    return jnp.sum(jnp.where(eye, column, jnp.zeros_like(column)), axis=0, keepdims=True)


def to_column(lanes):
    size = lanes.shape[1]
    eye = lax.broadcasted_iota(jnp.int32, (size, size), 0) == lax.broadcasted_iota(jnp.int32, (size, size), 1)
    return jnp.sum(jnp.where(eye, lanes, jnp.zeros_like(lanes)), axis=1, keepdims=True)


def allowed_entries(blocks, shape):
    half = blocks.shape[1]
    flags = jnp.concatenate([blocks[step] for step in range(DECODE_STEPS)], axis=0)
    block = lax.broadcasted_iota(jnp.int32, shape, 1) // BLK
    flag = jnp.zeros(shape, jnp.int32)
    for index in range(blocks.shape[2]):
        flag = jnp.where(block == index, flags[:, index : index + 1], flag)
    return flag > 0


def stats_kernel(mine, received, blocks, sampled, guided_out, stats):
    guided = mine[...] + received[...]
    guided_out[...] = guided
    count, width = guided.shape
    half = count // DECODE_STEPS
    allowed = allowed_entries(blocks, guided.shape)
    top = jnp.max(jnp.where(allowed, guided, NEG_FILL), axis=1, keepdims=True)
    total = jnp.sum(jnp.where(allowed, jnp.exp(guided - top), 0.0), axis=1, keepdims=True)
    chosen = jnp.concatenate([to_column(sampled[pl.ds(step, 1), :]) for step in range(DECODE_STEPS)], axis=0)
    column = lax.broadcasted_iota(jnp.int32, guided.shape, 1) + lax.axis_index("wide") * width
    picked = jnp.sum(jnp.where(column == chosen, guided, 0.0), axis=1, keepdims=True)
    lanes = jnp.concatenate([to_lanes(top), to_lanes(total), to_lanes(picked)], axis=1)
    pad = stats.shape[2] - lanes.shape[1]
    if pad > 0:
        lanes = jnp.concatenate([lanes, jnp.zeros((1, pad), jnp.float32)], axis=1)
    stats[...] = jnp.broadcast_to(lanes[None], stats.shape)


def finish_kernel(guided, stats, blocks, logprobs, tokens):
    count, width = guided.shape
    half = count // DECODE_STEPS
    parts = stats[...].reshape(stats.shape[0], stats.shape[2])
    tops = parts[:, 0:count]
    top = jnp.max(tops, axis=0, keepdims=True)
    total = jnp.sum(parts[:, count : 2 * count] * jnp.exp(tops - top), axis=0, keepdims=True)
    picked = jnp.sum(parts[:, 2 * count : 3 * count], axis=0, keepdims=True)
    normalizer = top + jnp.log(total)
    token = picked - normalizer
    for step in range(DECODE_STEPS):
        tokens[pl.ds(step, 1), :] = token[:, step * half : (step + 1) * half]
    allowed = allowed_entries(blocks, guided.shape)
    result = jnp.where(allowed, guided[...] - to_column(normalizer), 0.0)
    logprobs[...] = result.reshape(logprobs.shape)


def by_head(array):
    return array.reshape(array.shape[0], 2, KEY_VALUE_HEADS, HEAD_SIZE).transpose(0, 2, 1, 3)


def step_rows(array):
    split = array.reshape(DECODE_STEPS, QUERY_HEADS, HEAD_SIZE)
    return split.transpose(1, 0, 2).reshape(QUERY_HEADS * DECODE_STEPS, HEAD_SIZE)


def shards(
    wide,
    queries,
    cache,
    fresh_key_value,
    lengths,
    residual,
    norm_gain,
    vocab_weight,
    guidance,
    allowed_blocks,
    sampled,
):
    steps, half_pairs, blocks_here = allowed_blocks.shape
    width = vocab_weight.shape[1]
    pairs = guidance.shape[0]
    rows = steps * QUERY_HEADS
    cache_by_head = by_head(cache[0, 0])
    vmem, smem, hbm = in_vmem(), in_smem(), pl.BlockSpec(memory_space=pltpu.HBM)
    half_rows = jax.ShapeDtypeStruct((rows // 2, HEAD_SIZE), jnp.bfloat16)
    flat = jax.ShapeDtypeStruct((steps * half_pairs, width), jnp.float32)

    def swap(array):
        return lax.ppermute(array, "pair", [(0, 1), (1, 0)])

    mine, theirs = call(
        attend_kernel,
        (half_rows, half_rows),
        [smem] + [hbm] * 5,
        [
            pltpu.VMEM((KEY_VALUE_HEADS, cache.shape[2], 2, HEAD_SIZE), jnp.bfloat16),
            pltpu.VMEM((rows, HEAD_SIZE), jnp.float32),
            pltpu.VMEM((rows, HEAD_SIZE), jnp.bfloat16),
            pltpu.VMEM((rows, HEAD_SIZE), jnp.bfloat16),
            pltpu.VMEM((QUERY_HEADS, HEAD_SIZE), jnp.float32),
            pltpu.SemaphoreType.DMA(((BLOCKS + 1) * KEY_VALUE_HEADS + 3,)),
        ],
        limit=60 << 20,
    )(
        lengths,
        step_rows(queries[0, 0]),
        cache_by_head,
        by_head(fresh_key_value[0, 0]),
        step_rows(residual[0, 0]),
        norm_gain.reshape(QUERY_HEADS, HEAD_SIZE),
    )
    received = swap(theirs)
    own_part, factor = call(
        own_part_kernel,
        (jax.ShapeDtypeStruct(half_rows.shape, jnp.float32), jax.ShapeDtypeStruct((8, HEAD_SIZE), jnp.float32)),
        [smem, vmem],
    )(guidance, mine)
    spread = call(combine_kernel, jax.ShapeDtypeStruct((wide,) + half_rows.shape, jnp.bfloat16), [vmem] * 3)(
        factor, own_part, received
    )

    gathered = lax.all_to_all(spread, "wide", 0, 0, tiled=True)
    mine, theirs = call(
        project_kernel,
        (flat, flat),
        [vmem, vmem],
        [pltpu.VMEM((pairs * rows // 2, HEAD_SIZE), jnp.float32)],
    )(gathered, vocab_weight)

    lanes = pl.cdiv(3 * steps * half_pairs, 128) * 128
    guided, stats = call(
        stats_kernel,
        (flat, jax.ShapeDtypeStruct((wide, 1, lanes), jnp.float32)),
        [vmem] * 4,
    )(mine, swap(theirs), allowed_blocks, sampled)
    logprobs, tokens = call(
        finish_kernel,
        (
            jax.ShapeDtypeStruct((steps, half_pairs, width), jnp.float32),
            jax.ShapeDtypeStruct((steps, half_pairs), jnp.float32),
        ),
        [vmem] * 3,
    )(guided, lax.all_to_all(stats, "wide", 0, 0, tiled=True), allowed_blocks)
    return (logprobs, tokens)


def solution(mesh):
    placed = (
        P("pair", "wide", None, None),
        P("pair", "wide", None, None, None),
        P("pair", "wide", None, None, None),
        P("pair", "wide"),
        P("pair", "wide", None, None),
        P(),
        P("pair", "wide"),
        P(),
        P(None, "pair", "wide"),
        P(None, "pair"),
    )
    return jax.shard_map(
        functools.partial(shards, mesh.shape["wide"]),
        mesh=mesh,
        in_specs=placed,
        out_specs=(P(None, "pair", "wide"), P(None, "pair")),
        check_vma=False,
    )
```

time: 441 us -> 42.9 us (0.10)
  local copies, waits for them, and re-layouts: 169 us -> 0.74 us
  other arithmetic: 132 us -> 0 us
  blocking collectives: 103 us -> 25.5 us
  between operations: 14.9 us -> 1.49 us
  Pallas kernels: 0 us -> 7.41 us
  waiting for transfers between devices: 8.67 us -> 2.89 us
    unnamed x2 -> x0, other arithmetic: 125 us -> none
    all_to_all x2 -> x0, local copies, waits for them, and re-layouts: 124 us -> none  [finish(): lax.all_to_all(row_block, 'pair', split_axis=2, concat_axis=1, tiled=True)]
    all_gather x2 -> x0, blocking collectives: 41.2 us -> none  [finish(): lax.all_gather(spread, 'wide', axis=2, tiled=True)]
    pmax x1 -> x0, blocking collectives: 32.7 us -> none  [finish(): top = lax.pmax(local_top, 'wide')]
    psum x1 -> x0, blocking collectives: 29.5 us -> none  [finish(): total, picked = lax.psum((local_total, picked_local), 'wide')]
    all_to_all x0 -> x2, blocking collectives: none -> 25.5 us  [the longest x1 16.3 us: shards(): gathered = lax.all_to_all(spread, 'wide', 0, 0, tiled=True)]
    unnamed x23 -> x10, local copies, waits for them, and re-layouts: 23.1 us -> 0.74 us
    slice x7 -> x0, local copies, waits for them, and re-layouts: 21.7 us -> none  [the longest x3 13.6 us: shards(): normed[index_of_step:index_of_step + 1]]
  transfers between devices with their start and end apart: 4 -> 2, of which waited for: 1 -> 2; matrix products, arithmetic and copies ran while one was open for 47% -> 0% of each run, Pallas kernels for 0% -> 1%
where the time goes in v1:
time: 42.9 us; the launch traced here: 42.6 us
  blocking collectives  25.5 us (59%)
  Pallas kernels  7.41 us (17%)
  starting transfers between devices  4.56 us (11%)
  waiting for transfers between devices  2.89 us (7%)
  between operations  1.49 us (3%)
  local copies, waits for them, and re-layouts  0.74 us (2%)
    all_to_all x1, blocking collectives, shards(): gathered = lax.all_to_all(spread, 'wide', 0, 0, tiled=True)  16.3 us
    all_to_all x1, blocking collectives, shards(): lax.all_to_all(stats, 'wide', 0, 0, tiled=True)  9.18 us
    pallas_call x1, Pallas kernels, shards(): call(attend_kernel, (half_rows, half_rows), [smem] + [hbm] * 5, [pltpu.VM...  5.11 us
    ppermute x2, starting transfers between devices, swap(): return lax.ppermute(array, 'pair', [(0, 1), (1, 0)])  4.56 us
    ppermute x2, waiting for transfers between devices, swap(): return lax.ppermute(array, 'pair', [(0, 1), (1, 0)])  2.89 us
  transfers between devices with their start and end apart: 2, of which 2 were waited for; matrix products, arithmetic and copies ran while one was open for 0% of the time, Pallas kernels for 1%

profile of v1, /device:TPU:0, one launch (start us, length us, event | category | flops | bytes accessed | tf_op | source)
XLA Modules:
  0.0 42.6 jit_solution(8666831668909870118)
XLA Ops:
  0.6 0.0 copy-start.4
  0.6 0.0 copy-start
  1.4 0.0 copy-start.3
  1.5 5.1 %shard_map.113 = (bf16[64,128]{1,0:T(8,128)(2,1)}, bf16[64,128]{1,0:T(8,128)(2,1)}) custom-call(s32[1,1]{1,0:T(1,128)S(6)} %copy.14.lengths, bf16[128,128]{1,0:T(8,128)(2,1)} %bitcast.18, bf16[512,8,2,128]{3,2,1,0:T(2,128)(2,1)} %bitcast.17, bf16[2,8,2,128]{3,2,1,0:T(2,128)(2,1)} %bitcast.21, bf16[128,128]{1,0:T(8,128)(2,1)} %bitcast.19, f32[64,128]{1,0:T(8,128)} %bitcast.20), custom_call_target="tpu_custom_call" | custom-call | tf_op jit(solution)/shard_map/pallas_call | solution.py:270
  6.6 0.0 copy-start.1
  6.6 3.0 %collective-permute-start = (bf16[64,128]{1,0:T(8,128)(2,1)}, bf16[64,128]{1,0:T(8,128)(2,1)S(1)}, u32[]{:S(2)}, u32[]{:S(2)}) collective-permute-start(bf16[64,128]{1,0:T(8,128)(2,1)} %get-tuple-element.13), channel_id=1, source_target_pairs={{0,1},{1,0},{2,3},{3,2},{4,5},{5,4},{6,7},{7,6},{8,9},{9,8},{10,11... | collective-permute-start | bytes 49160 | tf_op jit(solution)/shard_map/ppermute | solution.py:268
  9.6 0.0 copy-done.4
  9.6 0.0 copy-start.2
  9.6 0.7 %copy-done.2 = bf16[64,128]{1,0:T(8,128)(2,1)S(1)} copy-done((bf16[64,128]{1,0:T(8,128)(2,1)S(1)}, bf16[64,128]{1,0:T(8,128)(2,1)}, u32[]{:S(2)}) %copy-start.2) | copy-done | bytes 16408
  10.3 0.6 %shard_map.114 = (f32[64,128]{1,0:T(8,128)S(1)}, f32[8,128]{1,0:T(8,128)S(1)}) custom-call(f32[16]{0:T(128)S(1)} %copy-done.4, bf16[64,128]{1,0:T(8,128)(2,1)S(1)} %copy-done.2), custom_call_target="tpu_custom_call" | custom-call | tf_op jit(solution)/shard_map/pallas_call | solution.py:292
  10.9 0.6 %collective-permute-done.received = bf16[64,128]{1,0:T(8,128)(2,1)S(1)} collective-permute-done((bf16[64,128]{1,0:T(8,128)(2,1)}, bf16[64,128]{1,0:T(8,128)(2,1)S(1)}, u32[]{:S(2)}, u32[]{:S(2)}) %collective-permute-start) | collective-permute-done | bytes 16416 | tf_op jit(solution)/shard_map/ppermute | solution.py:268
  11.5 16.3 %all_to_all.10.rows = bf16[16,64,128]{2,1,0:T(8,128)(2,1)S(1)} all-to-all(bf16[16,64,128]{2,1,0:T(8,128)(2,1)S(1)} %shard_map.115), channel_id=1, replica_groups=mesh['wide'=16,'pair'=2] {'wide'}, dimensions={0} | all-to-all | bytes 524288 | tf_op jit(solution)/shard_map/all_to_all | solution.py:301
  27.9 0.0 copy-done
  27.9 0.5 %shard_map.116 = (f32[16,256]{1,0:T(8,128)S(1)}, f32[16,256]{1,0:T(8,128)S(1)}) custom-call(bf16[16,64,128]{2,1,0:T(8,128)(2,1)S(1)} %all_to_all.10.rows, bf16[4096,256]{1,0:T(8,128)(2,1)S(1)} %copy-done), custom_call_target="tpu_custom_call" | custom-call | tf_op jit(solution)/shard_map/pallas_call | solution.py:302
  28.4 1.6 %collective-permute-start.1 = (f32[16,256]{1,0:T(8,128)S(1)}, f32[16,256]{1,0:T(8,128)S(1)}, u32[]{:S(2)}, u32[]{:S(2)}) collective-permute-start(f32[16,256]{1,0:T(8,128)S(1)} %get-tuple-element.15), channel_id=1, source_target_pairs={{0,1},{1,0},{2,3},{3,2},{4,5},{5,4},{6,7},{7,6},{8,9},{9,8},{10,11... | collective-permute-start | bytes 49160 | tf_op jit(solution)/shard_map/ppermute | solution.py:268
  30.0 2.2 %collective-permute-done.1.received = f32[16,256]{1,0:T(8,128)S(1)} collective-permute-done((f32[16,256]{1,0:T(8,128)S(1)}, f32[16,256]{1,0:T(8,128)S(1)}, u32[]{:S(2)}, u32[]{:S(2)}) %collective-permute-start.1) | collective-permute-done | bytes 16416 | tf_op jit(solution)/shard_map/ppermute | solution.py:268
  32.2 0.0 copy-done.3
  32.2 0.0 copy-done.1
  32.2 0.3 shard_map.117
  32.6 9.2 %all_to_all.11.stats = f32[16,1,128]{2,1,0:T(1,128)S(1)} all-to-all(f32[16,1,128]{2,1,0:T(1,128)S(1)} %get-tuple-element.17), channel_id=1, replica_groups=mesh['wide'=16,'pair'=2] {'wide'}, dimensions={0} | all-to-all | bytes 16384 | tf_op jit(solution)/shard_map/all_to_all | solution.py:322
  41.7 0.8 %shard_map.118 = (f32[2,8,256]{2,1,0:T(8,128)}, f32[2,8]{1,0:T(2,128)}) custom-call(f32[16,256]{1,0:T(8,128)S(1)} %get-tuple-element.16.guided, f32[16,1,128]{2,1,0:T(1,128)S(1)} %all_to_all.11.stats, s32[2,8,8]{2,1,0:T(8,128)S(1)} %copy-done.1), custom_call_target="tpu_custom_call" | custom-call | tf_op jit(solution)/shard_map/pallas_call | solution.py:315
  (1 shorter events, 0.0 us)
Async XLA Ops:
  0.6 9.0 %copy-start.4 = (f32[16]{0:T(128)S(1)}, f32[16]{0:T(128)}, u32[]{:S(2)}) copy-start(f32[16]{0:T(128)} %scale.1) | copy-start | bytes 196
  0.6 27.2 %copy-start = (bf16[4096,256]{1,0:T(8,128)(2,1)S(1)}, bf16[4096,256]{1,0:T(8,128)(2,1)}, u32[]{:S(2)}) copy-start(bf16[4096,256]{1,0:T(8,128)(2,1)} %weight.1) | copy-start | bytes 6291460
  1.4 30.8 %copy-start.3 = (s32[2,8]{1,0:T(2,128)S(1)}, s32[2,8]{1,0:T(2,128)}, u32[]{:S(2)}) copy-start(s32[2,8]{1,0:T(2,128)} %sampled.1) | copy-start | bytes 196
  6.6 25.6 %copy-start.1 = (s32[2,8,8]{2,1,0:T(8,128)S(1)}, s32[2,8,8]{2,1,0:T(8,128)}, u32[]{:S(2)}) copy-start(s32[2,8,8]{2,1,0:T(8,128)} %blocks.3) | copy-start | bytes 1540
  6.6 4.9 %collective-permute-start = (bf16[64,128]{1,0:T(8,128)(2,1)}, bf16[64,128]{1,0:T(8,128)(2,1)S(1)}, u32[]{:S(2)}, u32[]{:S(2)}) collective-permute-start(bf16[64,128]{1,0:T(8,128)(2,1)} %get-tuple-element.13), channel_id=1, source_target_pairs={{0,1},{1,0},{2,3},{3,2},{4,5},{5,4},{6,7},{7,6},{8,9},{9,8},{10,11... | collective-permute-start | bytes 49160 | tf_op jit(solution)/shard_map/ppermute | solution.py:268
  9.6 0.7 %copy-start.2 = (bf16[64,128]{1,0:T(8,128)(2,1)S(1)}, bf16[64,128]{1,0:T(8,128)(2,1)}, u32[]{:S(2)}) copy-start(bf16[64,128]{1,0:T(8,128)(2,1)} %get-tuple-element.10.mine) | copy-start | bytes 49156
  28.4 3.8 %collective-permute-start.1 = (f32[16,256]{1,0:T(8,128)S(1)}, f32[16,256]{1,0:T(8,128)S(1)}, u32[]{:S(2)}, u32[]{:S(2)}) collective-permute-start(f32[16,256]{1,0:T(8,128)S(1)} %get-tuple-element.15), channel_id=1, source_target_pairs={{0,1},{1,0},{2,3},{3,2},{4,5},{5,4},{6,7},{7,6},{8,9},{9,8},{10,11... | collective-permute-start | bytes 49160 | tf_op jit(solution)/shard_map/ppermute | solution.py:268

commit v2 on v1

--- a/solution.py
+++ b/solution.py
@@ -13,9 +13,10 @@
 HEAD_SIZE = 128
 BLK = 32
 DECODE_STEPS = 2
+SLOT_ROWS = 2 * KEY_VALUE_HEADS
 HEAD_ROWS = DECODE_STEPS * (QUERY_HEADS // KEY_VALUE_HEADS)
 NEG_FILL = -1e30
-BLOCKS = 4
+CHUNKS = 4
 
 
 def in_vmem():
@@ -40,83 +41,67 @@
 
 def attend_kernel(
     lengths, queries_in, cache, fresh_in, residual_in, gain_in, mine, theirs,
-    slots, gain_rows, queries, residual, gain, arrived,
+    stage, wide_rows, gain_rows, queries, fresh, residual, gain, arrived,
 ):
-    count = cache.shape[0]
-    first_fresh = count - DECODE_STEPS
+    rows = cache.shape[0]
+    slots = rows // SLOT_ROWS
+    part = rows // CHUNKS
+    copies = [
+        pltpu.make_async_copy(
+            cache.at[pl.ds(index * part, part)], stage.at[pl.ds(index * part, part)], arrived.at[index]
+        )
+        for index in range(CHUNKS)
+    ]
     small = [
-        pltpu.make_async_copy(source, target, arrived.at[index])
-        for index, (source, target) in enumerate(((queries_in, queries), (residual_in, residual), (gain_in, gain)))
+        pltpu.make_async_copy(source, target, arrived.at[CHUNKS + index])
+        for index, (source, target) in enumerate(
+            ((gain_in, gain), (fresh_in, fresh), (queries_in, queries), (residual_in, residual))
+        )
     ]
-    block = count // BLOCKS
-    pieces = [
-        [
-            pltpu.make_async_copy(
-                cache.at[pl.ds(part * block, size), head],
-                slots.at[head, pl.ds(part * block, size)],
-                arrived.at[len(small) + part * KEY_VALUE_HEADS + head],
-            )
-            for head in range(KEY_VALUE_HEADS)
-        ]
-        for part, size in enumerate([block] * (BLOCKS - 1) + [block - DECODE_STEPS])
-    ]
-    pieces[-1] += [
-        pltpu.make_async_copy(
-            fresh_in.at[:, head],
-            slots.at[head, pl.ds(first_fresh, DECODE_STEPS)],
-            arrived.at[len(small) + BLOCKS * KEY_VALUE_HEADS + head],
-        )
-        for head in range(KEY_VALUE_HEADS)
-    ]
-    small[0].start()
-    for part in pieces:
-        for copy in part:
-            copy.start()
-    small[1].start()
-    small[2].start()
-    small[0].wait()
-
-    query_rows = queries.shape[0]
-    head_of_row = lax.broadcasted_iota(jnp.int32, queries.shape, 0) // HEAD_ROWS
-    wide_queries = queries[...].astype(jnp.float32)
-    of_head = [
-        jnp.where(head_of_row == head, wide_queries, 0.0).astype(jnp.bfloat16) for head in range(KEY_VALUE_HEADS)
-    ]
-    of_two = [jnp.concatenate(of_head[head : head + 2], axis=1) for head in range(0, KEY_VALUE_HEADS, 2)]
-    interleaved = [slots.at[head].reshape(2 * count, HEAD_SIZE) for head in range(KEY_VALUE_HEADS)]
-    parts = []
-    for part, copies in enumerate(pieces):
-        for copy in copies:
-            copy.wait()
-        rows = pl.ds(part * 2 * block, 2 * block)
-        total = jnp.zeros((2 * block, query_rows), jnp.float32)
-        for two, heads in enumerate(of_two):
-            keys = jnp.concatenate([interleaved[2 * two][rows, :], interleaved[2 * two + 1][rows, :]], axis=1)
-            total = total + lax.dot_general(
-                keys, heads, (((1,), (1,)), ((), ())), preferred_element_type=jnp.float32
-            )
-        parts.append(total)
-    score = jnp.concatenate(parts, axis=0)
-    row = lax.broadcasted_iota(jnp.int32, score.shape, 0)
-    step_of_query = lax.rem(lax.broadcasted_iota(jnp.int32, score.shape, 1), DECODE_STEPS)
-    live = (row < 2 * lengths[0, 0]) | ((row >= 2 * first_fresh) & (row - 2 * first_fresh <= 2 * step_of_query))
-    live = live & (lax.rem(row, 2) == 0)
-    score = jnp.where(live, score * (1.0 / math.sqrt(HEAD_SIZE)), NEG_FILL)
-    weight = jnp.exp(score - jnp.max(score, axis=0, keepdims=True))
-    weight = weight * (1.0 / jnp.sum(weight, axis=0, keepdims=True))
-    weight = pltpu.roll(weight, 1, 0).T.astype(jnp.bfloat16)
-    mixed = [
-        jnp.dot(
-            weight[head * HEAD_ROWS : (head + 1) * HEAD_ROWS],
-            interleaved[head][...],
-            preferred_element_type=jnp.float32,
-        )
-        for head in range(KEY_VALUE_HEADS)
-    ]
-    for copy in small[1:]:
+    for copy in copies + small:
+        copy.start()
+    for index, copy in enumerate(copies):
+        copy.wait()
+
+        def widen(step, carry):
+            at = pl.ds(pl.multiple_of(index * part + step * 256, 256), 256)
+            wide_rows[at, :] = stage[at, :].astype(jnp.float32)
+            return carry
+
+        lax.fori_loop(0, part // 256, widen, 0)
+    for copy in small:
         copy.wait()
     gain_rows[pl.ds(0, QUERY_HEADS, stride=2), :] = gain[...]
     gain_rows[pl.ds(1, QUERY_HEADS, stride=2), :] = gain[...]
+    wide_rows[pl.ds(rows - DECODE_STEPS * SLOT_ROWS, DECODE_STEPS * SLOT_ROWS), :] = fresh[...].astype(jnp.float32)
+    factor = 1.0 / math.sqrt(HEAD_SIZE)
+    scores = []
+    for head in range(KEY_VALUE_HEADS):
+        keys = wide_rows[pl.ds(2 * head, slots, stride=SLOT_ROWS), :].astype(jnp.bfloat16)
+        scores.append(
+            lax.dot_general(
+                queries[pl.ds(head * HEAD_ROWS, HEAD_ROWS), :],
+                keys,
+                (((1,), (1,)), ((), ())),
+                preferred_element_type=jnp.float32,
+            )
+        )
+    score = jnp.concatenate(scores, axis=0)
+    slot = lax.broadcasted_iota(jnp.int32, score.shape, 1)
+    step_of_row = lax.rem(lax.broadcasted_iota(jnp.int32, score.shape, 0), DECODE_STEPS)
+    first_fresh = slots - DECODE_STEPS
+    live = (slot < lengths[0, 0]) | ((slot >= first_fresh) & (slot - first_fresh <= step_of_row))
+    score = jnp.where(live, score * factor, NEG_FILL)
+    weight = jnp.exp(score - jnp.max(score, axis=1, keepdims=True))
+    weight = (weight / jnp.sum(weight, axis=1, keepdims=True)).astype(jnp.bfloat16)
+    mixed = []
+    for head in range(KEY_VALUE_HEADS):
+        values = wide_rows[pl.ds(2 * head + 1, slots, stride=SLOT_ROWS), :].astype(jnp.bfloat16)
+        mixed.append(
+            jnp.dot(
+                weight[head * HEAD_ROWS : (head + 1) * HEAD_ROWS], values, preferred_element_type=jnp.float32
+            )
+        )
     hidden = jnp.concatenate(mixed, axis=0) + residual[...].astype(jnp.float32)
     row_power = jnp.sum(hidden * hidden, axis=1, keepdims=True)
     step_of_row = lax.rem(lax.broadcasted_iota(jnp.int32, row_power.shape, 0), DECODE_STEPS)
@@ -149,11 +134,15 @@
     spread[...] = jnp.broadcast_to(guided[None], spread.shape)
 
 
-def project_kernel(rows, weight, mine, theirs, wide_rows):
-    pairs, per_pair, lanes = rows.shape
+def project_kernel(near, far, weight, mine, theirs, wide_rows):
+    pairs = 2 * near.shape[0]
+    per_pair, lanes = near.shape[1:]
     half = pairs // 2
-    for pair in range(pairs):
-        wide_rows[pl.ds(pair * per_pair, per_pair), :] = rows[pair].astype(jnp.float32)
+    parity = lax.axis_index("wide") % 2
+    for rows, offset in ((near, parity), (far, 1 - parity)):
+        for index in range(half):
+            at = pl.multiple_of((2 * index + offset) * per_pair, per_pair)
+            wide_rows[pl.ds(at, per_pair), :] = rows[index].astype(jnp.float32)
 
     def head_rows(head):
         steps = [
@@ -233,8 +222,10 @@
     logprobs[...] = result.reshape(logprobs.shape)
 
 
-def by_head(array):
-    return array.reshape(array.shape[0], 2, KEY_VALUE_HEADS, HEAD_SIZE).transpose(0, 2, 1, 3)
+def slot_rows(array):
+    slots = array.shape[0]
+    split = array.reshape(slots, 2, KEY_VALUE_HEADS, HEAD_SIZE)
+    return split.transpose(0, 2, 1, 3).reshape(slots * SLOT_ROWS, HEAD_SIZE)
 
 
 def step_rows(array):
@@ -259,7 +250,7 @@
     width = vocab_weight.shape[1]
     pairs = guidance.shape[0]
     rows = steps * QUERY_HEADS
-    cache_by_head = by_head(cache[0, 0])
+    cache_rows = slot_rows(cache[0, 0])
     vmem, smem, hbm = in_vmem(), in_smem(), pl.BlockSpec(memory_space=pltpu.HBM)
     half_rows = jax.ShapeDtypeStruct((rows // 2, HEAD_SIZE), jnp.bfloat16)
     flat = jax.ShapeDtypeStruct((steps * half_pairs, width), jnp.float32)
@@ -272,19 +263,21 @@
         (half_rows, half_rows),
         [smem] + [hbm] * 5,
         [
-            pltpu.VMEM((KEY_VALUE_HEADS, cache.shape[2], 2, HEAD_SIZE), jnp.bfloat16),
+            pltpu.VMEM(cache_rows.shape, jnp.bfloat16),
+            pltpu.VMEM(cache_rows.shape, jnp.float32),
             pltpu.VMEM((rows, HEAD_SIZE), jnp.float32),
             pltpu.VMEM((rows, HEAD_SIZE), jnp.bfloat16),
+            pltpu.VMEM((steps * SLOT_ROWS, HEAD_SIZE), jnp.bfloat16),
             pltpu.VMEM((rows, HEAD_SIZE), jnp.bfloat16),
             pltpu.VMEM((QUERY_HEADS, HEAD_SIZE), jnp.float32),
-            pltpu.SemaphoreType.DMA(((BLOCKS + 1) * KEY_VALUE_HEADS + 3,)),
+            pltpu.SemaphoreType.DMA((CHUNKS + 4,)),
         ],
         limit=60 << 20,
     )(
         lengths,
         step_rows(queries[0, 0]),
-        cache_by_head,
-        by_head(fresh_key_value[0, 0]),
+        cache_rows,
+        slot_rows(fresh_key_value[0, 0]),
         step_rows(residual[0, 0]),
         norm_gain.reshape(QUERY_HEADS, HEAD_SIZE),
     )
@@ -294,17 +287,18 @@
         (jax.ShapeDtypeStruct(half_rows.shape, jnp.float32), jax.ShapeDtypeStruct((8, HEAD_SIZE), jnp.float32)),
         [smem, vmem],
     )(guidance, mine)
-    spread = call(combine_kernel, jax.ShapeDtypeStruct((wide,) + half_rows.shape, jnp.bfloat16), [vmem] * 3)(
+    spread = call(combine_kernel, jax.ShapeDtypeStruct((wide // 2,) + half_rows.shape, jnp.bfloat16), [vmem] * 3)(
         factor, own_part, received
     )
-
-    gathered = lax.all_to_all(spread, "wide", 0, 0, tiled=True)
+    same_core = [list(range(core, wide, 2)) for core in range(2)]
+    near = lax.all_to_all(spread, "wide", 0, 0, axis_index_groups=same_core, tiled=True)
+    far = lax.ppermute(near, "wide", [(source, source ^ 1) for source in range(wide)])
     mine, theirs = call(
         project_kernel,
         (flat, flat),
-        [vmem, vmem],
+        [vmem] * 3,
         [pltpu.VMEM((pairs * rows // 2, HEAD_SIZE), jnp.float32)],
-    )(gathered, vocab_weight)
+    )(near, far, vocab_weight)
 
     lanes = pl.cdiv(3 * steps * half_pairs, 128) * 128
     guided, stats = call(

time: 42.9 us -> 40.7 us (0.949)
  blocking collectives: 25.5 us -> 22.5 us
  waiting for transfers between devices: 2.89 us -> 4.23 us
  Pallas kernels: 7.41 us -> 6.92 us
    all_to_all x1, blocking collectives: 16.3 us -> 13.5 us  [shards(): lax.all_to_all(spread, 'wide', 0, 0, axis_index_groups=same_core, tiled=T...]
    ppermute x0 -> x1, waiting for transfers between devices: none -> 1.35 us  [shards(): lax.ppermute(near, 'wide', [(source, source ^ 1) for source in range(wide)])]
    pallas_call x1, Pallas kernels: 5.11 us -> 4.58 us  [shards(): call(attend_kernel, (half_rows, half_rows), [smem] + [hbm] * 5, [pltpu.VM...]
  transfers between devices with their start and end apart: 2 -> 3, of which waited for: 2 -> 3; matrix products, arithmetic and copies ran while one was open for 0% -> 0% of each run, Pallas kernels for 1% -> 1%
where the time goes in v2:
time: 40.7 us; the launch traced here: 40.4 us
  blocking collectives  22.5 us (55%)
  Pallas kernels  6.92 us (17%)
  starting transfers between devices  4.56 us (11%)
  waiting for transfers between devices  4.23 us (10%)
  between operations  1.49 us (4%)
  local copies, waits for them, and re-layouts  0.73 us (2%)
    all_to_all x1, blocking collectives, shards(): lax.all_to_all(spread, 'wide', 0, 0, axis_index_groups=same_core, tiled=T...  13.5 us
    all_to_all x1, blocking collectives, shards(): lax.all_to_all(stats, 'wide', 0, 0, tiled=True)  8.97 us
    pallas_call x1, Pallas kernels, shards(): call(attend_kernel, (half_rows, half_rows), [smem] + [hbm] * 5, [pltpu.VM...  4.58 us
    ppermute x2, starting transfers between devices, swap(): return lax.ppermute(array, 'pair', [(0, 1), (1, 0)])  4.56 us
    ppermute x2, waiting for transfers between devices, swap(): return lax.ppermute(array, 'pair', [(0, 1), (1, 0)])  2.89 us
    ppermute x1, waiting for transfers between devices, shards(): lax.ppermute(near, 'wide', [(source, source ^ 1) for source in range(wide)])  1.35 us
    pallas_call x1, Pallas kernels, shards(): call(finish_kernel, (jax.ShapeDtypeStruct((steps, half_pairs, width), jnp...  0.84 us
  transfers between devices with their start and end apart: 3, of which 3 were waited for; matrix products, arithmetic and copies ran while one was open for 0% of the time, Pallas kernels for 1%

profile of v2, /device:TPU:0, one launch (start us, length us, event | category | flops | bytes accessed | tf_op | source)
XLA Modules:
  0.0 40.4 jit_solution(9226787189061415619)
XLA Ops:
  0.6 0.0 copy-start.4
  0.6 0.0 copy-start
  1.4 0.0 copy-start.1
  1.5 0.0 copy-start.3
  1.5 4.6 %shard_map.113 = (bf16[64,128]{1,0:T(8,128)(2,1)}, bf16[64,128]{1,0:T(8,128)(2,1)}) custom-call(s32[1,1]{1,0:T(1,128)S(6)} %copy.16.lengths, bf16[128,128]{1,0:T(8,128)(2,1)} %bitcast.22, bf16[8192,128]{1,0:T(8,128)(2,1)} %bitcast.21, bf16[32,128]{1,0:T(8,128)(2,1)} %bitcast.25, bf16[128,128]{1,0:T(8,128)(2,1)} %bitcast.23, f32[64,128]{1,0:T(8,128)} %bitcast.24), custom_call_target="tpu_custom_call" | custom-call | tf_op jit(solution)/shard_map/pallas_call | solution.py:261
  6.1 3.0 %collective-permute-start = (bf16[64,128]{1,0:T(8,128)(2,1)}, bf16[64,128]{1,0:T(8,128)(2,1)S(1)}, u32[]{:S(2)}, u32[]{:S(2)}) collective-permute-start(bf16[64,128]{1,0:T(8,128)(2,1)} %get-tuple-element.13), channel_id=1, source_target_pairs={{0,1},{1,0},{2,3},{3,2},{4,5},{5,4},{6,7},{7,6},{8,9},{9,8},{10,11... | collective-permute-start | bytes 49160 | tf_op jit(solution)/shard_map/ppermute | solution.py:259
  9.1 0.0 copy-done.4
  9.1 0.0 copy-start.2
  9.1 0.7 %copy-done.2 = bf16[64,128]{1,0:T(8,128)(2,1)S(1)} copy-done((bf16[64,128]{1,0:T(8,128)(2,1)S(1)}, bf16[64,128]{1,0:T(8,128)(2,1)}, u32[]{:S(2)}) %copy-start.2) | copy-done | bytes 16408
  9.8 0.6 %shard_map.114 = (f32[64,128]{1,0:T(8,128)S(1)}, f32[8,128]{1,0:T(8,128)S(1)}) custom-call(f32[16]{0:T(128)S(1)} %copy-done.4, bf16[64,128]{1,0:T(8,128)(2,1)S(1)} %copy-done.2), custom_call_target="tpu_custom_call" | custom-call | tf_op jit(solution)/shard_map/pallas_call | solution.py:285
  10.4 0.6 %collective-permute-done.received = bf16[64,128]{1,0:T(8,128)(2,1)S(1)} collective-permute-done((bf16[64,128]{1,0:T(8,128)(2,1)}, bf16[64,128]{1,0:T(8,128)(2,1)S(1)}, u32[]{:S(2)}, u32[]{:S(2)}) %collective-permute-start) | collective-permute-done | bytes 16416 | tf_op jit(solution)/shard_map/ppermute | solution.py:259
  11.0 13.5 %all_to_all.10.near = bf16[8,64,128]{2,1,0:T(8,128)(2,1)S(1)} all-to-all(bf16[8,64,128]{2,1,0:T(8,128)(2,1)S(1)} %shard_map.115), channel_id=1, replica_groups={{0,4,8,12,16,20,24,28},{2,6,10,14,18,22,26,30},{1,5,9,13,17,21,25,29},{..., dimensions={0} | all-to-all | bytes 262144 | tf_op jit(solution)/shard_map/all_to_all | solution.py:294
  24.5 0.0 collective-permute-start.1
  24.5 1.3 %collective-permute-done.1.far = bf16[8,64,128]{2,1,0:T(8,128)(2,1)S(1)} collective-permute-done((bf16[8,64,128]{2,1,0:T(8,128)(2,1)S(1)}, bf16[8,64,128]{2,1,0:T(8,128)(2,1)S(1)}, u32[]{:S(2)}, u32[]{:S(2)}) %collective-permute-start.1) | collective-permute-done | bytes 131104 | tf_op jit(solution)/shard_map/ppermute | solution.py:295
  25.9 0.0 copy-done
  25.9 0.6 %shard_map.116 = (f32[16,256]{1,0:T(8,128)S(1)}, f32[16,256]{1,0:T(8,128)S(1)}) custom-call(bf16[8,64,128]{2,1,0:T(8,128)(2,1)S(1)} %all_to_all.10.near, bf16[8,64,128]{2,1,0:T(8,128)(2,1)S(1)} %collective-permute-done.1.far, bf16[4096,256]{1,0:T(8,128)(2,1)S(1)} %copy-done), custom_call_target="tpu_custom_call" | custom-call | tf_op jit(solution)/shard_map/pallas_call | solution.py:296
  26.4 1.6 %collective-permute-start.2 = (f32[16,256]{1,0:T(8,128)S(1)}, f32[16,256]{1,0:T(8,128)S(1)}, u32[]{:S(2)}, u32[]{:S(2)}) collective-permute-start(f32[16,256]{1,0:T(8,128)S(1)} %get-tuple-element.15), channel_id=1, source_target_pairs={{0,1},{1,0},{2,3},{3,2},{4,5},{5,4},{6,7},{7,6},{8,9},{9,8},{10,11... | collective-permute-start | bytes 49160 | tf_op jit(solution)/shard_map/ppermute | solution.py:259
  28.0 2.2 %collective-permute-done.2.received = f32[16,256]{1,0:T(8,128)S(1)} collective-permute-done((f32[16,256]{1,0:T(8,128)S(1)}, f32[16,256]{1,0:T(8,128)S(1)}, u32[]{:S(2)}, u32[]{:S(2)}) %collective-permute-start.2) | collective-permute-done | bytes 16416 | tf_op jit(solution)/shard_map/ppermute | solution.py:259
  30.3 0.0 copy-done.1
  30.3 0.0 copy-done.3
  30.3 0.3 shard_map.117
  30.6 9.0 %all_to_all.11.stats = f32[16,1,128]{2,1,0:T(1,128)S(1)} all-to-all(f32[16,1,128]{2,1,0:T(1,128)S(1)} %get-tuple-element.17), channel_id=1, replica_groups=mesh['wide'=16,'pair'=2] {'wide'}, dimensions={0} | all-to-all | bytes 16384 | tf_op jit(solution)/shard_map/all_to_all | solution.py:316
  39.6 0.8 %shard_map.118 = (f32[2,8,256]{2,1,0:T(8,128)}, f32[2,8]{1,0:T(2,128)}) custom-call(f32[16,256]{1,0:T(8,128)S(1)} %get-tuple-element.16.guided, f32[16,1,128]{2,1,0:T(1,128)S(1)} %all_to_all.11.stats, s32[2,8,8]{2,1,0:T(8,128)S(1)} %copy-done.1), custom_call_target="tpu_custom_call" | custom-call | tf_op jit(solution)/shard_map/pallas_call | solution.py:309
  (1 shorter events, 0.0 us)
Async XLA Ops:
  0.6 8.4 %copy-start.4 = (f32[16]{0:T(128)S(1)}, f32[16]{0:T(128)}, u32[]{:S(2)}) copy-start(f32[16]{0:T(128)} %scale.1) | copy-start | bytes 196
  0.6 25.2 %copy-start = (bf16[4096,256]{1,0:T(8,128)(2,1)S(1)}, bf16[4096,256]{1,0:T(8,128)(2,1)}, u32[]{:S(2)}) copy-start(bf16[4096,256]{1,0:T(8,128)(2,1)} %weight.1) | copy-start | bytes 6291460
  1.4 28.8 %copy-start.1 = (s32[2,8,8]{2,1,0:T(8,128)S(1)}, s32[2,8,8]{2,1,0:T(8,128)}, u32[]{:S(2)}) copy-start(s32[2,8,8]{2,1,0:T(8,128)} %blocks.3) | copy-start | bytes 1540
  1.5 28.8 %copy-start.3 = (s32[2,8]{1,0:T(2,128)S(1)}, s32[2,8]{1,0:T(2,128)}, u32[]{:S(2)}) copy-start(s32[2,8]{1,0:T(2,128)} %sampled.1) | copy-start | bytes 196
  6.1 4.9 %collective-permute-start = (bf16[64,128]{1,0:T(8,128)(2,1)}, bf16[64,128]{1,0:T(8,128)(2,1)S(1)}, u32[]{:S(2)}, u32[]{:S(2)}) collective-permute-start(bf16[64,128]{1,0:T(8,128)(2,1)} %get-tuple-element.13), channel_id=1, source_target_pairs={{0,1},{1,0},{2,3},{3,2},{4,5},{5,4},{6,7},{7,6},{8,9},{9,8},{10,11... | collective-permute-start | bytes 49160 | tf_op jit(solution)/shard_map/ppermute | solution.py:259
  9.1 0.7 %copy-start.2 = (bf16[64,128]{1,0:T(8,128)(2,1)S(1)}, bf16[64,128]{1,0:T(8,128)(2,1)}, u32[]{:S(2)}) copy-start(bf16[64,128]{1,0:T(8,128)(2,1)} %get-tuple-element.10.mine) | copy-start | bytes 49156
  24.5 1.3 %collective-permute-start.1 = (bf16[8,64,128]{2,1,0:T(8,128)(2,1)S(1)}, bf16[8,64,128]{2,1,0:T(8,128)(2,1)S(1)}, u32[]{:S(2)}, u32[]{:S(2)}) collective-permute-start(bf16[8,64,128]{2,1,0:T(8,128)(2,1)S(1)} %all_to_all.10.near), channel_id=1, source_target_pairs={{0,2},{2,0},{4,6},{6,4},{8,10},{10,8},{12,14},{14,12},{16,18},{18,... | collective-permute-start | bytes 393224 | tf_op jit(solution)/shard_map/ppermute | solution.py:295
  26.4 3.8 %collective-permute-start.2 = (f32[16,256]{1,0:T(8,128)S(1)}, f32[16,256]{1,0:T(8,128)S(1)}, u32[]{:S(2)}, u32[]{:S(2)}) collective-permute-start(f32[16,256]{1,0:T(8,128)S(1)} %get-tuple-element.15), channel_id=1, source_target_pairs={{0,1},{1,0},{2,3},{3,2},{4,5},{5,4},{6,7},{7,6},{8,9},{9,8},{10,11... | collective-permute-start | bytes 49160 | tf_op jit(solution)/shard_map/ppermute | solution.py:259

commit v3 on v2

--- a/solution.py
+++ b/solution.py
@@ -14,6 +14,8 @@
 BLK = 32
 DECODE_STEPS = 2
 SLOT_ROWS = 2 * KEY_VALUE_HEADS
+SLOT_PITCH = SLOT_ROWS + 1
+UNROLL = 32
 HEAD_ROWS = DECODE_STEPS * (QUERY_HEADS // KEY_VALUE_HEADS)
 NEG_FILL = -1e30
 CHUNKS = 4
@@ -64,20 +66,28 @@
         copy.wait()
 
         def widen(step, carry):
-            at = pl.ds(pl.multiple_of(index * part + step * 256, 256), 256)
-            wide_rows[at, :] = stage[at, :].astype(jnp.float32)
+            first = index * (part // SLOT_ROWS) + step * UNROLL
+            source = pl.multiple_of(first * SLOT_ROWS, UNROLL * SLOT_ROWS)
+            target = pl.multiple_of(first * SLOT_PITCH, 8)
+            for slot in range(UNROLL):
+                wide_rows[pl.ds(target + slot * SLOT_PITCH, SLOT_ROWS), :] = stage[
+                    pl.ds(source + slot * SLOT_ROWS, SLOT_ROWS), :
+                ].astype(jnp.float32)
             return carry
 
-        lax.fori_loop(0, part // 256, widen, 0)
+        lax.fori_loop(0, part // (SLOT_ROWS * UNROLL), widen, 0)
     for copy in small:
         copy.wait()
     gain_rows[pl.ds(0, QUERY_HEADS, stride=2), :] = gain[...]
     gain_rows[pl.ds(1, QUERY_HEADS, stride=2), :] = gain[...]
-    wide_rows[pl.ds(rows - DECODE_STEPS * SLOT_ROWS, DECODE_STEPS * SLOT_ROWS), :] = fresh[...].astype(jnp.float32)
+    for step in range(DECODE_STEPS):
+        wide_rows[pl.ds((slots - DECODE_STEPS + step) * SLOT_PITCH, SLOT_ROWS), :] = fresh[
+            pl.ds(step * SLOT_ROWS, SLOT_ROWS), :
+        ].astype(jnp.float32)
     factor = 1.0 / math.sqrt(HEAD_SIZE)
     scores = []
     for head in range(KEY_VALUE_HEADS):
-        keys = wide_rows[pl.ds(2 * head, slots, stride=SLOT_ROWS), :].astype(jnp.bfloat16)
+        keys = wide_rows[pl.ds(2 * head, slots, stride=SLOT_PITCH), :].astype(jnp.bfloat16)
         scores.append(
             lax.dot_general(
                 queries[pl.ds(head * HEAD_ROWS, HEAD_ROWS), :],
@@ -96,7 +106,7 @@
     weight = (weight / jnp.sum(weight, axis=1, keepdims=True)).astype(jnp.bfloat16)
     mixed = []
     for head in range(KEY_VALUE_HEADS):
-        values = wide_rows[pl.ds(2 * head + 1, slots, stride=SLOT_ROWS), :].astype(jnp.bfloat16)
+        values = wide_rows[pl.ds(2 * head + 1, slots, stride=SLOT_PITCH), :].astype(jnp.bfloat16)
         mixed.append(
             jnp.dot(
                 weight[head * HEAD_ROWS : (head + 1) * HEAD_ROWS], values, preferred_element_type=jnp.float32
@@ -138,15 +148,15 @@
     pairs = 2 * near.shape[0]
     per_pair, lanes = near.shape[1:]
     half = pairs // 2
+    pitch = per_pair + 1
     parity = lax.axis_index("wide") % 2
     for rows, offset in ((near, parity), (far, 1 - parity)):
         for index in range(half):
-            at = pl.multiple_of((2 * index + offset) * per_pair, per_pair)
-            wide_rows[pl.ds(at, per_pair), :] = rows[index].astype(jnp.float32)
+            wide_rows[pl.ds((2 * index + offset) * pitch, per_pair), :] = rows[index].astype(jnp.float32)
 
     def head_rows(head):
         steps = [
-            wide_rows[pl.ds(head * DECODE_STEPS + step, pairs, stride=per_pair), :]
+            wide_rows[pl.ds(head * DECODE_STEPS + step, pairs, stride=pitch), :]
             for step in range(DECODE_STEPS)
         ]
         return jnp.concatenate(
@@ -264,7 +274,7 @@
         [smem] + [hbm] * 5,
         [
             pltpu.VMEM(cache_rows.shape, jnp.bfloat16),
-            pltpu.VMEM(cache_rows.shape, jnp.float32),
+            pltpu.VMEM((cache.shape[2] * SLOT_PITCH, HEAD_SIZE), jnp.float32),
             pltpu.VMEM((rows, HEAD_SIZE), jnp.float32),
             pltpu.VMEM((rows, HEAD_SIZE), jnp.bfloat16),
             pltpu.VMEM((steps * SLOT_ROWS, HEAD_SIZE), jnp.bfloat16),
@@ -297,7 +307,7 @@
         project_kernel,
         (flat, flat),
         [vmem] * 3,
-        [pltpu.VMEM((pairs * rows // 2, HEAD_SIZE), jnp.float32)],
+        [pltpu.VMEM((pairs * (rows // 2 + 1), HEAD_SIZE), jnp.float32)],
     )(near, far, vocab_weight)
 
     lanes = pl.cdiv(3 * steps * half_pairs, 128) * 128

time: 40.7 us -> 39.1 us (0.961)
  Pallas kernels: 6.92 us -> 5.32 us
    pallas_call x1, Pallas kernels: 4.58 us -> 3.15 us  [shards(): call(attend_kernel, (half_rows, half_rows), [smem] + [hbm] * 5, [pltpu.VM...]
where the time goes in v3:
time: 39.1 us; the launch traced here: 38.8 us
  blocking collectives  22.5 us (58%)
  Pallas kernels  5.32 us (14%)
  starting transfers between devices  4.56 us (12%)
  waiting for transfers between devices  4.23 us (11%)
  between operations  1.5 us (4%)
  local copies, waits for them, and re-layouts  0.73 us (2%)
    all_to_all x1, blocking collectives, shards(): lax.all_to_all(spread, 'wide', 0, 0, axis_index_groups=same_core, tiled=T...  13.5 us
    all_to_all x1, blocking collectives, shards(): lax.all_to_all(stats, 'wide', 0, 0, tiled=True)  8.97 us
    ppermute x2, starting transfers between devices, swap(): return lax.ppermute(array, 'pair', [(0, 1), (1, 0)])  4.56 us
    pallas_call x1, Pallas kernels, shards(): call(attend_kernel, (half_rows, half_rows), [smem] + [hbm] * 5, [pltpu.VM...  3.15 us
    ppermute x2, waiting for transfers between devices, swap(): return lax.ppermute(array, 'pair', [(0, 1), (1, 0)])  2.89 us
    ppermute x1, waiting for transfers between devices, shards(): lax.ppermute(near, 'wide', [(source, source ^ 1) for source in range(wide)])  1.35 us
    pallas_call x1, Pallas kernels, shards(): call(finish_kernel, (jax.ShapeDtypeStruct((steps, half_pairs, width), jnp...  0.84 us
  transfers between devices with their start and end apart: 3, of which 3 were waited for; matrix products, arithmetic and copies ran while one was open for 0% of the time, Pallas kernels for 1%

profile of v3, /device:TPU:0, one launch (start us, length us, event | category | flops | bytes accessed | tf_op | source)
XLA Modules:
  0.0 38.8 jit_solution(5755605121331471231)
XLA Ops:
  0.6 0.0 copy-start.4
  0.6 0.0 copy-start
  1.4 0.0 copy-start.1
  1.5 0.0 copy-start.3
  1.5 3.1 %shard_map.113 = (bf16[64,128]{1,0:T(8,128)(2,1)}, bf16[64,128]{1,0:T(8,128)(2,1)}) custom-call(s32[1,1]{1,0:T(1,128)S(6)} %copy.16.lengths, bf16[128,128]{1,0:T(8,128)(2,1)} %bitcast.22, bf16[8192,128]{1,0:T(8,128)(2,1)} %bitcast.21, bf16[32,128]{1,0:T(8,128)(2,1)} %bitcast.25, bf16[128,128]{1,0:T(8,128)(2,1)} %bitcast.23, f32[64,128]{1,0:T(8,128)} %bitcast.24), custom_call_target="tpu_custom_call" | custom-call | tf_op jit(solution)/shard_map/pallas_call | solution.py:271
  4.6 3.0 %collective-permute-start = (bf16[64,128]{1,0:T(8,128)(2,1)}, bf16[64,128]{1,0:T(8,128)(2,1)S(1)}, u32[]{:S(2)}, u32[]{:S(2)}) collective-permute-start(bf16[64,128]{1,0:T(8,128)(2,1)} %get-tuple-element.13), channel_id=1, source_target_pairs={{0,1},{1,0},{2,3},{3,2},{4,5},{5,4},{6,7},{7,6},{8,9},{9,8},{10,11... | collective-permute-start | bytes 49160 | tf_op jit(solution)/shard_map/ppermute | solution.py:269
  7.6 0.0 copy-done.4
  7.6 0.0 copy-start.2
  7.6 0.7 %copy-done.2 = bf16[64,128]{1,0:T(8,128)(2,1)S(1)} copy-done((bf16[64,128]{1,0:T(8,128)(2,1)S(1)}, bf16[64,128]{1,0:T(8,128)(2,1)}, u32[]{:S(2)}) %copy-start.2) | copy-done | bytes 16408
  8.3 0.6 %shard_map.114 = (f32[64,128]{1,0:T(8,128)S(1)}, f32[8,128]{1,0:T(8,128)S(1)}) custom-call(f32[16]{0:T(128)S(1)} %copy-done.4, bf16[64,128]{1,0:T(8,128)(2,1)S(1)} %copy-done.2), custom_call_target="tpu_custom_call" | custom-call | tf_op jit(solution)/shard_map/pallas_call | solution.py:295
  8.9 0.6 %collective-permute-done.received = bf16[64,128]{1,0:T(8,128)(2,1)S(1)} collective-permute-done((bf16[64,128]{1,0:T(8,128)(2,1)}, bf16[64,128]{1,0:T(8,128)(2,1)S(1)}, u32[]{:S(2)}, u32[]{:S(2)}) %collective-permute-start) | collective-permute-done | bytes 16416 | tf_op jit(solution)/shard_map/ppermute | solution.py:269
  9.6 13.5 %all_to_all.10.near = bf16[8,64,128]{2,1,0:T(8,128)(2,1)S(1)} all-to-all(bf16[8,64,128]{2,1,0:T(8,128)(2,1)S(1)} %shard_map.115), channel_id=1, replica_groups={{0,4,8,12,16,20,24,28},{2,6,10,14,18,22,26,30},{1,5,9,13,17,21,25,29},{..., dimensions={0} | all-to-all | bytes 262144 | tf_op jit(solution)/shard_map/all_to_all | solution.py:304
  23.1 0.0 collective-permute-start.1
  23.1 1.3 %collective-permute-done.1.far = bf16[8,64,128]{2,1,0:T(8,128)(2,1)S(1)} collective-permute-done((bf16[8,64,128]{2,1,0:T(8,128)(2,1)S(1)}, bf16[8,64,128]{2,1,0:T(8,128)(2,1)S(1)}, u32[]{:S(2)}, u32[]{:S(2)}) %collective-permute-start.1) | collective-permute-done | bytes 131104 | tf_op jit(solution)/shard_map/ppermute | solution.py:305
  24.4 0.0 copy-done
  24.4 0.4 %shard_map.116 = (f32[16,256]{1,0:T(8,128)S(1)}, f32[16,256]{1,0:T(8,128)S(1)}) custom-call(bf16[8,64,128]{2,1,0:T(8,128)(2,1)S(1)} %all_to_all.10.near, bf16[8,64,128]{2,1,0:T(8,128)(2,1)S(1)} %collective-permute-done.1.far, bf16[4096,256]{1,0:T(8,128)(2,1)S(1)} %copy-done), custom_call_target="tpu_custom_call" | custom-call | tf_op jit(solution)/shard_map/pallas_call | solution.py:306
  24.9 1.6 %collective-permute-start.2 = (f32[16,256]{1,0:T(8,128)S(1)}, f32[16,256]{1,0:T(8,128)S(1)}, u32[]{:S(2)}, u32[]{:S(2)}) collective-permute-start(f32[16,256]{1,0:T(8,128)S(1)} %get-tuple-element.15), channel_id=1, source_target_pairs={{0,1},{1,0},{2,3},{3,2},{4,5},{5,4},{6,7},{7,6},{8,9},{9,8},{10,11... | collective-permute-start | bytes 49160 | tf_op jit(solution)/shard_map/ppermute | solution.py:269
  26.4 2.2 %collective-permute-done.2.received = f32[16,256]{1,0:T(8,128)S(1)} collective-permute-done((f32[16,256]{1,0:T(8,128)S(1)}, f32[16,256]{1,0:T(8,128)S(1)}, u32[]{:S(2)}, u32[]{:S(2)}) %collective-permute-start.2) | collective-permute-done | bytes 16416 | tf_op jit(solution)/shard_map/ppermute | solution.py:269
  28.7 0.0 copy-done.1
  28.7 0.0 copy-done.3
  28.7 0.3 shard_map.117
  29.0 9.0 %all_to_all.11.stats = f32[16,1,128]{2,1,0:T(1,128)S(1)} all-to-all(f32[16,1,128]{2,1,0:T(1,128)S(1)} %get-tuple-element.17), channel_id=1, replica_groups=mesh['wide'=16,'pair'=2] {'wide'}, dimensions={0} | all-to-all | bytes 16384 | tf_op jit(solution)/shard_map/all_to_all | solution.py:326
  38.0 0.8 %shard_map.118 = (f32[2,8,256]{2,1,0:T(8,128)}, f32[2,8]{1,0:T(2,128)}) custom-call(f32[16,256]{1,0:T(8,128)S(1)} %get-tuple-element.16.guided, f32[16,1,128]{2,1,0:T(1,128)S(1)} %all_to_all.11.stats, s32[2,8,8]{2,1,0:T(8,128)S(1)} %copy-done.1), custom_call_target="tpu_custom_call" | custom-call | tf_op jit(solution)/shard_map/pallas_call | solution.py:319
  (1 shorter events, 0.0 us)
Async XLA Ops:
  0.6 7.0 %copy-start.4 = (f32[16]{0:T(128)S(1)}, f32[16]{0:T(128)}, u32[]{:S(2)}) copy-start(f32[16]{0:T(128)} %scale.1) | copy-start | bytes 196
  0.6 23.8 %copy-start = (bf16[4096,256]{1,0:T(8,128)(2,1)S(1)}, bf16[4096,256]{1,0:T(8,128)(2,1)}, u32[]{:S(2)}) copy-start(bf16[4096,256]{1,0:T(8,128)(2,1)} %weight.1) | copy-start | bytes 6291460
  1.4 27.2 %copy-start.1 = (s32[2,8,8]{2,1,0:T(8,128)S(1)}, s32[2,8,8]{2,1,0:T(8,128)}, u32[]{:S(2)}) copy-start(s32[2,8,8]{2,1,0:T(8,128)} %blocks.3) | copy-start | bytes 1540
  1.5 27.2 %copy-start.3 = (s32[2,8]{1,0:T(2,128)S(1)}, s32[2,8]{1,0:T(2,128)}, u32[]{:S(2)}) copy-start(s32[2,8]{1,0:T(2,128)} %sampled.1) | copy-start | bytes 196
  4.6 4.9 %collective-permute-start = (bf16[64,128]{1,0:T(8,128)(2,1)}, bf16[64,128]{1,0:T(8,128)(2,1)S(1)}, u32[]{:S(2)}, u32[]{:S(2)}) collective-permute-start(bf16[64,128]{1,0:T(8,128)(2,1)} %get-tuple-element.13), channel_id=1, source_target_pairs={{0,1},{1,0},{2,3},{3,2},{4,5},{5,4},{6,7},{7,6},{8,9},{9,8},{10,11... | collective-permute-start | bytes 49160 | tf_op jit(solution)/shard_map/ppermute | solution.py:269
  7.6 0.7 %copy-start.2 = (bf16[64,128]{1,0:T(8,128)(2,1)S(1)}, bf16[64,128]{1,0:T(8,128)(2,1)}, u32[]{:S(2)}) copy-start(bf16[64,128]{1,0:T(8,128)(2,1)} %get-tuple-element.10.mine) | copy-start | bytes 49156
  23.1 1.3 %collective-permute-start.1 = (bf16[8,64,128]{2,1,0:T(8,128)(2,1)S(1)}, bf16[8,64,128]{2,1,0:T(8,128)(2,1)S(1)}, u32[]{:S(2)}, u32[]{:S(2)}) collective-permute-start(bf16[8,64,128]{2,1,0:T(8,128)(2,1)S(1)} %all_to_all.10.near), channel_id=1, source_target_pairs={{0,2},{2,0},{4,6},{6,4},{8,10},{10,8},{12,14},{14,12},{16,18},{18,... | collective-permute-start | bytes 393224 | tf_op jit(solution)/shard_map/ppermute | solution.py:305
  24.9 3.8 %collective-permute-start.2 = (f32[16,256]{1,0:T(8,128)S(1)}, f32[16,256]{1,0:T(8,128)S(1)}, u32[]{:S(2)}, u32[]{:S(2)}) collective-permute-start(f32[16,256]{1,0:T(8,128)S(1)} %get-tuple-element.15), channel_id=1, source_target_pairs={{0,1},{1,0},{2,3},{3,2},{4,5},{5,4},{6,7},{7,6},{8,9},{9,8},{10,11... | collective-permute-start | bytes 49160 | tf_op jit(solution)/shard_map/ppermute | solution.py:269

commit v4 on v3

--- a/solution.py
+++ b/solution.py
@@ -15,10 +15,9 @@
 DECODE_STEPS = 2
 SLOT_ROWS = 2 * KEY_VALUE_HEADS
 SLOT_PITCH = SLOT_ROWS + 1
-UNROLL = 32
+BLOCK = 64
 HEAD_ROWS = DECODE_STEPS * (QUERY_HEADS // KEY_VALUE_HEADS)
 NEG_FILL = -1e30
-CHUNKS = 4
 
 
 def in_vmem():
@@ -47,35 +46,43 @@
 ):
     rows = cache.shape[0]
     slots = rows // SLOT_ROWS
-    part = rows // CHUNKS
-    copies = [
-        pltpu.make_async_copy(
-            cache.at[pl.ds(index * part, part)], stage.at[pl.ds(index * part, part)], arrived.at[index]
-        )
-        for index in range(CHUNKS)
-    ]
+
+    def block_copy(block):
+        at = pl.ds(pl.multiple_of(block * (BLOCK * SLOT_ROWS), BLOCK * SLOT_ROWS), BLOCK * SLOT_ROWS)
+        return pltpu.make_async_copy(cache.at[at], stage.at[at], arrived.at[block])
+
+    def start(block, carry):
+        block_copy(block).start()
+        return carry
+
+    def clear(block, carry):
+        target = pl.multiple_of(block * (BLOCK * SLOT_PITCH), 8)
+        wide_rows[pl.ds(target, BLOCK * SLOT_PITCH), :] = jnp.zeros((BLOCK * SLOT_PITCH, HEAD_SIZE), jnp.float32)
+        return carry
+
+    def widen(block, carry):
+        block_copy(block).wait()
+        source = pl.multiple_of(block * (BLOCK * SLOT_ROWS), BLOCK * SLOT_ROWS)
+        target = pl.multiple_of(block * (BLOCK * SLOT_PITCH), 8)
+        for slot in range(BLOCK):
+            wide_rows[pl.ds(target + slot * SLOT_PITCH, SLOT_ROWS), :] = stage[
+                pl.ds(source + slot * SLOT_ROWS, SLOT_ROWS), :
+            ].astype(jnp.float32)
+        return carry
+
+    blocks = slots // BLOCK
+    live_blocks = lax.div(lengths[0, 0] + (BLOCK - 1), BLOCK)
+    lax.fori_loop(0, live_blocks, start, 0)
     small = [
-        pltpu.make_async_copy(source, target, arrived.at[CHUNKS + index])
+        pltpu.make_async_copy(source, target, arrived.at[blocks + index])
         for index, (source, target) in enumerate(
             ((gain_in, gain), (fresh_in, fresh), (queries_in, queries), (residual_in, residual))
         )
     ]
-    for copy in copies + small:
+    for copy in small:
         copy.start()
-    for index, copy in enumerate(copies):
-        copy.wait()
-
-        def widen(step, carry):
-            first = index * (part // SLOT_ROWS) + step * UNROLL
-            source = pl.multiple_of(first * SLOT_ROWS, UNROLL * SLOT_ROWS)
-            target = pl.multiple_of(first * SLOT_PITCH, 8)
-            for slot in range(UNROLL):
-                wide_rows[pl.ds(target + slot * SLOT_PITCH, SLOT_ROWS), :] = stage[
-                    pl.ds(source + slot * SLOT_ROWS, SLOT_ROWS), :
-                ].astype(jnp.float32)
-            return carry
-
-        lax.fori_loop(0, part // (SLOT_ROWS * UNROLL), widen, 0)
+    lax.fori_loop(live_blocks, blocks, clear, 0)
+    lax.fori_loop(0, live_blocks, widen, 0)
     for copy in small:
         copy.wait()
     gain_rows[pl.ds(0, QUERY_HEADS, stride=2), :] = gain[...]
@@ -280,7 +287,7 @@
             pltpu.VMEM((steps * SLOT_ROWS, HEAD_SIZE), jnp.bfloat16),
             pltpu.VMEM((rows, HEAD_SIZE), jnp.bfloat16),
             pltpu.VMEM((QUERY_HEADS, HEAD_SIZE), jnp.float32),
-            pltpu.SemaphoreType.DMA((CHUNKS + 4,)),
+            pltpu.SemaphoreType.DMA((cache.shape[2] // BLOCK + 4,)),
         ],
         limit=60 << 20,
     )(

time: 39.1 us -> 38.7 us (0.990)
  no operation moved by 1% of the time
where the time goes in v4:
time: 38.7 us; the launch traced here: 38.4 us
  blocking collectives  22.2 us (57%)
  Pallas kernels  5.04 us (13%)
  starting transfers between devices  4.48 us (12%)
  waiting for transfers between devices  4.39 us (11%)
  between operations  1.5 us (4%)
  local copies, waits for them, and re-layouts  0.73 us (2%)
    all_to_all x1, blocking collectives, shards(): lax.all_to_all(spread, 'wide', 0, 0, axis_index_groups=same_core, tiled=T...  13.3 us
    all_to_all x1, blocking collectives, shards(): lax.all_to_all(stats, 'wide', 0, 0, tiled=True)  8.97 us
    ppermute x2, starting transfers between devices, swap(): return lax.ppermute(array, 'pair', [(0, 1), (1, 0)])  4.48 us
    ppermute x2, waiting for transfers between devices, swap(): return lax.ppermute(array, 'pair', [(0, 1), (1, 0)])  3.05 us
    pallas_call x1, Pallas kernels, shards(): call(attend_kernel, (half_rows, half_rows), [smem] + [hbm] * 5, [pltpu.VM...  2.86 us
    ppermute x1, waiting for transfers between devices, shards(): lax.ppermute(near, 'wide', [(source, source ^ 1) for source in range(wide)])  1.35 us
    pallas_call x1, Pallas kernels, shards(): call(finish_kernel, (jax.ShapeDtypeStruct((steps, half_pairs, width), jnp...  0.84 us
  transfers between devices with their start and end apart: 3, of which 3 were waited for; matrix products, arithmetic and copies ran while one was open for 0% of the time, Pallas kernels for 1%

profile of v4, /device:TPU:0, one launch (start us, length us, event | category | flops | bytes accessed | tf_op | source)
XLA Modules:
  0.0 38.4 jit_solution(1114552974320779580)
XLA Ops:
  0.6 0.0 copy-start.4
  0.6 0.0 copy-start
  1.4 0.0 copy-start.1
  1.5 0.0 copy-start.3
  1.5 2.9 %shard_map.113 = (bf16[64,128]{1,0:T(8,128)(2,1)}, bf16[64,128]{1,0:T(8,128)(2,1)}) custom-call(s32[1,1]{1,0:T(1,128)S(6)} %copy.16.lengths, bf16[128,128]{1,0:T(8,128)(2,1)} %bitcast.22, bf16[8192,128]{1,0:T(8,128)(2,1)} %bitcast.21, bf16[32,128]{1,0:T(8,128)(2,1)} %bitcast.25, bf16[128,128]{1,0:T(8,128)(2,1)} %bitcast.23, f32[64,128]{1,0:T(8,128)} %bitcast.24), custom_call_target="tpu_custom_call" | custom-call | tf_op jit(solution)/shard_map/pallas_call | solution.py:278
  4.3 3.1 %collective-permute-start = (bf16[64,128]{1,0:T(8,128)(2,1)}, bf16[64,128]{1,0:T(8,128)(2,1)S(1)}, u32[]{:S(2)}, u32[]{:S(2)}) collective-permute-start(bf16[64,128]{1,0:T(8,128)(2,1)} %get-tuple-element.13), channel_id=1, source_target_pairs={{0,1},{1,0},{2,3},{3,2},{4,5},{5,4},{6,7},{7,6},{8,9},{9,8},{10,11... | collective-permute-start | bytes 49160 | tf_op jit(solution)/shard_map/ppermute | solution.py:276
  7.4 0.0 copy-done.4
  7.4 0.0 copy-start.2
  7.4 0.7 %copy-done.2 = bf16[64,128]{1,0:T(8,128)(2,1)S(1)} copy-done((bf16[64,128]{1,0:T(8,128)(2,1)S(1)}, bf16[64,128]{1,0:T(8,128)(2,1)}, u32[]{:S(2)}) %copy-start.2) | copy-done | bytes 16408
  8.1 0.6 %shard_map.114 = (f32[64,128]{1,0:T(8,128)S(1)}, f32[8,128]{1,0:T(8,128)S(1)}) custom-call(f32[16]{0:T(128)S(1)} %copy-done.4, bf16[64,128]{1,0:T(8,128)(2,1)S(1)} %copy-done.2), custom_call_target="tpu_custom_call" | custom-call | tf_op jit(solution)/shard_map/pallas_call | solution.py:302
  8.7 0.6 %collective-permute-done.received = bf16[64,128]{1,0:T(8,128)(2,1)S(1)} collective-permute-done((bf16[64,128]{1,0:T(8,128)(2,1)}, bf16[64,128]{1,0:T(8,128)(2,1)S(1)}, u32[]{:S(2)}, u32[]{:S(2)}) %collective-permute-start) | collective-permute-done | bytes 16416 | tf_op jit(solution)/shard_map/ppermute | solution.py:276
  9.4 13.3 %all_to_all.10.near = bf16[8,64,128]{2,1,0:T(8,128)(2,1)S(1)} all-to-all(bf16[8,64,128]{2,1,0:T(8,128)(2,1)S(1)} %shard_map.115), channel_id=1, replica_groups={{0,4,8,12,16,20,24,28},{2,6,10,14,18,22,26,30},{1,5,9,13,17,21,25,29},{..., dimensions={0} | all-to-all | bytes 262144 | tf_op jit(solution)/shard_map/all_to_all | solution.py:311
  22.6 0.0 collective-permute-start.1
  22.6 1.3 %collective-permute-done.1.far = bf16[8,64,128]{2,1,0:T(8,128)(2,1)S(1)} collective-permute-done((bf16[8,64,128]{2,1,0:T(8,128)(2,1)S(1)}, bf16[8,64,128]{2,1,0:T(8,128)(2,1)S(1)}, u32[]{:S(2)}, u32[]{:S(2)}) %collective-permute-start.1) | collective-permute-done | bytes 131104 | tf_op jit(solution)/shard_map/ppermute | solution.py:312
  24.0 0.0 copy-done
  24.0 0.4 %shard_map.116 = (f32[16,256]{1,0:T(8,128)S(1)}, f32[16,256]{1,0:T(8,128)S(1)}) custom-call(bf16[8,64,128]{2,1,0:T(8,128)(2,1)S(1)} %all_to_all.10.near, bf16[8,64,128]{2,1,0:T(8,128)(2,1)S(1)} %collective-permute-done.1.far, bf16[4096,256]{1,0:T(8,128)(2,1)S(1)} %copy-done), custom_call_target="tpu_custom_call" | custom-call | tf_op jit(solution)/shard_map/pallas_call | solution.py:313
  24.4 1.4 %collective-permute-start.2 = (f32[16,256]{1,0:T(8,128)S(1)}, f32[16,256]{1,0:T(8,128)S(1)}, u32[]{:S(2)}, u32[]{:S(2)}) collective-permute-start(f32[16,256]{1,0:T(8,128)S(1)} %get-tuple-element.15), channel_id=1, source_target_pairs={{0,1},{1,0},{2,3},{3,2},{4,5},{5,4},{6,7},{7,6},{8,9},{9,8},{10,11... | collective-permute-start | bytes 49160 | tf_op jit(solution)/shard_map/ppermute | solution.py:276
  25.8 2.4 %collective-permute-done.2.received = f32[16,256]{1,0:T(8,128)S(1)} collective-permute-done((f32[16,256]{1,0:T(8,128)S(1)}, f32[16,256]{1,0:T(8,128)S(1)}, u32[]{:S(2)}, u32[]{:S(2)}) %collective-permute-start.2) | collective-permute-done | bytes 16416 | tf_op jit(solution)/shard_map/ppermute | solution.py:276
  28.2 0.0 copy-done.1
  28.2 0.0 copy-done.3
  28.2 0.3 shard_map.117
  28.6 9.0 %all_to_all.11.stats = f32[16,1,128]{2,1,0:T(1,128)S(1)} all-to-all(f32[16,1,128]{2,1,0:T(1,128)S(1)} %get-tuple-element.17), channel_id=1, replica_groups=mesh['wide'=16,'pair'=2] {'wide'}, dimensions={0} | all-to-all | bytes 16384 | tf_op jit(solution)/shard_map/all_to_all | solution.py:333
  37.5 0.8 %shard_map.118 = (f32[2,8,256]{2,1,0:T(8,128)}, f32[2,8]{1,0:T(2,128)}) custom-call(f32[16,256]{1,0:T(8,128)S(1)} %get-tuple-element.16.guided, f32[16,1,128]{2,1,0:T(1,128)S(1)} %all_to_all.11.stats, s32[2,8,8]{2,1,0:T(8,128)S(1)} %copy-done.1), custom_call_target="tpu_custom_call" | custom-call | tf_op jit(solution)/shard_map/pallas_call | solution.py:326
  (1 shorter events, 0.0 us)
Async XLA Ops:
  0.6 6.8 %copy-start.4 = (f32[16]{0:T(128)S(1)}, f32[16]{0:T(128)}, u32[]{:S(2)}) copy-start(f32[16]{0:T(128)} %scale.1) | copy-start | bytes 196
  0.6 23.3 %copy-start = (bf16[4096,256]{1,0:T(8,128)(2,1)S(1)}, bf16[4096,256]{1,0:T(8,128)(2,1)}, u32[]{:S(2)}) copy-start(bf16[4096,256]{1,0:T(8,128)(2,1)} %weight.1) | copy-start | bytes 6291460
  1.4 26.8 %copy-start.1 = (s32[2,8,8]{2,1,0:T(8,128)S(1)}, s32[2,8,8]{2,1,0:T(8,128)}, u32[]{:S(2)}) copy-start(s32[2,8,8]{2,1,0:T(8,128)} %blocks.3) | copy-start | bytes 1540
  1.5 26.8 %copy-start.3 = (s32[2,8]{1,0:T(2,128)S(1)}, s32[2,8]{1,0:T(2,128)}, u32[]{:S(2)}) copy-start(s32[2,8]{1,0:T(2,128)} %sampled.1) | copy-start | bytes 196
  4.3 5.0 %collective-permute-start = (bf16[64,128]{1,0:T(8,128)(2,1)}, bf16[64,128]{1,0:T(8,128)(2,1)S(1)}, u32[]{:S(2)}, u32[]{:S(2)}) collective-permute-start(bf16[64,128]{1,0:T(8,128)(2,1)} %get-tuple-element.13), channel_id=1, source_target_pairs={{0,1},{1,0},{2,3},{3,2},{4,5},{5,4},{6,7},{7,6},{8,9},{9,8},{10,11... | collective-permute-start | bytes 49160 | tf_op jit(solution)/shard_map/ppermute | solution.py:276
  7.4 0.7 %copy-start.2 = (bf16[64,128]{1,0:T(8,128)(2,1)S(1)}, bf16[64,128]{1,0:T(8,128)(2,1)}, u32[]{:S(2)}) copy-start(bf16[64,128]{1,0:T(8,128)(2,1)} %get-tuple-element.10.mine) | copy-start | bytes 49156
  22.6 1.3 %collective-permute-start.1 = (bf16[8,64,128]{2,1,0:T(8,128)(2,1)S(1)}, bf16[8,64,128]{2,1,0:T(8,128)(2,1)S(1)}, u32[]{:S(2)}, u32[]{:S(2)}) collective-permute-start(bf16[8,64,128]{2,1,0:T(8,128)(2,1)S(1)} %all_to_all.10.near), channel_id=1, source_target_pairs={{0,2},{2,0},{4,6},{6,4},{8,10},{10,8},{12,14},{14,12},{16,18},{18,... | collective-permute-start | bytes 393224 | tf_op jit(solution)/shard_map/ppermute | solution.py:312
  24.4 3.8 %collective-permute-start.2 = (f32[16,256]{1,0:T(8,128)S(1)}, f32[16,256]{1,0:T(8,128)S(1)}, u32[]{:S(2)}, u32[]{:S(2)}) collective-permute-start(f32[16,256]{1,0:T(8,128)S(1)} %get-tuple-element.15), channel_id=1, source_target_pairs={{0,1},{1,0},{2,3},{3,2},{4,5},{5,4},{6,7},{7,6},{8,9},{9,8},{10,11... | collective-permute-start | bytes 49160 | tf_op jit(solution)/shard_map/ppermute | solution.py:276

commit v5 on v4

--- a/solution.py
+++ b/solution.py
@@ -151,33 +151,35 @@
     spread[...] = jnp.broadcast_to(guided[None], spread.shape)
 
 
-def project_kernel(near, far, weight, mine, theirs, wide_rows):
-    pairs = 2 * near.shape[0]
-    per_pair, lanes = near.shape[1:]
+def project_kernel(rows, weight, other_weight, mine, theirs, wide_rows):
+    pairs, per_pair, lanes = rows.shape
     half = pairs // 2
     pitch = per_pair + 1
-    parity = lax.axis_index("wide") % 2
-    for rows, offset in ((near, parity), (far, 1 - parity)):
-        for index in range(half):
-            wide_rows[pl.ds((2 * index + offset) * pitch, per_pair), :] = rows[index].astype(jnp.float32)
+    for pair in range(pairs):
+        wide_rows[pl.ds(pair * pitch, per_pair), :] = rows[pair].astype(jnp.float32)
 
     def head_rows(head):
         steps = [
-            wide_rows[pl.ds(head * DECODE_STEPS + step, pairs, stride=pitch), :]
-            for step in range(DECODE_STEPS)
+            wide_rows[pl.ds(head * DECODE_STEPS + step, pairs, stride=pitch), :] for step in range(DECODE_STEPS)
         ]
-        return jnp.concatenate(
-            [rows_of_step[part * half : (part + 1) * half] for part in range(2) for rows_of_step in steps], axis=0
-        ).astype(jnp.bfloat16)
-
-    total = jnp.zeros((DECODE_STEPS * pairs, mine.shape[1]), jnp.float32)
+        return jnp.concatenate(steps, axis=0).astype(jnp.bfloat16)
+
+    totals = [jnp.zeros((DECODE_STEPS * pairs, weight.shape[1]), jnp.float32)] * 2
     for two in range(per_pair // DECODE_STEPS // 2):
         left = jnp.concatenate([head_rows(2 * two), head_rows(2 * two + 1)], axis=1)
-        total = total + jnp.dot(
-            left, weight[pl.ds(two * 2 * lanes, 2 * lanes), :], preferred_element_type=jnp.float32
+        totals = [
+            total + jnp.dot(left, part[pl.ds(two * 2 * lanes, 2 * lanes), :], preferred_element_type=jnp.float32)
+            for total, part in zip(totals, (weight, other_weight))
+        ]
+    total = jnp.concatenate(totals, axis=1)
+    low, high = (
+        jnp.concatenate(
+            [total[step * pairs + part * half : step * pairs + (part + 1) * half] for step in range(DECODE_STEPS)],
+            axis=0,
         )
+        for part in range(2)
+    )
     first = lax.axis_index("pair") == 0
-    low, high = total[: mine.shape[0]], total[mine.shape[0] :]
     mine[...] = jnp.where(first, low, high)
     theirs[...] = jnp.where(first, high, low)
 
@@ -194,49 +196,80 @@
     return jnp.sum(jnp.where(eye, lanes, jnp.zeros_like(lanes)), axis=1, keepdims=True)
 
 
-def allowed_entries(blocks, shape):
-    half = blocks.shape[1]
-    flags = jnp.concatenate([blocks[step] for step in range(DECODE_STEPS)], axis=0)
-    block = lax.broadcasted_iota(jnp.int32, shape, 1) // BLK
-    flag = jnp.zeros(shape, jnp.int32)
+def allowed_entries(blocks, parity, width):
+    count = blocks.shape[1] // 2
+    flags = jnp.concatenate(
+        [blocks[step, pl.ds(2 * pair + parity, 1), :] for step in range(DECODE_STEPS) for pair in range(count)], axis=0
+    )
+    block = lax.broadcasted_iota(jnp.int32, (flags.shape[0], width), 1) // BLK
+    flag = jnp.zeros(block.shape, jnp.int32)
     for index in range(blocks.shape[2]):
         flag = jnp.where(block == index, flags[:, index : index + 1], flag)
     return flag > 0
 
 
-def stats_kernel(mine, received, blocks, sampled, guided_out, stats):
+def stats_kernel(mine, received, blocks, other_blocks, sampled, guided_out, other_out, stats):
     guided = mine[...] + received[...]
-    guided_out[...] = guided
-    count, width = guided.shape
-    half = count // DECODE_STEPS
-    allowed = allowed_entries(blocks, guided.shape)
+    rows, both = guided.shape
+    width = both // 2
+    guided_out[...] = guided[:, :width]
+    other_out[...] = guided[:, width:]
+    position = lax.axis_index("wide")
+    parity = position % 2
+    allowed = jnp.concatenate(
+        [
+            jnp.where(parity == 0, *(allowed_entries(part, q, width).astype(jnp.int32) for q in range(2)))
+            for part in (blocks, other_blocks)
+        ],
+        axis=1,
+    ) > 0
     top = jnp.max(jnp.where(allowed, guided, NEG_FILL), axis=1, keepdims=True)
     total = jnp.sum(jnp.where(allowed, jnp.exp(guided - top), 0.0), axis=1, keepdims=True)
-    chosen = jnp.concatenate([to_column(sampled[pl.ds(step, 1), :]) for step in range(DECODE_STEPS)], axis=0)
-    column = lax.broadcasted_iota(jnp.int32, guided.shape, 1) + lax.axis_index("wide") * width
+    count = rows // DECODE_STEPS
+    spot = (count, 2 * count)
+    of_parity = lax.broadcasted_iota(jnp.int32, spot, 1) == 2 * lax.broadcasted_iota(jnp.int32, spot, 0) + parity
+    chosen = jnp.concatenate(
+        [
+            jnp.sum(jnp.where(of_parity, sampled[pl.ds(step, 1), :], 0), axis=1, keepdims=True)
+            for step in range(DECODE_STEPS)
+        ],
+        axis=0,
+    )
+    lane = lax.broadcasted_iota(jnp.int32, guided.shape, 1)
+    column = jnp.where(lane < width, position * width + lane, (position ^ 1) * width + lane - width)
     picked = jnp.sum(jnp.where(column == chosen, guided, 0.0), axis=1, keepdims=True)
-    lanes = jnp.concatenate([to_lanes(top), to_lanes(total), to_lanes(picked)], axis=1)
-    pad = stats.shape[2] - lanes.shape[1]
-    if pad > 0:
-        lanes = jnp.concatenate([lanes, jnp.zeros((1, pad), jnp.float32)], axis=1)
-    stats[...] = jnp.broadcast_to(lanes[None], stats.shape)
-
-
-def finish_kernel(guided, stats, blocks, logprobs, tokens):
-    count, width = guided.shape
-    half = count // DECODE_STEPS
-    parts = stats[...].reshape(stats.shape[0], stats.shape[2])
-    tops = parts[:, 0:count]
-    top = jnp.max(tops, axis=0, keepdims=True)
-    total = jnp.sum(parts[:, count : 2 * count] * jnp.exp(tops - top), axis=0, keepdims=True)
-    picked = jnp.sum(parts[:, 2 * count : 3 * count], axis=0, keepdims=True)
-    normalizer = top + jnp.log(total)
-    token = picked - normalizer
+    stats[...] = jnp.broadcast_to(
+        jnp.concatenate([to_lanes(top), to_lanes(total), to_lanes(picked)], axis=0)[None], stats.shape
+    )
+
+
+def finish_kernel(guided, received, stats, blocks, logprobs, tokens):
+    rows, width = guided.shape
+    count = rows // DECODE_STEPS
+    chips = stats.shape[0] // 2
+    near = lax.axis_index("wide") % 2
+    token_rows = [jnp.zeros((1, 2 * count), jnp.float32)] * DECODE_STEPS
+    results = []
+    for parity in range(2):
+        parts = [stats[2 * chip + parity] for chip in range(chips)]
+        top = functools.reduce(jnp.maximum, [part[0:1] for part in parts])
+        total = sum(part[1:2] * jnp.exp(part[0:1] - top) for part in parts)
+        normalizer = top + jnp.log(total)
+        token = sum(part[2:3] for part in parts) - normalizer
+        values = jnp.where(near == parity, guided[...], received[...])
+        results.append(jnp.where(allowed_entries(blocks, parity, width), values - to_column(normalizer), 0.0))
+        spot = (count, 2 * count)
+        here = lax.broadcasted_iota(jnp.int32, spot, 1) == 2 * lax.broadcasted_iota(jnp.int32, spot, 0) + parity
+        for step in range(DECODE_STEPS):
+            mine = slice(step * count, (step + 1) * count)
+            spread = jnp.sum(jnp.where(here, to_column(token[:, mine]), 0.0), axis=0, keepdims=True)
+            token_rows[step] = token_rows[step] + spread
     for step in range(DECODE_STEPS):
-        tokens[pl.ds(step, 1), :] = token[:, step * half : (step + 1) * half]
-    allowed = allowed_entries(blocks, guided.shape)
-    result = jnp.where(allowed, guided[...] - to_column(normalizer), 0.0)
-    logprobs[...] = result.reshape(logprobs.shape)
+        tokens[pl.ds(step, 1), :] = token_rows[step]
+        for pair in range(count):
+            row = step * count + pair
+            for parity, result in enumerate(results):
+                logprobs[step, pl.ds(2 * pair + parity, 1), :] = result[row : row + 1]
 
 
 def slot_rows(array):
@@ -270,7 +303,12 @@
     cache_rows = slot_rows(cache[0, 0])
     vmem, smem, hbm = in_vmem(), in_smem(), pl.BlockSpec(memory_space=pltpu.HBM)
     half_rows = jax.ShapeDtypeStruct((rows // 2, HEAD_SIZE), jnp.bfloat16)
-    flat = jax.ShapeDtypeStruct((steps * half_pairs, width), jnp.float32)
+    chips = wide // 2
+    flat = jax.ShapeDtypeStruct((steps * chips // 2, width), jnp.float32)
+    flat_two = jax.ShapeDtypeStruct((steps * chips // 2, 2 * width), jnp.float32)
+
+    def other_core(array):
+        return lax.ppermute(array, "wide", [(source, source ^ 1) for source in range(wide)])
 
     def swap(array):
         return lax.ppermute(array, "pair", [(0, 1), (1, 0)])
@@ -304,33 +342,33 @@
         (jax.ShapeDtypeStruct(half_rows.shape, jnp.float32), jax.ShapeDtypeStruct((8, HEAD_SIZE), jnp.float32)),
         [smem, vmem],
     )(guidance, mine)
-    spread = call(combine_kernel, jax.ShapeDtypeStruct((wide // 2,) + half_rows.shape, jnp.bfloat16), [vmem] * 3)(
+    weight_in, received = lax.optimization_barrier((vocab_weight, received))
+    other_weight, other_blocks = other_core(weight_in), other_core(allowed_blocks)
+    spread = call(combine_kernel, jax.ShapeDtypeStruct((chips,) + half_rows.shape, jnp.bfloat16), [vmem] * 3)(
         factor, own_part, received
     )
     same_core = [list(range(core, wide, 2)) for core in range(2)]
-    near = lax.all_to_all(spread, "wide", 0, 0, axis_index_groups=same_core, tiled=True)
-    far = lax.ppermute(near, "wide", [(source, source ^ 1) for source in range(wide)])
+    gathered = lax.all_to_all(spread, "wide", 0, 0, axis_index_groups=same_core, tiled=True)
     mine, theirs = call(
         project_kernel,
-        (flat, flat),
+        (flat_two, flat_two),
         [vmem] * 3,
-        [pltpu.VMEM((pairs * (rows // 2 + 1), HEAD_SIZE), jnp.float32)],
-    )(near, far, vocab_weight)
-
-    lanes = pl.cdiv(3 * steps * half_pairs, 128) * 128
-    guided, stats = call(
+        [pltpu.VMEM((chips * (rows // 2 + 1), HEAD_SIZE), jnp.float32)],
+    )(gathered, vocab_weight, other_weight)
+    guided, other_guided, stats = call(
         stats_kernel,
-        (flat, jax.ShapeDtypeStruct((wide, 1, lanes), jnp.float32)),
-        [vmem] * 4,
-    )(mine, swap(theirs), allowed_blocks, sampled)
+        (flat, flat, jax.ShapeDtypeStruct((wide, 3, steps * chips // 2), jnp.float32)),
+        [vmem] * 5,
+    )(mine, swap(theirs), allowed_blocks, other_blocks, sampled)
+    other_guided = other_core(other_guided)
     logprobs, tokens = call(
         finish_kernel,
         (
             jax.ShapeDtypeStruct((steps, half_pairs, width), jnp.float32),
             jax.ShapeDtypeStruct((steps, half_pairs), jnp.float32),
         ),
-        [vmem] * 3,
-    )(guided, lax.all_to_all(stats, "wide", 0, 0, tiled=True), allowed_blocks)
+        [vmem] * 4,
+    )(guided, other_guided, lax.all_to_all(stats, "wide", 0, 0, tiled=True), allowed_blocks)
     return (logprobs, tokens)
 
 

time: 38.7 us -> 39.5 us (1.021)
  blocking collectives: 22.2 us -> 23.3 us
    all_to_all x1, blocking collectives: 13.3 us -> 14 us  [shards(): lax.all_to_all(spread, 'wide', 0, 0, axis_index_groups=same_core, tiled=T...]
    ppermute x1 -> x3, waiting for transfers between devices: 1.35 us -> 1.17 us  [other_core(): lax.ppermute(array, 'wide', [(source, source ^ 1) for source in range(wid...]
  transfers between devices with their start and end apart: 3 -> 5, of which waited for: 3 -> 3; matrix products, arithmetic and copies ran while one was open for 0% -> 0% of each run, Pallas kernels for 1% -> 1%
where the time goes in v5:
time: 39.5 us; the launch traced here: 39.3 us
  blocking collectives  23.3 us (59%)
  Pallas kernels  5.29 us (13%)
  starting transfers between devices  4.42 us (11%)
  waiting for transfers between devices  4.09 us (10%)
  between operations  1.5 us (4%)
  local copies, waits for them, and re-layouts  0.73 us (2%)
    all_to_all x1, blocking collectives, shards(): lax.all_to_all(spread, 'wide', 0, 0, axis_index_groups=same_core, tiled=T...  14 us
    all_to_all x1, blocking collectives, shards(): lax.all_to_all(stats, 'wide', 0, 0, tiled=True)  9.34 us
    ppermute x2, starting transfers between devices, swap(): return lax.ppermute(array, 'pair', [(0, 1), (1, 0)])  4.34 us
    pallas_call x1, Pallas kernels, shards(): call(attend_kernel, (half_rows, half_rows), [smem] + [hbm] * 5, [pltpu.VM...  2.94 us
    ppermute x2, waiting for transfers between devices, swap(): return lax.ppermute(array, 'pair', [(0, 1), (1, 0)])  2.92 us
    ppermute x3, waiting for transfers between devices, other_core(): lax.ppermute(array, 'wide', [(source, source ^ 1) for source in range(wid...  1.17 us
    pallas_call x1, Pallas kernels, shards(): call(finish_kernel, (jax.ShapeDtypeStruct((steps, half_pairs, width), jnp...  0.82 us
  transfers between devices with their start and end apart: 5, of which 3 were waited for; matrix products, arithmetic and copies ran while one was open for 0% of the time, Pallas kernels for 1%

profile of v5, /device:TPU:0, one launch (start us, length us, event | category | flops | bytes accessed | tf_op | source)
XLA Modules:
  0.0 39.3 jit_solution(2273562736535828606)
XLA Ops:
  0.6 0.0 copy-start
  0.6 0.0 copy-start.4
  1.4 2.9 %shard_map.113 = (bf16[64,128]{1,0:T(8,128)(2,1)}, bf16[64,128]{1,0:T(8,128)(2,1)}) custom-call(s32[1,1]{1,0:T(1,128)S(6)} %copy.16.lengths, bf16[128,128]{1,0:T(8,128)(2,1)} %bitcast.22, bf16[8192,128]{1,0:T(8,128)(2,1)} %bitcast.21, bf16[32,128]{1,0:T(8,128)(2,1)} %bitcast.25, bf16[128,128]{1,0:T(8,128)(2,1)} %bitcast.23, f32[64,128]{1,0:T(8,128)} %bitcast.24), custom_call_target="tpu_custom_call" | custom-call | tf_op jit(solution)/shard_map/pallas_call | solution.py:316
  4.4 2.8 %collective-permute-start = (bf16[64,128]{1,0:T(8,128)(2,1)}, bf16[64,128]{1,0:T(8,128)(2,1)S(1)}, u32[]{:S(2)}, u32[]{:S(2)}) collective-permute-start(bf16[64,128]{1,0:T(8,128)(2,1)} %get-tuple-element.16), channel_id=1, source_target_pairs={{0,1},{1,0},{2,3},{3,2},{4,5},{5,4},{6,7},{7,6},{8,9},{9,8},{10,11... | collective-permute-start | bytes 49160 | tf_op jit(solution)/shard_map/ppermute | solution.py:314
  7.2 1.9 %collective-permute-done.received = bf16[64,128]{1,0:T(8,128)(2,1)S(1)} collective-permute-done((bf16[64,128]{1,0:T(8,128)(2,1)}, bf16[64,128]{1,0:T(8,128)(2,1)S(1)}, u32[]{:S(2)}, u32[]{:S(2)}) %collective-permute-start) | collective-permute-done | bytes 16416 | tf_op jit(solution)/shard_map/ppermute | solution.py:314
  9.1 0.0 copy-done
  9.1 0.0 collective-permute-start.1
  9.1 0.0 copy-done.4
  9.1 0.0 copy-start.2
  9.1 0.7 %copy-done.2 = bf16[64,128]{1,0:T(8,128)(2,1)S(1)} copy-done((bf16[64,128]{1,0:T(8,128)(2,1)S(1)}, bf16[64,128]{1,0:T(8,128)(2,1)}, u32[]{:S(2)}) %copy-start.2) | copy-done | bytes 16408
  9.8 0.6 %shard_map.114 = (f32[64,128]{1,0:T(8,128)S(1)}, f32[8,128]{1,0:T(8,128)S(1)}) custom-call(f32[16]{0:T(128)S(1)} %copy-done.4, bf16[64,128]{1,0:T(8,128)(2,1)S(1)} %copy-done.2), custom_call_target="tpu_custom_call" | custom-call | tf_op jit(solution)/shard_map/pallas_call | solution.py:340
  10.4 14.0 %all_to_all.10.rows = bf16[8,64,128]{2,1,0:T(8,128)(2,1)S(1)} all-to-all(bf16[8,64,128]{2,1,0:T(8,128)(2,1)S(1)} %shard_map.115), channel_id=1, replica_groups={{0,4,8,12,16,20,24,28},{2,6,10,14,18,22,26,30},{1,5,9,13,17,21,25,29},{..., dimensions={0} | all-to-all | bytes 262144 | tf_op jit(solution)/shard_map/all_to_all | solution.py:351
  24.4 0.0 collective-permute-done.1.other_weight
  24.4 0.7 %shard_map.116 = (f32[8,512]{1,0:T(8,128)S(1)}, f32[8,512]{1,0:T(8,128)S(1)}) custom-call(bf16[8,64,128]{2,1,0:T(8,128)(2,1)S(1)} %all_to_all.10.rows, bf16[4096,256]{1,0:T(8,128)(2,1)S(1)} %copy-done, bf16[4096,256]{1,0:T(8,128)(2,1)S(1)} %collective-permute-done.1.other_weight), custom_call_target="tpu_custom_call" | custom-call | tf_op jit(solution)/shard_map/pallas_call | solution.py:352
  25.0 1.6 %collective-permute-start.2 = (f32[8,512]{1,0:T(8,128)S(1)}, f32[8,512]{1,0:T(8,128)S(1)}, u32[]{:S(2)}, u32[]{:S(2)}) collective-permute-start(f32[8,512]{1,0:T(8,128)S(1)} %get-tuple-element.20), channel_id=1, source_target_pairs={{0,1},{1,0},{2,3},{3,2},{4,5},{5,4},{6,7},{7,6},{8,9},{9,8},{10,11... | collective-permute-start | bytes 49160 | tf_op jit(solution)/shard_map/ppermute | solution.py:314
  26.6 0.0 collective-permute-start.3
  26.6 1.2 %collective-permute-done.3.other_blocks = s32[2,8,8]{2,1,0:T(8,128)S(1)} collective-permute-done((s32[2,8,8]{2,1,0:T(8,128)S(1)}, s32[2,8,8]{2,1,0:T(8,128)S(1)}, u32[]{:S(2)}, u32[]{:S(2)}) %collective-permute-start.3) | collective-permute-done | bytes 544 | tf_op jit(solution)/shard_map/ppermute | solution.py:311
  27.8 1.0 %collective-permute-done.2.received = f32[8,512]{1,0:T(8,128)S(1)} collective-permute-done((f32[8,512]{1,0:T(8,128)S(1)}, f32[8,512]{1,0:T(8,128)S(1)}, u32[]{:S(2)}, u32[]{:S(2)}) %collective-permute-start.2) | collective-permute-done | bytes 16416 | tf_op jit(solution)/shard_map/ppermute | solution.py:314
  28.8 0.0 copy-done.3
  28.8 0.3 shard_map.117
  29.1 0.1 collective-permute-start.4
  29.2 9.3 %all_to_all.11.stats = f32[16,3,8]{2,1,0:T(4,128)S(1)} all-to-all(f32[16,3,8]{2,1,0:T(4,128)S(1)} %get-tuple-element.23), channel_id=1, replica_groups=mesh['wide'=16,'pair'=2] {'wide'}, dimensions={0} | all-to-all | bytes 3072 | tf_op jit(solution)/shard_map/all_to_all | solution.py:371
  38.5 0.0 collective-permute-done.4.received
  38.5 0.8 %shard_map.118 = (f32[2,8,256]{2,1,0:T(8,128)}, f32[2,8]{1,0:T(2,128)}) custom-call(f32[8,256]{1,0:T(8,128)S(1)} %get-tuple-element.21.guided, f32[8,256]{1,0:T(8,128)S(1)} %collective-permute-done.4.received, f32[16,3,8]{2,1,0:T(4,128)S(1)} %all_to_all.11.stats, s32[2,8,8]{2,1,0:T(8,128)S(1)} %copy-done.1), custom_call_target="tpu_custom_call" | custom-call | tf_op jit(solution)/shard_map/pallas_call | solution.py:364
  (4 shorter events, 0.0 us)
Async XLA Ops:
  0.6 8.5 %copy-start = (bf16[4096,256]{1,0:T(8,128)(2,1)S(1)}, bf16[4096,256]{1,0:T(8,128)(2,1)}, u32[]{:S(2)}) copy-start(bf16[4096,256]{1,0:T(8,128)(2,1)} %weight.1) | copy-start | bytes 6291460
  0.6 8.5 %copy-start.4 = (f32[16]{0:T(128)S(1)}, f32[16]{0:T(128)}, u32[]{:S(2)}) copy-start(f32[16]{0:T(128)} %scale.1) | copy-start | bytes 196
  4.4 4.7 %collective-permute-start = (bf16[64,128]{1,0:T(8,128)(2,1)}, bf16[64,128]{1,0:T(8,128)(2,1)S(1)}, u32[]{:S(2)}, u32[]{:S(2)}) collective-permute-start(bf16[64,128]{1,0:T(8,128)(2,1)} %get-tuple-element.16), channel_id=1, source_target_pairs={{0,1},{1,0},{2,3},{3,2},{4,5},{5,4},{6,7},{7,6},{8,9},{9,8},{10,11... | collective-permute-start | bytes 49160 | tf_op jit(solution)/shard_map/ppermute | solution.py:314
  9.1 15.3 %collective-permute-start.1 = (bf16[4096,256]{1,0:T(8,128)(2,1)S(1)}, bf16[4096,256]{1,0:T(8,128)(2,1)S(1)}, u32[]{:S(2)}, u32[]{:S(2)}) collective-permute-start(bf16[4096,256]{1,0:T(8,128)(2,1)S(1)} %copy-done), channel_id=1, source_target_pairs={{0,2},{2,0},{4,6},{6,4},{8,10},{10,8},{12,14},{14,12},{16,18},{18,... | collective-permute-start | bytes 6291464 | tf_op jit(solution)/shard_map/ppermute | solution.py:311
  9.1 0.7 %copy-start.2 = (bf16[64,128]{1,0:T(8,128)(2,1)S(1)}, bf16[64,128]{1,0:T(8,128)(2,1)}, u32[]{:S(2)}) copy-start(bf16[64,128]{1,0:T(8,128)(2,1)} %get-tuple-element.13.mine) | copy-start | bytes 49156
  24.4 2.2 %copy-start.1 = (s32[2,8,8]{2,1,0:T(8,128)S(1)}, s32[2,8,8]{2,1,0:T(8,128)}, u32[]{:S(2)}) copy-start(s32[2,8,8]{2,1,0:T(8,128)} %blocks.3) | copy-start | bytes 1540
  24.4 4.4 %copy-start.3 = (s32[2,8]{1,0:T(2,128)S(1)}, s32[2,8]{1,0:T(2,128)}, u32[]{:S(2)}) copy-start(s32[2,8]{1,0:T(2,128)} %sampled.1) | copy-start | bytes 196
  25.0 3.7 %collective-permute-start.2 = (f32[8,512]{1,0:T(8,128)S(1)}, f32[8,512]{1,0:T(8,128)S(1)}, u32[]{:S(2)}, u32[]{:S(2)}) collective-permute-start(f32[8,512]{1,0:T(8,128)S(1)} %get-tuple-element.20), channel_id=1, source_target_pairs={{0,1},{1,0},{2,3},{3,2},{4,5},{5,4},{6,7},{7,6},{8,9},{9,8},{10,11... | collective-permute-start | bytes 49160 | tf_op jit(solution)/shard_map/ppermute | solution.py:314
  26.6 1.2 %collective-permute-start.3 = (s32[2,8,8]{2,1,0:T(8,128)S(1)}, s32[2,8,8]{2,1,0:T(8,128)S(1)}, u32[]{:S(2)}, u32[]{:S(2)}) collective-permute-start(s32[2,8,8]{2,1,0:T(8,128)S(1)} %copy-done.1), channel_id=1, source_target_pairs={{0,2},{2,0},{4,6},{6,4},{8,10},{10,8},{12,14},{14,12},{16,18},{18,... | collective-permute-start | bytes 1544 | tf_op jit(solution)/shard_map/ppermute | solution.py:311
  29.1 9.4 %collective-permute-start.4 = (f32[8,256]{1,0:T(8,128)S(1)}, f32[8,256]{1,0:T(8,128)S(1)}, u32[]{:S(2)}, u32[]{:S(2)}) collective-permute-start(f32[8,256]{1,0:T(8,128)S(1)} %get-tuple-element.22), channel_id=1, source_target_pairs={{0,2},{2,0},{4,6},{6,4},{8,10},{10,8},{12,14},{14,12},{16,18},{18,... | collective-permute-start | bytes 24584 | tf_op jit(solution)/shard_map/ppermute | solution.py:311

commit v6 on v5

--- a/solution.py
+++ b/solution.py
@@ -342,7 +342,7 @@
         (jax.ShapeDtypeStruct(half_rows.shape, jnp.float32), jax.ShapeDtypeStruct((8, HEAD_SIZE), jnp.float32)),
         [smem, vmem],
     )(guidance, mine)
-    weight_in, received = lax.optimization_barrier((vocab_weight, received))
+    weight_in, own_part, received = lax.optimization_barrier((vocab_weight, own_part, received))
     other_weight, other_blocks = other_core(weight_in), other_core(allowed_blocks)
     spread = call(combine_kernel, jax.ShapeDtypeStruct((chips,) + half_rows.shape, jnp.bfloat16), [vmem] * 3)(
         factor, own_part, received

time: 39.5 us -> 38.4 us (0.972)
  waiting for transfers between devices: 4.09 us -> 2.81 us
  starting transfers between devices: 4.42 us -> 5.06 us
  Pallas kernels: 5.29 us -> 4.89 us
    ppermute x2, waiting for transfers between devices: 2.92 us -> 1.63 us  [swap(): return lax.ppermute(array, 'pair', [(0, 1), (1, 0)])]
    ppermute x2, starting transfers between devices: 4.34 us -> 4.98 us  [swap(): return lax.ppermute(array, 'pair', [(0, 1), (1, 0)])]
    pallas_call x1, Pallas kernels: 2.94 us -> 2.54 us  [shards(): call(attend_kernel, (half_rows, half_rows), [smem] + [hbm] * 5, [pltpu.VM...]
  transfers between devices with their start and end apart: 5 -> 5, of which waited for: 3 -> 3; matrix products, arithmetic and copies ran while one was open for 0% -> 0% of each run, Pallas kernels for 1% -> 2%
where the time goes in v6:
time: 38.4 us; the launch traced here: 38.1 us
  blocking collectives  23.1 us (60%)
  starting transfers between devices  5.06 us (13%)
  Pallas kernels  4.89 us (13%)
  waiting for transfers between devices  2.81 us (7%)
  between operations  1.49 us (4%)
  local copies, waits for them, and re-layouts  0.73 us (2%)
    all_to_all x1, blocking collectives, shards(): lax.all_to_all(spread, 'wide', 0, 0, axis_index_groups=same_core, tiled=T...  13.7 us
    all_to_all x1, blocking collectives, shards(): lax.all_to_all(stats, 'wide', 0, 0, tiled=True)  9.34 us
    ppermute x2, starting transfers between devices, swap(): return lax.ppermute(array, 'pair', [(0, 1), (1, 0)])  4.98 us
    pallas_call x1, Pallas kernels, shards(): call(attend_kernel, (half_rows, half_rows), [smem] + [hbm] * 5, [pltpu.VM...  2.54 us
    ppermute x2, waiting for transfers between devices, swap(): return lax.ppermute(array, 'pair', [(0, 1), (1, 0)])  1.63 us
    ppermute x3, waiting for transfers between devices, other_core(): lax.ppermute(array, 'wide', [(source, source ^ 1) for source in range(wid...  1.17 us
    pallas_call x1, Pallas kernels, shards(): call(finish_kernel, (jax.ShapeDtypeStruct((steps, half_pairs, width), jnp...  0.82 us
  transfers between devices with their start and end apart: 5, of which 3 were waited for; matrix products, arithmetic and copies ran while one was open for 0% of the time, Pallas kernels for 2%

profile of v6, /device:TPU:0, one launch (start us, length us, event | category | flops | bytes accessed | tf_op | source)
XLA Modules:
  0.0 38.1 jit_solution(7455030675254644067)
XLA Ops:
  0.6 0.0 copy-start.4
  0.6 0.0 copy-start
  1.4 2.5 %shard_map.113 = (bf16[64,128]{1,0:T(8,128)(2,1)}, bf16[64,128]{1,0:T(8,128)(2,1)}) custom-call(s32[1,1]{1,0:T(1,128)S(6)} %copy.16.lengths, bf16[128,128]{1,0:T(8,128)(2,1)} %bitcast.22, bf16[8192,128]{1,0:T(8,128)(2,1)} %bitcast.21, bf16[32,128]{1,0:T(8,128)(2,1)} %bitcast.25, bf16[128,128]{1,0:T(8,128)(2,1)} %bitcast.23, f32[64,128]{1,0:T(8,128)} %bitcast.24), custom_call_target="tpu_custom_call" | custom-call | tf_op jit(solution)/shard_map/pallas_call | solution.py:316
  4.0 3.4 %collective-permute-start = (bf16[64,128]{1,0:T(8,128)(2,1)}, bf16[64,128]{1,0:T(8,128)(2,1)S(1)}, u32[]{:S(2)}, u32[]{:S(2)}) collective-permute-start(bf16[64,128]{1,0:T(8,128)(2,1)} %get-tuple-element.17), channel_id=1, source_target_pairs={{0,1},{1,0},{2,3},{3,2},{4,5},{5,4},{6,7},{7,6},{8,9},{9,8},{10,11... | collective-permute-start | bytes 49160 | tf_op jit(solution)/shard_map/ppermute | solution.py:314
  7.4 0.0 copy-done.4
  7.4 0.7 %copy-done.2 = bf16[64,128]{1,0:T(8,128)(2,1)S(1)} copy-done((bf16[64,128]{1,0:T(8,128)(2,1)S(1)}, bf16[64,128]{1,0:T(8,128)(2,1)}, u32[]{:S(2)}) %copy-start.2) | copy-done | bytes 16408
  8.1 0.6 %shard_map.114 = (f32[64,128]{1,0:T(8,128)S(1)}, f32[8,128]{1,0:T(8,128)S(1)}) custom-call(f32[16]{0:T(128)S(1)} %copy-done.4, bf16[64,128]{1,0:T(8,128)(2,1)S(1)} %copy-done.2), custom_call_target="tpu_custom_call" | custom-call | tf_op jit(solution)/shard_map/pallas_call | solution.py:340
  8.7 0.6 %collective-permute-done.received = bf16[64,128]{1,0:T(8,128)(2,1)S(1)} collective-permute-done((bf16[64,128]{1,0:T(8,128)(2,1)}, bf16[64,128]{1,0:T(8,128)(2,1)S(1)}, u32[]{:S(2)}, u32[]{:S(2)}) %collective-permute-start) | collective-permute-done | bytes 16416 | tf_op jit(solution)/shard_map/ppermute | solution.py:314
  9.3 0.0 copy-done
  9.3 0.0 collective-permute-start.1
  9.4 13.7 %all_to_all.10.rows = bf16[8,64,128]{2,1,0:T(8,128)(2,1)S(1)} all-to-all(bf16[8,64,128]{2,1,0:T(8,128)(2,1)S(1)} %shard_map.115), channel_id=1, replica_groups={{0,4,8,12,16,20,24,28},{2,6,10,14,18,22,26,30},{1,5,9,13,17,21,25,29},{..., dimensions={0} | all-to-all | bytes 262144 | tf_op jit(solution)/shard_map/all_to_all | solution.py:351
  23.1 0.0 collective-permute-done.1.other_weight
  23.1 0.7 %shard_map.116 = (f32[8,512]{1,0:T(8,128)S(1)}, f32[8,512]{1,0:T(8,128)S(1)}) custom-call(bf16[8,64,128]{2,1,0:T(8,128)(2,1)S(1)} %all_to_all.10.rows, bf16[4096,256]{1,0:T(8,128)(2,1)S(1)} %copy-done, bf16[4096,256]{1,0:T(8,128)(2,1)S(1)} %collective-permute-done.1.other_weight), custom_call_target="tpu_custom_call" | custom-call | tf_op jit(solution)/shard_map/pallas_call | solution.py:352
  23.8 1.6 %collective-permute-start.2 = (f32[8,512]{1,0:T(8,128)S(1)}, f32[8,512]{1,0:T(8,128)S(1)}, u32[]{:S(2)}, u32[]{:S(2)}) collective-permute-start(f32[8,512]{1,0:T(8,128)S(1)} %get-tuple-element.22), channel_id=1, source_target_pairs={{0,1},{1,0},{2,3},{3,2},{4,5},{5,4},{6,7},{7,6},{8,9},{9,8},{10,11... | collective-permute-start | bytes 49160 | tf_op jit(solution)/shard_map/ppermute | solution.py:314
  25.3 0.0 copy-done.1
  25.3 0.0 collective-permute-start.3
  25.3 1.2 %collective-permute-done.3.other_blocks = s32[2,8,8]{2,1,0:T(8,128)S(1)} collective-permute-done((s32[2,8,8]{2,1,0:T(8,128)S(1)}, s32[2,8,8]{2,1,0:T(8,128)S(1)}, u32[]{:S(2)}, u32[]{:S(2)}) %collective-permute-start.3) | collective-permute-done | bytes 544 | tf_op jit(solution)/shard_map/ppermute | solution.py:311
  26.5 1.0 %collective-permute-done.2.received = f32[8,512]{1,0:T(8,128)S(1)} collective-permute-done((f32[8,512]{1,0:T(8,128)S(1)}, f32[8,512]{1,0:T(8,128)S(1)}, u32[]{:S(2)}, u32[]{:S(2)}) %collective-permute-start.2) | collective-permute-done | bytes 16416 | tf_op jit(solution)/shard_map/ppermute | solution.py:314
  27.5 0.0 copy-done.3
  27.5 0.3 shard_map.117
  27.8 0.1 collective-permute-start.4
  27.9 9.3 %all_to_all.11.stats = f32[16,3,8]{2,1,0:T(4,128)S(1)} all-to-all(f32[16,3,8]{2,1,0:T(4,128)S(1)} %get-tuple-element.25), channel_id=1, replica_groups=mesh['wide'=16,'pair'=2] {'wide'}, dimensions={0} | all-to-all | bytes 3072 | tf_op jit(solution)/shard_map/all_to_all | solution.py:371
  37.2 0.0 collective-permute-done.4.received
  37.2 0.8 %shard_map.118 = (f32[2,8,256]{2,1,0:T(8,128)}, f32[2,8]{1,0:T(2,128)}) custom-call(f32[8,256]{1,0:T(8,128)S(1)} %get-tuple-element.23.guided, f32[8,256]{1,0:T(8,128)S(1)} %collective-permute-done.4.received, f32[16,3,8]{2,1,0:T(4,128)S(1)} %all_to_all.11.stats, s32[2,8,8]{2,1,0:T(8,128)S(1)} %copy-done.1), custom_call_target="tpu_custom_call" | custom-call | tf_op jit(solution)/shard_map/pallas_call | solution.py:364
  (4 shorter events, 0.0 us)
Async XLA Ops:
  0.6 6.8 %copy-start.4 = (f32[16]{0:T(128)S(1)}, f32[16]{0:T(128)}, u32[]{:S(2)}) copy-start(f32[16]{0:T(128)} %scale.1) | copy-start | bytes 196
  0.6 8.7 %copy-start = (bf16[4096,256]{1,0:T(8,128)(2,1)S(1)}, bf16[4096,256]{1,0:T(8,128)(2,1)}, u32[]{:S(2)}) copy-start(bf16[4096,256]{1,0:T(8,128)(2,1)} %weight.1) | copy-start | bytes 6291460
  4.0 5.3 %collective-permute-start = (bf16[64,128]{1,0:T(8,128)(2,1)}, bf16[64,128]{1,0:T(8,128)(2,1)S(1)}, u32[]{:S(2)}, u32[]{:S(2)}) collective-permute-start(bf16[64,128]{1,0:T(8,128)(2,1)} %get-tuple-element.17), channel_id=1, source_target_pairs={{0,1},{1,0},{2,3},{3,2},{4,5},{5,4},{6,7},{7,6},{8,9},{9,8},{10,11... | collective-permute-start | bytes 49160 | tf_op jit(solution)/shard_map/ppermute | solution.py:314
  7.4 0.7 %copy-start.2 = (bf16[64,128]{1,0:T(8,128)(2,1)S(1)}, bf16[64,128]{1,0:T(8,128)(2,1)}, u32[]{:S(2)}) copy-start(bf16[64,128]{1,0:T(8,128)(2,1)} %get-tuple-element.14.mine) | copy-start | bytes 49156
  9.3 13.8 %collective-permute-start.1 = (bf16[4096,256]{1,0:T(8,128)(2,1)S(1)}, bf16[4096,256]{1,0:T(8,128)(2,1)S(1)}, u32[]{:S(2)}, u32[]{:S(2)}) collective-permute-start(bf16[4096,256]{1,0:T(8,128)(2,1)S(1)} %copy-done), channel_id=1, source_target_pairs={{0,2},{2,0},{4,6},{6,4},{8,10},{10,8},{12,14},{14,12},{16,18},{18,... | collective-permute-start | bytes 6291464 | tf_op jit(solution)/shard_map/ppermute | solution.py:311
  23.1 2.2 %copy-start.1 = (s32[2,8,8]{2,1,0:T(8,128)S(1)}, s32[2,8,8]{2,1,0:T(8,128)}, u32[]{:S(2)}) copy-start(s32[2,8,8]{2,1,0:T(8,128)} %blocks.3) | copy-start | bytes 1540
  23.1 4.4 %copy-start.3 = (s32[2,8]{1,0:T(2,128)S(1)}, s32[2,8]{1,0:T(2,128)}, u32[]{:S(2)}) copy-start(s32[2,8]{1,0:T(2,128)} %sampled.1) | copy-start | bytes 196
  23.8 3.7 %collective-permute-start.2 = (f32[8,512]{1,0:T(8,128)S(1)}, f32[8,512]{1,0:T(8,128)S(1)}, u32[]{:S(2)}, u32[]{:S(2)}) collective-permute-start(f32[8,512]{1,0:T(8,128)S(1)} %get-tuple-element.22), channel_id=1, source_target_pairs={{0,1},{1,0},{2,3},{3,2},{4,5},{5,4},{6,7},{7,6},{8,9},{9,8},{10,11... | collective-permute-start | bytes 49160 | tf_op jit(solution)/shard_map/ppermute | solution.py:314
  25.3 1.2 %collective-permute-start.3 = (s32[2,8,8]{2,1,0:T(8,128)S(1)}, s32[2,8,8]{2,1,0:T(8,128)S(1)}, u32[]{:S(2)}, u32[]{:S(2)}) collective-permute-start(s32[2,8,8]{2,1,0:T(8,128)S(1)} %copy-done.1), channel_id=1, source_target_pairs={{0,2},{2,0},{4,6},{6,4},{8,10},{10,8},{12,14},{14,12},{16,18},{18,... | collective-permute-start | bytes 1544 | tf_op jit(solution)/shard_map/ppermute | solution.py:311
  27.8 9.4 %collective-permute-start.4 = (f32[8,256]{1,0:T(8,128)S(1)}, f32[8,256]{1,0:T(8,128)S(1)}, u32[]{:S(2)}, u32[]{:S(2)}) collective-permute-start(f32[8,256]{1,0:T(8,128)S(1)} %get-tuple-element.24), channel_id=1, source_target_pairs={{0,2},{2,0},{4,6},{6,4},{8,10},{10,8},{12,14},{14,12},{16,18},{18,... | collective-permute-start | bytes 24584 | tf_op jit(solution)/shard_map/ppermute | solution.py:311

commit v7 on v6

--- a/solution.py
+++ b/solution.py
@@ -327,7 +327,7 @@
             pltpu.VMEM((QUERY_HEADS, HEAD_SIZE), jnp.float32),
             pltpu.SemaphoreType.DMA((cache.shape[2] // BLOCK + 4,)),
         ],
-        limit=60 << 20,
+        limit=58 << 20,
     )(
         lengths,
         step_rows(queries[0, 0]),
@@ -342,8 +342,7 @@
         (jax.ShapeDtypeStruct(half_rows.shape, jnp.float32), jax.ShapeDtypeStruct((8, HEAD_SIZE), jnp.float32)),
         [smem, vmem],
     )(guidance, mine)
-    weight_in, own_part, received = lax.optimization_barrier((vocab_weight, own_part, received))
-    other_weight, other_blocks = other_core(weight_in), other_core(allowed_blocks)
+    other_weight, other_blocks = other_core(vocab_weight), other_core(allowed_blocks)
     spread = call(combine_kernel, jax.ShapeDtypeStruct((chips,) + half_rows.shape, jnp.bfloat16), [vmem] * 3)(
         factor, own_part, received
     )

time: 38.4 us -> 37.9 us (0.987)
  starting transfers between devices: 5.06 us -> 4.43 us
    ppermute x2, starting transfers between devices: 4.98 us -> 3.84 us  [swap(): return lax.ppermute(array, 'pair', [(0, 1), (1, 0)])]
    ppermute x3, starting transfers between devices: 0.08 us -> 0.59 us  [other_core(): lax.ppermute(array, 'wide', [(source, source ^ 1) for source in range(wid...]
    ppermute x2, waiting for transfers between devices: 1.63 us -> 2.02 us  [swap(): return lax.ppermute(array, 'pair', [(0, 1), (1, 0)])]
  transfers between devices with their start and end apart: 5 -> 5, of which waited for: 3 -> 3; matrix products, arithmetic and copies ran while one was open for 0% -> 0% of each run, Pallas kernels for 2% -> 9%
where the time goes in v7:
time: 37.9 us; the launch traced here: 37.7 us
  blocking collectives  22.9 us (60%)
  Pallas kernels  5.05 us (13%)
  starting transfers between devices  4.43 us (12%)
  waiting for transfers between devices  3.19 us (8%)
  between operations  1.39 us (4%)
  local copies, waits for them, and re-layouts  0.73 us (2%)
    all_to_all x1, blocking collectives, shards(): lax.all_to_all(spread, 'wide', 0, 0, axis_index_groups=same_core, tiled=T...  13.7 us
    all_to_all x1, blocking collectives, shards(): lax.all_to_all(stats, 'wide', 0, 0, tiled=True)  9.2 us
    ppermute x2, starting transfers between devices, swap(): return lax.ppermute(array, 'pair', [(0, 1), (1, 0)])  3.84 us
    pallas_call x1, Pallas kernels, shards(): call(attend_kernel, (half_rows, half_rows), [smem] + [hbm] * 5, [pltpu.VM...  2.7 us
    ppermute x2, waiting for transfers between devices, swap(): return lax.ppermute(array, 'pair', [(0, 1), (1, 0)])  2.02 us
    ppermute x3, waiting for transfers between devices, other_core(): lax.ppermute(array, 'wide', [(source, source ^ 1) for source in range(wid...  1.17 us
    pallas_call x1, Pallas kernels, shards(): call(finish_kernel, (jax.ShapeDtypeStruct((steps, half_pairs, width), jnp...  0.82 us
  transfers between devices with their start and end apart: 5, of which 3 were waited for; matrix products, arithmetic and copies ran while one was open for 0% of the time, Pallas kernels for 9%

profile of v7, /device:TPU:0, one launch (start us, length us, event | category | flops | bytes accessed | tf_op | source)
XLA Modules:
  0.0 37.7 jit_solution(8655776747246495693)
XLA Ops:
  0.6 0.0 copy-start
  0.6 0.0 copy-start.4
  0.7 0.5 %collective-permute-start.1 = (bf16[4096,256]{1,0:T(8,128)(2,1)}, bf16[4096,256]{1,0:T(8,128)(2,1)S(1)}, u32[]{:S(2)}, u32[]{:S(2)}) collective-permute-start(bf16[4096,256]{1,0:T(8,128)(2,1)} %weight.1), channel_id=1, source_target_pairs={{0,2},{2,0},{4,6},{6,4},{8,10},{10,8},{12,14},{14,12},{16,18},{18,... | collective-permute-start | bytes 6291464 | tf_op jit(solution)/shard_map/ppermute | solution.py:311
  1.9 2.7 %shard_map.113 = (bf16[64,128]{1,0:T(8,128)(2,1)}, bf16[64,128]{1,0:T(8,128)(2,1)}) custom-call(s32[1,1]{1,0:T(1,128)S(6)} %copy.16.lengths, bf16[128,128]{1,0:T(8,128)(2,1)} %bitcast.22, bf16[8192,128]{1,0:T(8,128)(2,1)} %bitcast.21, bf16[32,128]{1,0:T(8,128)(2,1)} %bitcast.25, bf16[128,128]{1,0:T(8,128)(2,1)} %bitcast.23, f32[64,128]{1,0:T(8,128)} %bitcast.24), custom_call_target="tpu_custom_call" | custom-call | tf_op jit(solution)/shard_map/pallas_call | solution.py:316
  4.6 2.6 %collective-permute-start = (bf16[64,128]{1,0:T(8,128)(2,1)}, bf16[64,128]{1,0:T(8,128)(2,1)S(1)}, u32[]{:S(2)}, u32[]{:S(2)}) collective-permute-start(bf16[64,128]{1,0:T(8,128)(2,1)} %get-tuple-element.14), channel_id=1, source_target_pairs={{0,1},{1,0},{2,3},{3,2},{4,5},{5,4},{6,7},{7,6},{8,9},{9,8},{10,11... | collective-permute-start | bytes 49160 | tf_op jit(solution)/shard_map/ppermute | solution.py:314
  7.2 0.0 copy-done.4
  7.2 0.7 %copy-done.2 = bf16[64,128]{1,0:T(8,128)(2,1)S(1)} copy-done((bf16[64,128]{1,0:T(8,128)(2,1)S(1)}, bf16[64,128]{1,0:T(8,128)(2,1)}, u32[]{:S(2)}) %copy-start.2) | copy-done | bytes 16408
  7.9 0.6 %shard_map.114 = (f32[64,128]{1,0:T(8,128)S(1)}, f32[8,128]{1,0:T(8,128)S(1)}) custom-call(f32[16]{0:T(128)S(1)} %copy-done.4, bf16[64,128]{1,0:T(8,128)(2,1)S(1)} %copy-done.2), custom_call_target="tpu_custom_call" | custom-call | tf_op jit(solution)/shard_map/pallas_call | solution.py:340
  8.5 0.6 %collective-permute-done.received = bf16[64,128]{1,0:T(8,128)(2,1)S(1)} collective-permute-done((bf16[64,128]{1,0:T(8,128)(2,1)}, bf16[64,128]{1,0:T(8,128)(2,1)S(1)}, u32[]{:S(2)}, u32[]{:S(2)}) %collective-permute-start) | collective-permute-done | bytes 16416 | tf_op jit(solution)/shard_map/ppermute | solution.py:314
  9.2 13.7 %all_to_all.10.rows = bf16[8,64,128]{2,1,0:T(8,128)(2,1)S(1)} all-to-all(bf16[8,64,128]{2,1,0:T(8,128)(2,1)S(1)} %shard_map.115), channel_id=1, replica_groups={{0,4,8,12,16,20,24,28},{2,6,10,14,18,22,26,30},{1,5,9,13,17,21,25,29},{..., dimensions={0} | all-to-all | bytes 262144 | tf_op jit(solution)/shard_map/all_to_all | solution.py:350
  22.9 0.0 collective-permute-done.1.other_weight
  22.9 0.0 copy-done
  22.9 0.7 %shard_map.116 = (f32[8,512]{1,0:T(8,128)S(1)}, f32[8,512]{1,0:T(8,128)S(1)}) custom-call(bf16[8,64,128]{2,1,0:T(8,128)(2,1)S(1)} %all_to_all.10.rows, bf16[4096,256]{1,0:T(8,128)(2,1)S(1)} %copy-done, bf16[4096,256]{1,0:T(8,128)(2,1)S(1)} %collective-permute-done.1.other_weight), custom_call_target="tpu_custom_call" | custom-call | tf_op jit(solution)/shard_map/pallas_call | solution.py:351
  23.6 1.2 %collective-permute-start.2 = (f32[8,512]{1,0:T(8,128)S(1)}, f32[8,512]{1,0:T(8,128)S(1)}, u32[]{:S(2)}, u32[]{:S(2)}) collective-permute-start(f32[8,512]{1,0:T(8,128)S(1)} %get-tuple-element.16), channel_id=1, source_target_pairs={{0,1},{1,0},{2,3},{3,2},{4,5},{5,4},{6,7},{7,6},{8,9},{9,8},{10,11... | collective-permute-start | bytes 49160 | tf_op jit(solution)/shard_map/ppermute | solution.py:314
  24.8 0.0 copy-done.1
  24.8 0.0 collective-permute-start.3
  24.8 1.2 %collective-permute-done.3.other_blocks = s32[2,8,8]{2,1,0:T(8,128)S(1)} collective-permute-done((s32[2,8,8]{2,1,0:T(8,128)S(1)}, s32[2,8,8]{2,1,0:T(8,128)S(1)}, u32[]{:S(2)}, u32[]{:S(2)}) %collective-permute-start.3) | collective-permute-done | bytes 544 | tf_op jit(solution)/shard_map/ppermute | solution.py:311
  26.0 1.4 %collective-permute-done.2.received = f32[8,512]{1,0:T(8,128)S(1)} collective-permute-done((f32[8,512]{1,0:T(8,128)S(1)}, f32[8,512]{1,0:T(8,128)S(1)}, u32[]{:S(2)}, u32[]{:S(2)}) %collective-permute-start.2) | collective-permute-done | bytes 16416 | tf_op jit(solution)/shard_map/ppermute | solution.py:314
  27.3 0.0 copy-done.3
  27.3 0.3 shard_map.117
  27.6 0.1 collective-permute-start.4
  27.7 9.2 %all_to_all.11.stats = f32[16,3,8]{2,1,0:T(4,128)S(1)} all-to-all(f32[16,3,8]{2,1,0:T(4,128)S(1)} %get-tuple-element.19), channel_id=1, replica_groups=mesh['wide'=16,'pair'=2] {'wide'}, dimensions={0} | all-to-all | bytes 3072 | tf_op jit(solution)/shard_map/all_to_all | solution.py:370
  36.9 0.0 collective-permute-done.4.received
  36.9 0.8 %shard_map.118 = (f32[2,8,256]{2,1,0:T(8,128)}, f32[2,8]{1,0:T(2,128)}) custom-call(f32[8,256]{1,0:T(8,128)S(1)} %get-tuple-element.17.guided, f32[8,256]{1,0:T(8,128)S(1)} %collective-permute-done.4.received, f32[16,3,8]{2,1,0:T(4,128)S(1)} %all_to_all.11.stats, s32[2,8,8]{2,1,0:T(8,128)S(1)} %copy-done.1), custom_call_target="tpu_custom_call" | custom-call | tf_op jit(solution)/shard_map/pallas_call | solution.py:363
  (4 shorter events, 0.0 us)
Async XLA Ops:
  0.6 22.3 %copy-start = (bf16[4096,256]{1,0:T(8,128)(2,1)S(1)}, bf16[4096,256]{1,0:T(8,128)(2,1)}, u32[]{:S(2)}) copy-start(bf16[4096,256]{1,0:T(8,128)(2,1)} %weight.1) | copy-start | bytes 6291460
  0.6 6.6 %copy-start.4 = (f32[16]{0:T(128)S(1)}, f32[16]{0:T(128)}, u32[]{:S(2)}) copy-start(f32[16]{0:T(128)} %scale.1) | copy-start | bytes 196
  0.7 22.3 %collective-permute-start.1 = (bf16[4096,256]{1,0:T(8,128)(2,1)}, bf16[4096,256]{1,0:T(8,128)(2,1)S(1)}, u32[]{:S(2)}, u32[]{:S(2)}) collective-permute-start(bf16[4096,256]{1,0:T(8,128)(2,1)} %weight.1), channel_id=1, source_target_pairs={{0,2},{2,0},{4,6},{6,4},{8,10},{10,8},{12,14},{14,12},{16,18},{18,... | collective-permute-start | bytes 6291464 | tf_op jit(solution)/shard_map/ppermute | solution.py:311
  4.6 4.6 %collective-permute-start = (bf16[64,128]{1,0:T(8,128)(2,1)}, bf16[64,128]{1,0:T(8,128)(2,1)S(1)}, u32[]{:S(2)}, u32[]{:S(2)}) collective-permute-start(bf16[64,128]{1,0:T(8,128)(2,1)} %get-tuple-element.14), channel_id=1, source_target_pairs={{0,1},{1,0},{2,3},{3,2},{4,5},{5,4},{6,7},{7,6},{8,9},{9,8},{10,11... | collective-permute-start | bytes 49160 | tf_op jit(solution)/shard_map/ppermute | solution.py:314
  7.2 0.7 %copy-start.2 = (bf16[64,128]{1,0:T(8,128)(2,1)S(1)}, bf16[64,128]{1,0:T(8,128)(2,1)}, u32[]{:S(2)}) copy-start(bf16[64,128]{1,0:T(8,128)(2,1)} %get-tuple-element.11.mine) | copy-start | bytes 49156
  22.9 1.9 %copy-start.1 = (s32[2,8,8]{2,1,0:T(8,128)S(1)}, s32[2,8,8]{2,1,0:T(8,128)}, u32[]{:S(2)}) copy-start(s32[2,8,8]{2,1,0:T(8,128)} %blocks.3) | copy-start | bytes 1540
  22.9 4.4 %copy-start.3 = (s32[2,8]{1,0:T(2,128)S(1)}, s32[2,8]{1,0:T(2,128)}, u32[]{:S(2)}) copy-start(s32[2,8]{1,0:T(2,128)} %sampled.1) | copy-start | bytes 196
  23.6 3.7 %collective-permute-start.2 = (f32[8,512]{1,0:T(8,128)S(1)}, f32[8,512]{1,0:T(8,128)S(1)}, u32[]{:S(2)}, u32[]{:S(2)}) collective-permute-start(f32[8,512]{1,0:T(8,128)S(1)} %get-tuple-element.16), channel_id=1, source_target_pairs={{0,1},{1,0},{2,3},{3,2},{4,5},{5,4},{6,7},{7,6},{8,9},{9,8},{10,11... | collective-permute-start | bytes 49160 | tf_op jit(solution)/shard_map/ppermute | solution.py:314
  24.8 1.2 %collective-permute-start.3 = (s32[2,8,8]{2,1,0:T(8,128)S(1)}, s32[2,8,8]{2,1,0:T(8,128)S(1)}, u32[]{:S(2)}, u32[]{:S(2)}) collective-permute-start(s32[2,8,8]{2,1,0:T(8,128)S(1)} %copy-done.1), channel_id=1, source_target_pairs={{0,2},{2,0},{4,6},{6,4},{8,10},{10,8},{12,14},{14,12},{16,18},{18,... | collective-permute-start | bytes 1544 | tf_op jit(solution)/shard_map/ppermute | solution.py:311
  27.6 9.3 %collective-permute-start.4 = (f32[8,256]{1,0:T(8,128)S(1)}, f32[8,256]{1,0:T(8,128)S(1)}, u32[]{:S(2)}, u32[]{:S(2)}) collective-permute-start(f32[8,256]{1,0:T(8,128)S(1)} %get-tuple-element.18), channel_id=1, source_target_pairs={{0,2},{2,0},{4,6},{6,4},{8,10},{10,8},{12,14},{14,12},{16,18},{18,... | collective-permute-start | bytes 24584 | tf_op jit(solution)/shard_map/ppermute | solution.py:311

commit v8 on v7

--- a/solution.py
+++ b/solution.py
@@ -42,7 +42,7 @@
 
 def attend_kernel(
     lengths, queries_in, cache, fresh_in, residual_in, gain_in, mine, theirs,
-    stage, wide_rows, gain_rows, queries, fresh, residual, gain, arrived,
+    stage, wide_rows, mixed, gain_rows, queries, fresh, residual, gain, arrived,
 ):
     rows = cache.shape[0]
     slots = rows // SLOT_ROWS
@@ -81,45 +81,51 @@
     ]
     for copy in small:
         copy.start()
-    lax.fori_loop(live_blocks, blocks, clear, 0)
+    sizes = [slots // 4, slots // 2, slots]
+    fits = [lengths[0, 0] <= size - DECODE_STEPS for size in sizes[:-1]]
+    used_blocks = jnp.where(fits[0], sizes[0] // BLOCK, jnp.where(fits[1], sizes[1] // BLOCK, blocks))
+    lax.fori_loop(live_blocks, used_blocks, clear, 0)
     lax.fori_loop(0, live_blocks, widen, 0)
     for copy in small:
         copy.wait()
     gain_rows[pl.ds(0, QUERY_HEADS, stride=2), :] = gain[...]
     gain_rows[pl.ds(1, QUERY_HEADS, stride=2), :] = gain[...]
-    for step in range(DECODE_STEPS):
-        wide_rows[pl.ds((slots - DECODE_STEPS + step) * SLOT_PITCH, SLOT_ROWS), :] = fresh[
-            pl.ds(step * SLOT_ROWS, SLOT_ROWS), :
-        ].astype(jnp.float32)
     factor = 1.0 / math.sqrt(HEAD_SIZE)
-    scores = []
-    for head in range(KEY_VALUE_HEADS):
-        keys = wide_rows[pl.ds(2 * head, slots, stride=SLOT_PITCH), :].astype(jnp.bfloat16)
-        scores.append(
-            lax.dot_general(
-                queries[pl.ds(head * HEAD_ROWS, HEAD_ROWS), :],
-                keys,
-                (((1,), (1,)), ((), ())),
-                preferred_element_type=jnp.float32,
+
+    def attend(count):
+        first_fresh = count - DECODE_STEPS
+        for step in range(DECODE_STEPS):
+            wide_rows[pl.ds((first_fresh + step) * SLOT_PITCH, SLOT_ROWS), :] = fresh[
+                pl.ds(step * SLOT_ROWS, SLOT_ROWS), :
+            ].astype(jnp.float32)
+        scores = []
+        for head in range(KEY_VALUE_HEADS):
+            keys = wide_rows[pl.ds(2 * head, count, stride=SLOT_PITCH), :].astype(jnp.bfloat16)
+            scores.append(
+                lax.dot_general(
+                    queries[pl.ds(head * HEAD_ROWS, HEAD_ROWS), :],
+                    keys,
+                    (((1,), (1,)), ((), ())),
+                    preferred_element_type=jnp.float32,
+                )
             )
-        )
-    score = jnp.concatenate(scores, axis=0)
-    slot = lax.broadcasted_iota(jnp.int32, score.shape, 1)
-    step_of_row = lax.rem(lax.broadcasted_iota(jnp.int32, score.shape, 0), DECODE_STEPS)
-    first_fresh = slots - DECODE_STEPS
-    live = (slot < lengths[0, 0]) | ((slot >= first_fresh) & (slot - first_fresh <= step_of_row))
-    score = jnp.where(live, score * factor, NEG_FILL)
-    weight = jnp.exp(score - jnp.max(score, axis=1, keepdims=True))
-    weight = (weight / jnp.sum(weight, axis=1, keepdims=True)).astype(jnp.bfloat16)
-    mixed = []
-    for head in range(KEY_VALUE_HEADS):
-        values = wide_rows[pl.ds(2 * head + 1, slots, stride=SLOT_PITCH), :].astype(jnp.bfloat16)
-        mixed.append(
-            jnp.dot(
+        score = jnp.concatenate(scores, axis=0)
+        slot = lax.broadcasted_iota(jnp.int32, score.shape, 1)
+        step_of_row = lax.rem(lax.broadcasted_iota(jnp.int32, score.shape, 0), DECODE_STEPS)
+        live = (slot < lengths[0, 0]) | ((slot >= first_fresh) & (slot - first_fresh <= step_of_row))
+        score = jnp.where(live, score * factor, NEG_FILL)
+        weight = jnp.exp(score - jnp.max(score, axis=1, keepdims=True))
+        weight = (weight / jnp.sum(weight, axis=1, keepdims=True)).astype(jnp.bfloat16)
+        for head in range(KEY_VALUE_HEADS):
+            values = wide_rows[pl.ds(2 * head + 1, count, stride=SLOT_PITCH), :].astype(jnp.bfloat16)
+            mixed[pl.ds(head * HEAD_ROWS, HEAD_ROWS), :] = jnp.dot(
                 weight[head * HEAD_ROWS : (head + 1) * HEAD_ROWS], values, preferred_element_type=jnp.float32
             )
-        )
-    hidden = jnp.concatenate(mixed, axis=0) + residual[...].astype(jnp.float32)
+
+    pl.when(fits[0])(lambda: attend(sizes[0]))
+    pl.when(jnp.logical_not(fits[0]) & fits[1])(lambda: attend(sizes[1]))
+    pl.when(jnp.logical_not(fits[1]))(lambda: attend(sizes[2]))
+    hidden = mixed[...] + residual[...].astype(jnp.float32)
     row_power = jnp.sum(hidden * hidden, axis=1, keepdims=True)
     step_of_row = lax.rem(lax.broadcasted_iota(jnp.int32, row_power.shape, 0), DECODE_STEPS)
     scale = jnp.zeros_like(row_power)
@@ -321,6 +327,7 @@
             pltpu.VMEM(cache_rows.shape, jnp.bfloat16),
             pltpu.VMEM((cache.shape[2] * SLOT_PITCH, HEAD_SIZE), jnp.float32),
             pltpu.VMEM((rows, HEAD_SIZE), jnp.float32),
+            pltpu.VMEM((rows, HEAD_SIZE), jnp.float32),
             pltpu.VMEM((rows, HEAD_SIZE), jnp.bfloat16),
             pltpu.VMEM((steps * SLOT_ROWS, HEAD_SIZE), jnp.bfloat16),
             pltpu.VMEM((rows, HEAD_SIZE), jnp.bfloat16),

time: 37.9 us -> 37.7 us (level)
  starting transfers between devices: 4.43 us -> 5.36 us
  blocking collectives: 22.9 us -> 22.2 us
    ppermute x2, starting transfers between devices: 3.84 us -> 4.77 us  [swap(): return lax.ppermute(array, 'pair', [(0, 1), (1, 0)])]
    all_to_all x1, blocking collectives: 13.7 us -> 13 us  [shards(): lax.all_to_all(spread, 'wide', 0, 0, axis_index_groups=same_core, tiled=T...]
  transfers between devices with their start and end apart: 5 -> 5, of which waited for: 3 -> 3; matrix products, arithmetic and copies ran while one was open for 0% -> 0% of each run, Pallas kernels for 9% -> 8%
where the time goes in v8:
time: 37.7 us; the launch traced here: 37.4 us
  blocking collectives  22.2 us (59%)
  starting transfers between devices  5.36 us (14%)
  Pallas kernels  4.86 us (13%)
  waiting for transfers between devices  2.89 us (8%)
  between operations  1.39 us (4%)
  local copies, waits for them, and re-layouts  0.73 us (2%)
    all_to_all x1, blocking collectives, shards(): lax.all_to_all(spread, 'wide', 0, 0, axis_index_groups=same_core, tiled=T...  13 us
    all_to_all x1, blocking collectives, shards(): lax.all_to_all(stats, 'wide', 0, 0, tiled=True)  9.2 us
    ppermute x2, starting transfers between devices, swap(): return lax.ppermute(array, 'pair', [(0, 1), (1, 0)])  4.77 us
    pallas_call x1, Pallas kernels, shards(): call(attend_kernel, (half_rows, half_rows), [smem] + [hbm] * 5, [pltpu.VM...  2.51 us
    ppermute x2, waiting for transfers between devices, swap(): return lax.ppermute(array, 'pair', [(0, 1), (1, 0)])  1.71 us
    ppermute x3, waiting for transfers between devices, other_core(): lax.ppermute(array, 'wide', [(source, source ^ 1) for source in range(wid...  1.17 us
    pallas_call x1, Pallas kernels, shards(): call(finish_kernel, (jax.ShapeDtypeStruct((steps, half_pairs, width), jnp...  0.82 us
  transfers between devices with their start and end apart: 5, of which 3 were waited for; matrix products, arithmetic and copies ran while one was open for 0% of the time, Pallas kernels for 8%

profile of v8, /device:TPU:0, one launch (start us, length us, event | category | flops | bytes accessed | tf_op | source)
XLA Modules:
  0.0 37.4 jit_solution(5783803862244987689)
XLA Ops:
  0.6 0.0 copy-start
  0.6 0.0 copy-start.4
  0.7 0.5 %collective-permute-start.1 = (bf16[4096,256]{1,0:T(8,128)(2,1)}, bf16[4096,256]{1,0:T(8,128)(2,1)S(1)}, u32[]{:S(2)}, u32[]{:S(2)}) collective-permute-start(bf16[4096,256]{1,0:T(8,128)(2,1)} %weight.1), channel_id=1, source_target_pairs={{0,2},{2,0},{4,6},{6,4},{8,10},{10,8},{12,14},{14,12},{16,18},{18,... | collective-permute-start | bytes 6291464 | tf_op jit(solution)/shard_map/ppermute | solution.py:317
  1.9 2.5 %shard_map.113 = (bf16[64,128]{1,0:T(8,128)(2,1)}, bf16[64,128]{1,0:T(8,128)(2,1)}) custom-call(s32[1,1]{1,0:T(1,128)S(6)} %copy.16.lengths, bf16[128,128]{1,0:T(8,128)(2,1)} %bitcast.22, bf16[8192,128]{1,0:T(8,128)(2,1)} %bitcast.21, bf16[32,128]{1,0:T(8,128)(2,1)} %bitcast.25, bf16[128,128]{1,0:T(8,128)(2,1)} %bitcast.23, f32[64,128]{1,0:T(8,128)} %bitcast.24), custom_call_target="tpu_custom_call" | custom-call | tf_op jit(solution)/shard_map/pallas_call | solution.py:322
  4.4 3.3 %collective-permute-start = (bf16[64,128]{1,0:T(8,128)(2,1)}, bf16[64,128]{1,0:T(8,128)(2,1)S(1)}, u32[]{:S(2)}, u32[]{:S(2)}) collective-permute-start(bf16[64,128]{1,0:T(8,128)(2,1)} %get-tuple-element.14), channel_id=1, source_target_pairs={{0,1},{1,0},{2,3},{3,2},{4,5},{5,4},{6,7},{7,6},{8,9},{9,8},{10,11... | collective-permute-start | bytes 49160 | tf_op jit(solution)/shard_map/ppermute | solution.py:320
  7.7 0.0 copy-done.4
  7.7 0.7 %copy-done.2 = bf16[64,128]{1,0:T(8,128)(2,1)S(1)} copy-done((bf16[64,128]{1,0:T(8,128)(2,1)S(1)}, bf16[64,128]{1,0:T(8,128)(2,1)}, u32[]{:S(2)}) %copy-start.2) | copy-done | bytes 16408
  8.4 0.6 %shard_map.114 = (f32[64,128]{1,0:T(8,128)S(1)}, f32[8,128]{1,0:T(8,128)S(1)}) custom-call(f32[16]{0:T(128)S(1)} %copy-done.4, bf16[64,128]{1,0:T(8,128)(2,1)S(1)} %copy-done.2), custom_call_target="tpu_custom_call" | custom-call | tf_op jit(solution)/shard_map/pallas_call | solution.py:347
  8.9 0.6 %collective-permute-done.received = bf16[64,128]{1,0:T(8,128)(2,1)S(1)} collective-permute-done((bf16[64,128]{1,0:T(8,128)(2,1)}, bf16[64,128]{1,0:T(8,128)(2,1)S(1)}, u32[]{:S(2)}, u32[]{:S(2)}) %collective-permute-start) | collective-permute-done | bytes 16416 | tf_op jit(solution)/shard_map/ppermute | solution.py:320
  9.6 13.0 %all_to_all.10.rows = bf16[8,64,128]{2,1,0:T(8,128)(2,1)S(1)} all-to-all(bf16[8,64,128]{2,1,0:T(8,128)(2,1)S(1)} %shard_map.115), channel_id=1, replica_groups={{0,4,8,12,16,20,24,28},{2,6,10,14,18,22,26,30},{1,5,9,13,17,21,25,29},{..., dimensions={0} | all-to-all | bytes 262144 | tf_op jit(solution)/shard_map/all_to_all | solution.py:357
  22.6 0.0 collective-permute-done.1.other_weight
  22.6 0.0 copy-done
  22.6 0.7 %shard_map.116 = (f32[8,512]{1,0:T(8,128)S(1)}, f32[8,512]{1,0:T(8,128)S(1)}) custom-call(bf16[8,64,128]{2,1,0:T(8,128)(2,1)S(1)} %all_to_all.10.rows, bf16[4096,256]{1,0:T(8,128)(2,1)S(1)} %copy-done, bf16[4096,256]{1,0:T(8,128)(2,1)S(1)} %collective-permute-done.1.other_weight), custom_call_target="tpu_custom_call" | custom-call | tf_op jit(solution)/shard_map/pallas_call | solution.py:358
  23.2 1.5 %collective-permute-start.2 = (f32[8,512]{1,0:T(8,128)S(1)}, f32[8,512]{1,0:T(8,128)S(1)}, u32[]{:S(2)}, u32[]{:S(2)}) collective-permute-start(f32[8,512]{1,0:T(8,128)S(1)} %get-tuple-element.16), channel_id=1, source_target_pairs={{0,1},{1,0},{2,3},{3,2},{4,5},{5,4},{6,7},{7,6},{8,9},{9,8},{10,11... | collective-permute-start | bytes 49160 | tf_op jit(solution)/shard_map/ppermute | solution.py:320
  24.7 0.0 copy-done.1
  24.7 0.0 collective-permute-start.3
  24.7 1.2 %collective-permute-done.3.other_blocks = s32[2,8,8]{2,1,0:T(8,128)S(1)} collective-permute-done((s32[2,8,8]{2,1,0:T(8,128)S(1)}, s32[2,8,8]{2,1,0:T(8,128)S(1)}, u32[]{:S(2)}, u32[]{:S(2)}) %collective-permute-start.3) | collective-permute-done | bytes 544 | tf_op jit(solution)/shard_map/ppermute | solution.py:317
  25.9 1.1 %collective-permute-done.2.received = f32[8,512]{1,0:T(8,128)S(1)} collective-permute-done((f32[8,512]{1,0:T(8,128)S(1)}, f32[8,512]{1,0:T(8,128)S(1)}, u32[]{:S(2)}, u32[]{:S(2)}) %collective-permute-start.2) | collective-permute-done | bytes 16416 | tf_op jit(solution)/shard_map/ppermute | solution.py:320
  27.0 0.0 copy-done.3
  27.0 0.3 shard_map.117
  27.3 0.1 collective-permute-start.4
  27.4 9.2 %all_to_all.11.stats = f32[16,3,8]{2,1,0:T(4,128)S(1)} all-to-all(f32[16,3,8]{2,1,0:T(4,128)S(1)} %get-tuple-element.19), channel_id=1, replica_groups=mesh['wide'=16,'pair'=2] {'wide'}, dimensions={0} | all-to-all | bytes 3072 | tf_op jit(solution)/shard_map/all_to_all | solution.py:377
  36.6 0.0 collective-permute-done.4.received
  36.6 0.8 %shard_map.118 = (f32[2,8,256]{2,1,0:T(8,128)}, f32[2,8]{1,0:T(2,128)}) custom-call(f32[8,256]{1,0:T(8,128)S(1)} %get-tuple-element.17.guided, f32[8,256]{1,0:T(8,128)S(1)} %collective-permute-done.4.received, f32[16,3,8]{2,1,0:T(4,128)S(1)} %all_to_all.11.stats, s32[2,8,8]{2,1,0:T(8,128)S(1)} %copy-done.1), custom_call_target="tpu_custom_call" | custom-call | tf_op jit(solution)/shard_map/pallas_call | solution.py:370
  (4 shorter events, 0.0 us)
Async XLA Ops:
  0.6 21.9 %copy-start = (bf16[4096,256]{1,0:T(8,128)(2,1)S(1)}, bf16[4096,256]{1,0:T(8,128)(2,1)}, u32[]{:S(2)}) copy-start(bf16[4096,256]{1,0:T(8,128)(2,1)} %weight.1) | copy-start | bytes 6291460
  0.6 7.0 %copy-start.4 = (f32[16]{0:T(128)S(1)}, f32[16]{0:T(128)}, u32[]{:S(2)}) copy-start(f32[16]{0:T(128)} %scale.1) | copy-start | bytes 196
  0.7 21.9 %collective-permute-start.1 = (bf16[4096,256]{1,0:T(8,128)(2,1)}, bf16[4096,256]{1,0:T(8,128)(2,1)S(1)}, u32[]{:S(2)}, u32[]{:S(2)}) collective-permute-start(bf16[4096,256]{1,0:T(8,128)(2,1)} %weight.1), channel_id=1, source_target_pairs={{0,2},{2,0},{4,6},{6,4},{8,10},{10,8},{12,14},{14,12},{16,18},{18,... | collective-permute-start | bytes 6291464 | tf_op jit(solution)/shard_map/ppermute | solution.py:317
  4.4 5.2 %collective-permute-start = (bf16[64,128]{1,0:T(8,128)(2,1)}, bf16[64,128]{1,0:T(8,128)(2,1)S(1)}, u32[]{:S(2)}, u32[]{:S(2)}) collective-permute-start(bf16[64,128]{1,0:T(8,128)(2,1)} %get-tuple-element.14), channel_id=1, source_target_pairs={{0,1},{1,0},{2,3},{3,2},{4,5},{5,4},{6,7},{7,6},{8,9},{9,8},{10,11... | collective-permute-start | bytes 49160 | tf_op jit(solution)/shard_map/ppermute | solution.py:320
  7.7 0.7 %copy-start.2 = (bf16[64,128]{1,0:T(8,128)(2,1)S(1)}, bf16[64,128]{1,0:T(8,128)(2,1)}, u32[]{:S(2)}) copy-start(bf16[64,128]{1,0:T(8,128)(2,1)} %get-tuple-element.11.mine) | copy-start | bytes 49156
  22.6 2.2 %copy-start.1 = (s32[2,8,8]{2,1,0:T(8,128)S(1)}, s32[2,8,8]{2,1,0:T(8,128)}, u32[]{:S(2)}) copy-start(s32[2,8,8]{2,1,0:T(8,128)} %blocks.3) | copy-start | bytes 1540
  22.6 4.4 %copy-start.3 = (s32[2,8]{1,0:T(2,128)S(1)}, s32[2,8]{1,0:T(2,128)}, u32[]{:S(2)}) copy-start(s32[2,8]{1,0:T(2,128)} %sampled.1) | copy-start | bytes 196
  23.2 3.7 %collective-permute-start.2 = (f32[8,512]{1,0:T(8,128)S(1)}, f32[8,512]{1,0:T(8,128)S(1)}, u32[]{:S(2)}, u32[]{:S(2)}) collective-permute-start(f32[8,512]{1,0:T(8,128)S(1)} %get-tuple-element.16), channel_id=1, source_target_pairs={{0,1},{1,0},{2,3},{3,2},{4,5},{5,4},{6,7},{7,6},{8,9},{9,8},{10,11... | collective-permute-start | bytes 49160 | tf_op jit(solution)/shard_map/ppermute | solution.py:320
  24.7 1.2 %collective-permute-start.3 = (s32[2,8,8]{2,1,0:T(8,128)S(1)}, s32[2,8,8]{2,1,0:T(8,128)S(1)}, u32[]{:S(2)}, u32[]{:S(2)}) collective-permute-start(s32[2,8,8]{2,1,0:T(8,128)S(1)} %copy-done.1), channel_id=1, source_target_pairs={{0,2},{2,0},{4,6},{6,4},{8,10},{10,8},{12,14},{14,12},{16,18},{18,... | collective-permute-start | bytes 1544 | tf_op jit(solution)/shard_map/ppermute | solution.py:317
  27.3 9.3 %collective-permute-start.4 = (f32[8,256]{1,0:T(8,128)S(1)}, f32[8,256]{1,0:T(8,128)S(1)}, u32[]{:S(2)}, u32[]{:S(2)}) collective-permute-start(f32[8,256]{1,0:T(8,128)S(1)} %get-tuple-element.18), channel_id=1, source_target_pairs={{0,2},{2,0},{4,6},{6,4},{8,10},{10,8},{12,14},{14,12},{16,18},{18,... | collective-permute-start | bytes 24584 | tf_op jit(solution)/shard_map/ppermute | solution.py:317

commit v9 on v7

--- a/solution.py
+++ b/solution.py
@@ -33,7 +33,7 @@
         kernel,
         out_shape=out_shape,
         in_specs=in_specs,
-        out_specs=jax.tree.map(lambda _: in_vmem(), out_shape),
+        out_specs=jax.tree.map(lambda _: in_vmem(), out_shape, is_leaf=lambda x: hasattr(x, 'shape')),
         scratch_shapes=list(scratch),
         compiler_params=pltpu.CompilerParams(vmem_limit_bytes=limit),
         cost_estimate=cost,
@@ -315,7 +315,7 @@
 
     mine, theirs = call(
         attend_kernel,
-        (half_rows, half_rows),
+        (pltpu.VMEM(half_rows.shape, half_rows.dtype), pltpu.VMEM(half_rows.shape, half_rows.dtype)),
         [smem] + [hbm] * 5,
         [
             pltpu.VMEM(cache_rows.shape, jnp.bfloat16),

time: 37.9 us -> 36.8 us (0.971)
  local copies, waits for them, and re-layouts: 0.73 us -> 0.02 us
    unnamed x10 -> x8, local copies, waits for them, and re-layouts: 0.73 us -> 0.02 us
  transfers between devices with their start and end apart: 5 -> 5, of which waited for: 3 -> 3; matrix products, arithmetic and copies ran while one was open for 0% -> 0% of each run, Pallas kernels for 9% -> 8%
where the time goes in v9:
time: 36.8 us; the launch traced here: 36.6 us
  blocking collectives  22.7 us (62%)
  Pallas kernels  4.68 us (13%)
  starting transfers between devices  4.43 us (12%)
  waiting for transfers between devices  3.38 us (9%)
  between operations  1.38 us (4%)
    all_to_all x1, blocking collectives, shards(): lax.all_to_all(spread, 'wide', 0, 0, axis_index_groups=same_core, tiled=T...  13.5 us
    all_to_all x1, blocking collectives, shards(): lax.all_to_all(stats, 'wide', 0, 0, tiled=True)  9.2 us
    ppermute x2, starting transfers between devices, swap(): return lax.ppermute(array, 'pair', [(0, 1), (1, 0)])  3.84 us
    pallas_call x1, Pallas kernels, shards(): call(attend_kernel, (pltpu.VMEM(half_rows.shape, half_rows.dtype), pltpu....  2.33 us
    ppermute x2, waiting for transfers between devices, swap(): return lax.ppermute(array, 'pair', [(0, 1), (1, 0)])  2.21 us
    ppermute x3, waiting for transfers between devices, other_core(): lax.ppermute(array, 'wide', [(source, source ^ 1) for source in range(wid...  1.17 us
    pallas_call x1, Pallas kernels, shards(): call(finish_kernel, (jax.ShapeDtypeStruct((steps, half_pairs, width), jnp...  0.82 us
  transfers between devices with their start and end apart: 5, of which 3 were waited for; matrix products, arithmetic and copies ran while one was open for 0% of the time, Pallas kernels for 8%

profile of v9, /device:TPU:0, one launch (start us, length us, event | category | flops | bytes accessed | tf_op | source)
XLA Modules:
  0.0 36.6 jit_solution(15826214091166797523)
XLA Ops:
  0.6 0.0 copy-start
  0.6 0.0 copy-start.3
  0.7 0.5 %collective-permute-start.1 = (bf16[4096,256]{1,0:T(8,128)(2,1)}, bf16[4096,256]{1,0:T(8,128)(2,1)S(1)}, u32[]{:S(2)}, u32[]{:S(2)}) collective-permute-start(bf16[4096,256]{1,0:T(8,128)(2,1)} %weight.1), channel_id=1, source_target_pairs={{0,2},{2,0},{4,6},{6,4},{8,10},{10,8},{12,14},{14,12},{16,18},{18,... | collective-permute-start | bytes 6291464 | tf_op jit(solution)/shard_map/ppermute | solution.py:311
  1.9 2.3 %shard_map.113 = (bf16[64,128]{1,0:T(8,128)(2,1)S(1)}, bf16[64,128]{1,0:T(8,128)(2,1)S(1)}) custom-call(s32[1,1]{1,0:T(1,128)S(6)} %copy.16.lengths, bf16[128,128]{1,0:T(8,128)(2,1)} %bitcast.22, bf16[8192,128]{1,0:T(8,128)(2,1)} %bitcast.21, bf16[32,128]{1,0:T(8,128)(2,1)} %bitcast.25, bf16[128,128]{1,0:T(8,128)(2,1)} %bitcast.23, f32[64,128]{1,0:T(8,128)} %bitcast.24), custom_call_target="tpu_custom_call" | custom-call | tf_op jit(solution)/shard_map/pallas_call | solution.py:316
  4.2 2.3 %collective-permute-start = (bf16[64,128]{1,0:T(8,128)(2,1)S(1)}, bf16[64,128]{1,0:T(8,128)(2,1)S(1)}, u32[]{:S(2)}, u32[]{:S(2)}) collective-permute-start(bf16[64,128]{1,0:T(8,128)(2,1)S(1)} %get-tuple-element.14), channel_id=1, source_target_pairs={{0,1},{1,0},{2,3},{3,2},{4,5},{5,4},{6,7},{7,6},{8,9},{9,8},{10,11... | collective-permute-start | bytes 49160 | tf_op jit(solution)/shard_map/ppermute | solution.py:314
  6.5 0.0 copy-done.3
  6.5 0.6 %shard_map.114 = (f32[64,128]{1,0:T(8,128)S(1)}, f32[8,128]{1,0:T(8,128)S(1)}) custom-call(f32[16]{0:T(128)S(1)} %copy-done.3, bf16[64,128]{1,0:T(8,128)(2,1)S(1)} %get-tuple-element.11.mine), custom_call_target="tpu_custom_call" | custom-call | tf_op jit(solution)/shard_map/pallas_call | solution.py:340
  7.1 1.1 %collective-permute-done.received = bf16[64,128]{1,0:T(8,128)(2,1)S(1)} collective-permute-done((bf16[64,128]{1,0:T(8,128)(2,1)S(1)}, bf16[64,128]{1,0:T(8,128)(2,1)S(1)}, u32[]{:S(2)}, u32[]{:S(2)}) %collective-permute-start) | collective-permute-done | bytes 16416 | tf_op jit(solution)/shard_map/ppermute | solution.py:314
  8.3 13.5 %all_to_all.10.rows = bf16[8,64,128]{2,1,0:T(8,128)(2,1)S(1)} all-to-all(bf16[8,64,128]{2,1,0:T(8,128)(2,1)S(1)} %shard_map.115), channel_id=1, replica_groups={{0,4,8,12,16,20,24,28},{2,6,10,14,18,22,26,30},{1,5,9,13,17,21,25,29},{..., dimensions={0} | all-to-all | bytes 262144 | tf_op jit(solution)/shard_map/all_to_all | solution.py:350
  21.8 0.0 copy-start.1
  21.8 0.0 collective-permute-done.1.other_weight
  21.8 0.0 copy-done
  21.8 0.7 %shard_map.116 = (f32[8,512]{1,0:T(8,128)S(1)}, f32[8,512]{1,0:T(8,128)S(1)}) custom-call(bf16[8,64,128]{2,1,0:T(8,128)(2,1)S(1)} %all_to_all.10.rows, bf16[4096,256]{1,0:T(8,128)(2,1)S(1)} %copy-done, bf16[4096,256]{1,0:T(8,128)(2,1)S(1)} %collective-permute-done.1.other_weight), custom_call_target="tpu_custom_call" | custom-call | tf_op jit(solution)/shard_map/pallas_call | solution.py:351
  22.5 1.5 %collective-permute-start.2 = (f32[8,512]{1,0:T(8,128)S(1)}, f32[8,512]{1,0:T(8,128)S(1)}, u32[]{:S(2)}, u32[]{:S(2)}) collective-permute-start(f32[8,512]{1,0:T(8,128)S(1)} %get-tuple-element.16), channel_id=1, source_target_pairs={{0,1},{1,0},{2,3},{3,2},{4,5},{5,4},{6,7},{7,6},{8,9},{9,8},{10,11... | collective-permute-start | bytes 49160 | tf_op jit(solution)/shard_map/ppermute | solution.py:314
  24.0 0.0 copy-done.1
  24.0 0.0 collective-permute-start.3
  24.0 1.2 %collective-permute-done.3.other_blocks = s32[2,8,8]{2,1,0:T(8,128)S(1)} collective-permute-done((s32[2,8,8]{2,1,0:T(8,128)S(1)}, s32[2,8,8]{2,1,0:T(8,128)S(1)}, u32[]{:S(2)}, u32[]{:S(2)}) %collective-permute-start.3) | collective-permute-done | bytes 544 | tf_op jit(solution)/shard_map/ppermute | solution.py:311
  25.1 1.1 %collective-permute-done.2.received = f32[8,512]{1,0:T(8,128)S(1)} collective-permute-done((f32[8,512]{1,0:T(8,128)S(1)}, f32[8,512]{1,0:T(8,128)S(1)}, u32[]{:S(2)}, u32[]{:S(2)}) %collective-permute-start.2) | collective-permute-done | bytes 16416 | tf_op jit(solution)/shard_map/ppermute | solution.py:314
  26.2 0.0 copy-done.2
  26.2 0.3 shard_map.117
  26.5 0.1 collective-permute-start.4
  26.6 9.2 %all_to_all.11.stats = f32[16,3,8]{2,1,0:T(4,128)S(1)} all-to-all(f32[16,3,8]{2,1,0:T(4,128)S(1)} %get-tuple-element.19), channel_id=1, replica_groups=mesh['wide'=16,'pair'=2] {'wide'}, dimensions={0} | all-to-all | bytes 3072 | tf_op jit(solution)/shard_map/all_to_all | solution.py:370
  35.8 0.0 collective-permute-done.4.received
  35.8 0.8 %shard_map.118 = (f32[2,8,256]{2,1,0:T(8,128)}, f32[2,8]{1,0:T(2,128)}) custom-call(f32[8,256]{1,0:T(8,128)S(1)} %get-tuple-element.17.guided, f32[8,256]{1,0:T(8,128)S(1)} %collective-permute-done.4.received, f32[16,3,8]{2,1,0:T(4,128)S(1)} %all_to_all.11.stats, s32[2,8,8]{2,1,0:T(8,128)S(1)} %copy-done.1), custom_call_target="tpu_custom_call" | custom-call | tf_op jit(solution)/shard_map/pallas_call | solution.py:363
  (2 shorter events, 0.0 us)
Async XLA Ops:
  0.6 21.2 %copy-start = (bf16[4096,256]{1,0:T(8,128)(2,1)S(1)}, bf16[4096,256]{1,0:T(8,128)(2,1)}, u32[]{:S(2)}) copy-start(bf16[4096,256]{1,0:T(8,128)(2,1)} %weight.1) | copy-start | bytes 6291460
  0.6 5.9 %copy-start.3 = (f32[16]{0:T(128)S(1)}, f32[16]{0:T(128)}, u32[]{:S(2)}) copy-start(f32[16]{0:T(128)} %scale.1) | copy-start | bytes 196
  0.7 21.1 %collective-permute-start.1 = (bf16[4096,256]{1,0:T(8,128)(2,1)}, bf16[4096,256]{1,0:T(8,128)(2,1)S(1)}, u32[]{:S(2)}, u32[]{:S(2)}) collective-permute-start(bf16[4096,256]{1,0:T(8,128)(2,1)} %weight.1), channel_id=1, source_target_pairs={{0,2},{2,0},{4,6},{6,4},{8,10},{10,8},{12,14},{14,12},{16,18},{18,... | collective-permute-start | bytes 6291464 | tf_op jit(solution)/shard_map/ppermute | solution.py:311
  4.2 4.0 %collective-permute-start = (bf16[64,128]{1,0:T(8,128)(2,1)S(1)}, bf16[64,128]{1,0:T(8,128)(2,1)S(1)}, u32[]{:S(2)}, u32[]{:S(2)}) collective-permute-start(bf16[64,128]{1,0:T(8,128)(2,1)S(1)} %get-tuple-element.14), channel_id=1, source_target_pairs={{0,1},{1,0},{2,3},{3,2},{4,5},{5,4},{6,7},{7,6},{8,9},{9,8},{10,11... | collective-permute-start | bytes 49160 | tf_op jit(solution)/shard_map/ppermute | solution.py:314
  21.8 2.2 %copy-start.1 = (s32[2,8,8]{2,1,0:T(8,128)S(1)}, s32[2,8,8]{2,1,0:T(8,128)}, u32[]{:S(2)}) copy-start(s32[2,8,8]{2,1,0:T(8,128)} %blocks.3) | copy-start | bytes 1540
  21.8 4.4 %copy-start.2 = (s32[2,8]{1,0:T(2,128)S(1)}, s32[2,8]{1,0:T(2,128)}, u32[]{:S(2)}) copy-start(s32[2,8]{1,0:T(2,128)} %sampled.1) | copy-start | bytes 196
  22.5 3.7 %collective-permute-start.2 = (f32[8,512]{1,0:T(8,128)S(1)}, f32[8,512]{1,0:T(8,128)S(1)}, u32[]{:S(2)}, u32[]{:S(2)}) collective-permute-start(f32[8,512]{1,0:T(8,128)S(1)} %get-tuple-element.16), channel_id=1, source_target_pairs={{0,1},{1,0},{2,3},{3,2},{4,5},{5,4},{6,7},{7,6},{8,9},{9,8},{10,11... | collective-permute-start | bytes 49160 | tf_op jit(solution)/shard_map/ppermute | solution.py:314
  24.0 1.2 %collective-permute-start.3 = (s32[2,8,8]{2,1,0:T(8,128)S(1)}, s32[2,8,8]{2,1,0:T(8,128)S(1)}, u32[]{:S(2)}, u32[]{:S(2)}) collective-permute-start(s32[2,8,8]{2,1,0:T(8,128)S(1)} %copy-done.1), channel_id=1, source_target_pairs={{0,2},{2,0},{4,6},{6,4},{8,10},{10,8},{12,14},{14,12},{16,18},{18,... | collective-permute-start | bytes 1544 | tf_op jit(solution)/shard_map/ppermute | solution.py:311
  26.5 9.3 %collective-permute-start.4 = (f32[8,256]{1,0:T(8,128)S(1)}, f32[8,256]{1,0:T(8,128)S(1)}, u32[]{:S(2)}, u32[]{:S(2)}) collective-permute-start(f32[8,256]{1,0:T(8,128)S(1)} %get-tuple-element.18), channel_id=1, source_target_pairs={{0,2},{2,0},{4,6},{6,4},{8,10},{10,8},{12,14},{14,12},{16,18},{18,... | collective-permute-start | bytes 24584 | tf_op jit(solution)/shard_map/ppermute | solution.py:311

commit v10 on v8

--- a/solution.py
+++ b/solution.py
@@ -33,7 +33,7 @@
         kernel,
         out_shape=out_shape,
         in_specs=in_specs,
-        out_specs=jax.tree.map(lambda _: in_vmem(), out_shape),
+        out_specs=jax.tree.map(lambda _: in_vmem(), out_shape, is_leaf=lambda x: hasattr(x, 'shape')),
         scratch_shapes=list(scratch),
         compiler_params=pltpu.CompilerParams(vmem_limit_bytes=limit),
         cost_estimate=cost,
@@ -244,9 +244,11 @@
     lane = lax.broadcasted_iota(jnp.int32, guided.shape, 1)
     column = jnp.where(lane < width, position * width + lane, (position ^ 1) * width + lane - width)
     picked = jnp.sum(jnp.where(column == chosen, guided, 0.0), axis=1, keepdims=True)
-    stats[...] = jnp.broadcast_to(
-        jnp.concatenate([to_lanes(top), to_lanes(total), to_lanes(picked)], axis=0)[None], stats.shape
-    )
+    lanes = jnp.concatenate([to_lanes(top), to_lanes(total), to_lanes(picked)], axis=1)
+    pad = stats.shape[2] - lanes.shape[1]
+    if pad > 0:
+        lanes = jnp.concatenate([lanes, jnp.zeros((1, pad), jnp.float32)], axis=1)
+    stats[...] = jnp.broadcast_to(lanes[None], stats.shape)
 
 
 def finish_kernel(guided, received, stats, blocks, logprobs, tokens):
@@ -257,11 +259,12 @@
     token_rows = [jnp.zeros((1, 2 * count), jnp.float32)] * DECODE_STEPS
     results = []
     for parity in range(2):
-        parts = [stats[2 * chip + parity] for chip in range(chips)]
-        top = functools.reduce(jnp.maximum, [part[0:1] for part in parts])
-        total = sum(part[1:2] * jnp.exp(part[0:1] - top) for part in parts)
+        parts = jnp.concatenate([stats[2 * chip + parity] for chip in range(chips)], axis=0)
+        tops = parts[:, 0:rows]
+        top = jnp.max(tops, axis=0, keepdims=True)
+        total = jnp.sum(parts[:, rows : 2 * rows] * jnp.exp(tops - top), axis=0, keepdims=True)
         normalizer = top + jnp.log(total)
-        token = sum(part[2:3] for part in parts) - normalizer
+        token = jnp.sum(parts[:, 2 * rows : 3 * rows], axis=0, keepdims=True) - normalizer
         values = jnp.where(near == parity, guided[...], received[...])
         results.append(jnp.where(allowed_entries(blocks, parity, width), values - to_column(normalizer), 0.0))
         spot = (count, 2 * count)
@@ -321,7 +324,7 @@
 
     mine, theirs = call(
         attend_kernel,
-        (half_rows, half_rows),
+        (pltpu.VMEM(half_rows.shape, half_rows.dtype), pltpu.VMEM(half_rows.shape, half_rows.dtype)),
         [smem] + [hbm] * 5,
         [
             pltpu.VMEM(cache_rows.shape, jnp.bfloat16),
@@ -361,9 +364,10 @@
         [vmem] * 3,
         [pltpu.VMEM((chips * (rows // 2 + 1), HEAD_SIZE), jnp.float32)],
     )(gathered, vocab_weight, other_weight)
+    lanes = pl.cdiv(3 * steps * chips // 2, 128) * 128
     guided, other_guided, stats = call(
         stats_kernel,
-        (flat, flat, jax.ShapeDtypeStruct((wide, 3, steps * chips // 2), jnp.float32)),
+        (flat, flat, jax.ShapeDtypeStruct((wide, 1, lanes), jnp.float32)),
         [vmem] * 5,
     )(mine, swap(theirs), allowed_blocks, other_blocks, sampled)
     other_guided = other_core(other_guided)

time: 37.7 us -> 38.7 us (1.027)
  blocking collectives: 22.2 us -> 14.2 us
  waiting for transfers between devices: 2.89 us -> 10 us
  starting transfers between devices: 5.36 us -> 7.34 us
  local copies, waits for them, and re-layouts: 0.73 us -> 0.02 us
  Pallas kernels: 4.86 us -> 5.5 us
    all_to_all x1 -> x0, blocking collectives: 9.2 us -> none  [shards(): lax.all_to_all(stats, 'wide', 0, 0, tiled=True)]
    all_to_all x0 -> x1, waiting for transfers between devices: none -> 5.06 us  [shards(): lax.all_to_all(stats, 'wide', 0, 0, tiled=True)]
    all_to_all x0 -> x1, starting transfers between devices: none -> 3.47 us  [shards(): lax.all_to_all(stats, 'wide', 0, 0, tiled=True)]
    ppermute x2, starting transfers between devices: 4.77 us -> 3.06 us  [swap(): return lax.ppermute(array, 'pair', [(0, 1), (1, 0)])]
    all_to_all x1, blocking collectives: 13 us -> 14.2 us  [shards(): lax.all_to_all(spread, 'wide', 0, 0, axis_index_groups=same_core, tiled=T...]
    ppermute x2, waiting for transfers between devices: 1.71 us -> 2.84 us  [swap(): return lax.ppermute(array, 'pair', [(0, 1), (1, 0)])]
    ppermute x3, waiting for transfers between devices: 1.17 us -> 2.12 us  [other_core(): lax.ppermute(array, 'wide', [(source, source ^ 1) for source in range(wid...]
    unnamed x10 -> x8, local copies, waits for them, and re-layouts: 0.73 us -> 0.02 us
  transfers between devices with their start and end apart: 5 -> 6, of which waited for: 3 -> 5; matrix products, arithmetic and copies ran while one was open for 0% -> 0% of each run, Pallas kernels for 8% -> 7%
where the time goes in v10:
time: 38.7 us; the launch traced here: 38.5 us
  blocking collectives  14.2 us (37%)
  waiting for transfers between devices  10 us (26%)
  starting transfers between devices  7.34 us (19%)
  Pallas kernels  5.5 us (14%)
  between operations  1.38 us (4%)
    all_to_all x1, blocking collectives, shards(): lax.all_to_all(spread, 'wide', 0, 0, axis_index_groups=same_core, tiled=T...  14.2 us
    all_to_all x1, waiting for transfers between devices, shards(): lax.all_to_all(stats, 'wide', 0, 0, tiled=True)  5.06 us
    all_to_all x1, starting transfers between devices, shards(): lax.all_to_all(stats, 'wide', 0, 0, tiled=True)  3.47 us
    ppermute x2, starting transfers between devices, swap(): return lax.ppermute(array, 'pair', [(0, 1), (1, 0)])  3.06 us
    ppermute x2, waiting for transfers between devices, swap(): return lax.ppermute(array, 'pair', [(0, 1), (1, 0)])  2.84 us
    pallas_call x1, Pallas kernels, shards(): call(attend_kernel, (pltpu.VMEM(half_rows.shape, half_rows.dtype), pltpu....  2.28 us
    ppermute x3, waiting for transfers between devices, other_core(): lax.ppermute(array, 'wide', [(source, source ^ 1) for source in range(wid...  2.12 us
    pallas_call x1, Pallas kernels, shards(): call(finish_kernel, (jax.ShapeDtypeStruct((steps, half_pairs, width), jnp...  1.01 us
  transfers between devices with their start and end apart: 6, of which 5 were waited for; matrix products, arithmetic and copies ran while one was open for 0% of the time, Pallas kernels for 7%

profile of v10, /device:TPU:0, one launch (start us, length us, event | category | flops | bytes accessed | tf_op | source)
XLA Modules:
  0.0 38.5 jit_solution(476066413863705932)
XLA Ops:
  0.6 0.0 copy-start
  0.6 0.0 copy-start.3
  0.7 0.5 %collective-permute-start.1 = (bf16[4096,256]{1,0:T(8,128)(2,1)}, bf16[4096,256]{1,0:T(8,128)(2,1)S(1)}, u32[]{:S(2)}, u32[]{:S(2)}) collective-permute-start(bf16[4096,256]{1,0:T(8,128)(2,1)} %weight.1), channel_id=1, source_target_pairs={{0,2},{2,0},{4,6},{6,4},{8,10},{10,8},{12,14},{14,12},{16,18},{18,... | collective-permute-start | bytes 6291464 | tf_op jit(solution)/shard_map/ppermute | solution.py:320
  1.9 2.3 %shard_map.113 = (bf16[64,128]{1,0:T(8,128)(2,1)S(1)}, bf16[64,128]{1,0:T(8,128)(2,1)S(1)}) custom-call(s32[1,1]{1,0:T(1,128)S(6)} %copy.16.lengths, bf16[128,128]{1,0:T(8,128)(2,1)} %bitcast.22, bf16[8192,128]{1,0:T(8,128)(2,1)} %bitcast.21, bf16[32,128]{1,0:T(8,128)(2,1)} %bitcast.25, bf16[128,128]{1,0:T(8,128)(2,1)} %bitcast.23, f32[64,128]{1,0:T(8,128)} %bitcast.24), custom_call_target="tpu_custom_call" | custom-call | tf_op jit(solution)/shard_map/pallas_call | solution.py:325
  4.1 2.2 %collective-permute-start = (bf16[64,128]{1,0:T(8,128)(2,1)S(1)}, bf16[64,128]{1,0:T(8,128)(2,1)S(1)}, u32[]{:S(2)}, u32[]{:S(2)}) collective-permute-start(bf16[64,128]{1,0:T(8,128)(2,1)S(1)} %get-tuple-element.14), channel_id=1, source_target_pairs={{0,1},{1,0},{2,3},{3,2},{4,5},{5,4},{6,7},{7,6},{8,9},{9,8},{10,11... | collective-permute-start | bytes 49160 | tf_op jit(solution)/shard_map/ppermute | solution.py:323
  6.3 0.0 copy-done.3
  6.3 0.6 %shard_map.114 = (f32[64,128]{1,0:T(8,128)S(1)}, f32[8,128]{1,0:T(8,128)S(1)}) custom-call(f32[16]{0:T(128)S(1)} %copy-done.3, bf16[64,128]{1,0:T(8,128)(2,1)S(1)} %get-tuple-element.11.mine), custom_call_target="tpu_custom_call" | custom-call | tf_op jit(solution)/shard_map/pallas_call | solution.py:350
  6.9 1.1 %collective-permute-done.received = bf16[64,128]{1,0:T(8,128)(2,1)S(1)} collective-permute-done((bf16[64,128]{1,0:T(8,128)(2,1)S(1)}, bf16[64,128]{1,0:T(8,128)(2,1)S(1)}, u32[]{:S(2)}, u32[]{:S(2)}) %collective-permute-start) | collective-permute-done | bytes 16416 | tf_op jit(solution)/shard_map/ppermute | solution.py:323
  8.1 14.2 %all_to_all.10.rows = bf16[8,64,128]{2,1,0:T(8,128)(2,1)S(1)} all-to-all(bf16[8,64,128]{2,1,0:T(8,128)(2,1)S(1)} %shard_map.115), channel_id=1, replica_groups={{0,4,8,12,16,20,24,28},{2,6,10,14,18,22,26,30},{1,5,9,13,17,21,25,29},{..., dimensions={0} | all-to-all | bytes 262144 | tf_op jit(solution)/shard_map/all_to_all | solution.py:360
  22.3 0.0 collective-permute-done.1.other_weight
  22.3 0.0 copy-done
  22.3 0.7 %shard_map.116 = (f32[8,512]{1,0:T(8,128)S(1)}, f32[8,512]{1,0:T(8,128)S(1)}) custom-call(bf16[8,64,128]{2,1,0:T(8,128)(2,1)S(1)} %all_to_all.10.rows, bf16[4096,256]{1,0:T(8,128)(2,1)S(1)} %copy-done, bf16[4096,256]{1,0:T(8,128)(2,1)S(1)} %collective-permute-done.1.other_weight), custom_call_target="tpu_custom_call" | custom-call | tf_op jit(solution)/shard_map/pallas_call | solution.py:361
  22.9 0.9 %collective-permute-start.2 = (f32[8,512]{1,0:T(8,128)S(1)}, f32[8,512]{1,0:T(8,128)S(1)}, u32[]{:S(2)}, u32[]{:S(2)}) collective-permute-start(f32[8,512]{1,0:T(8,128)S(1)} %get-tuple-element.16), channel_id=1, source_target_pairs={{0,1},{1,0},{2,3},{3,2},{4,5},{5,4},{6,7},{7,6},{8,9},{9,8},{10,11... | collective-permute-start | bytes 49160 | tf_op jit(solution)/shard_map/ppermute | solution.py:323
  23.8 0.0 copy-done.1
  23.8 0.0 collective-permute-start.3
  23.8 1.2 %collective-permute-done.3.other_blocks = s32[2,8,8]{2,1,0:T(8,128)S(1)} collective-permute-done((s32[2,8,8]{2,1,0:T(8,128)S(1)}, s32[2,8,8]{2,1,0:T(8,128)S(1)}, u32[]{:S(2)}, u32[]{:S(2)}) %collective-permute-start.3) | collective-permute-done | bytes 544 | tf_op jit(solution)/shard_map/ppermute | solution.py:320
  25.0 1.7 %collective-permute-done.2.received = f32[8,512]{1,0:T(8,128)S(1)} collective-permute-done((f32[8,512]{1,0:T(8,128)S(1)}, f32[8,512]{1,0:T(8,128)S(1)}, u32[]{:S(2)}, u32[]{:S(2)}) %collective-permute-start.2) | collective-permute-done | bytes 16416 | tf_op jit(solution)/shard_map/ppermute | solution.py:323
  26.7 0.0 copy-done.2
  26.7 1.0 %shard_map.117 = (f32[8,256]{1,0:T(8,128)S(1)}, f32[8,256]{1,0:T(8,128)S(1)}, f32[16,1,128]{2,1,0:T(1,128)}) custom-call(f32[8,512]{1,0:T(8,128)S(1)} %get-tuple-element.15.mine, f32[8,512]{1,0:T(8,128)S(1)} %collective-permute-done.2.received, s32[2,8,8]{2,1,0:T(8,128)S(1)} %copy-done.1, s32[2,8,8]{2,1,0:T(8,128)S(1)} %collective-permute-done.3.other_blocks, ...), custom_call_target="tpu_custom_call" | custom-call | tf_op jit(solution)/shard_map/pallas_call | solution.py:368
  27.7 3.5 %all-to-all-start.1 = ((f32[16,1,128]{2,1,0:T(1,128)}), f32[16,1,128]{2,1,0:T(1,128)S(1)}, u32[]{:S(2)}, u32[]{:S(2)}) async-start(f32[16,1,128]{2,1,0:T(1,128)} %get-tuple-element.19), calls=%async_computation.1 | async-start | bytes 16384 | tf_op jit(solution)/shard_map/all_to_all | solution.py:381
  31.2 0.3 collective-permute-start.4
  31.4 0.9 %collective-permute-done.4.received = f32[8,256]{1,0:T(8,128)S(1)} collective-permute-done((f32[8,256]{1,0:T(8,128)S(1)}, f32[8,256]{1,0:T(8,128)S(1)}, u32[]{:S(2)}, u32[]{:S(2)}) %collective-permute-start.4) | collective-permute-done | bytes 8224 | tf_op jit(solution)/shard_map/ppermute | solution.py:320
  32.4 5.1 %all-to-all-done.1.stats = f32[16,1,128]{2,1,0:T(1,128)S(1)} async-done(((f32[16,1,128]{2,1,0:T(1,128)}), f32[16,1,128]{2,1,0:T(1,128)S(1)}, u32[]{:S(2)}, u32[]{:S(2)}) %all-to-all-start.1) | async-done | bytes 8224 | tf_op jit(solution)/shard_map/all_to_all | solution.py:381
  37.4 1.0 %shard_map.118 = (f32[2,8,256]{2,1,0:T(8,128)}, f32[2,8]{1,0:T(2,128)}) custom-call(f32[8,256]{1,0:T(8,128)S(1)} %get-tuple-element.17.guided, f32[8,256]{1,0:T(8,128)S(1)} %collective-permute-done.4.received, f32[16,1,128]{2,1,0:T(1,128)S(1)} %all-to-all-done.1.stats, s32[2,8,8]{2,1,0:T(8,128)S(1)} %copy-done.1), custom_call_target="tpu_custom_call" | custom-call | tf_op jit(solution)/shard_map/pallas_call | solution.py:374
  (3 shorter events, 0.0 us)
Async XLA Ops:
  0.6 21.7 %copy-start = (bf16[4096,256]{1,0:T(8,128)(2,1)S(1)}, bf16[4096,256]{1,0:T(8,128)(2,1)}, u32[]{:S(2)}) copy-start(bf16[4096,256]{1,0:T(8,128)(2,1)} %weight.1) | copy-start | bytes 6291460
  0.6 5.7 %copy-start.3 = (f32[16]{0:T(128)S(1)}, f32[16]{0:T(128)}, u32[]{:S(2)}) copy-start(f32[16]{0:T(128)} %scale.1) | copy-start | bytes 196
  0.7 21.6 %collective-permute-start.1 = (bf16[4096,256]{1,0:T(8,128)(2,1)}, bf16[4096,256]{1,0:T(8,128)(2,1)S(1)}, u32[]{:S(2)}, u32[]{:S(2)}) collective-permute-start(bf16[4096,256]{1,0:T(8,128)(2,1)} %weight.1), channel_id=1, source_target_pairs={{0,2},{2,0},{4,6},{6,4},{8,10},{10,8},{12,14},{14,12},{16,18},{18,... | collective-permute-start | bytes 6291464 | tf_op jit(solution)/shard_map/ppermute | solution.py:320
  4.1 3.9 %collective-permute-start = (bf16[64,128]{1,0:T(8,128)(2,1)S(1)}, bf16[64,128]{1,0:T(8,128)(2,1)S(1)}, u32[]{:S(2)}, u32[]{:S(2)}) collective-permute-start(bf16[64,128]{1,0:T(8,128)(2,1)S(1)} %get-tuple-element.14), channel_id=1, source_target_pairs={{0,1},{1,0},{2,3},{3,2},{4,5},{5,4},{6,7},{7,6},{8,9},{9,8},{10,11... | collective-permute-start | bytes 49160 | tf_op jit(solution)/shard_map/ppermute | solution.py:323
  22.3 1.6 %copy-start.1 = (s32[2,8,8]{2,1,0:T(8,128)S(1)}, s32[2,8,8]{2,1,0:T(8,128)}, u32[]{:S(2)}) copy-start(s32[2,8,8]{2,1,0:T(8,128)} %blocks.3) | copy-start | bytes 1540
  22.3 4.4 %copy-start.2 = (s32[2,8]{1,0:T(2,128)S(1)}, s32[2,8]{1,0:T(2,128)}, u32[]{:S(2)}) copy-start(s32[2,8]{1,0:T(2,128)} %sampled.1) | copy-start | bytes 196
  22.9 3.7 %collective-permute-start.2 = (f32[8,512]{1,0:T(8,128)S(1)}, f32[8,512]{1,0:T(8,128)S(1)}, u32[]{:S(2)}, u32[]{:S(2)}) collective-permute-start(f32[8,512]{1,0:T(8,128)S(1)} %get-tuple-element.16), channel_id=1, source_target_pairs={{0,1},{1,0},{2,3},{3,2},{4,5},{5,4},{6,7},{7,6},{8,9},{9,8},{10,11... | collective-permute-start | bytes 49160 | tf_op jit(solution)/shard_map/ppermute | solution.py:323
  23.8 1.2 %collective-permute-start.3 = (s32[2,8,8]{2,1,0:T(8,128)S(1)}, s32[2,8,8]{2,1,0:T(8,128)S(1)}, u32[]{:S(2)}, u32[]{:S(2)}) collective-permute-start(s32[2,8,8]{2,1,0:T(8,128)S(1)} %copy-done.1), channel_id=1, source_target_pairs={{0,2},{2,0},{4,6},{6,4},{8,10},{10,8},{12,14},{14,12},{16,18},{18,... | collective-permute-start | bytes 1544 | tf_op jit(solution)/shard_map/ppermute | solution.py:320
  27.7 9.8 %all-to-all-start.1 = ((f32[16,1,128]{2,1,0:T(1,128)}), f32[16,1,128]{2,1,0:T(1,128)S(1)}, u32[]{:S(2)}, u32[]{:S(2)}) async-start(f32[16,1,128]{2,1,0:T(1,128)} %get-tuple-element.19), calls=%async_computation.1 | async-start | bytes 16384 | tf_op jit(solution)/shard_map/all_to_all | solution.py:381
  31.2 1.2 %collective-permute-start.4 = (f32[8,256]{1,0:T(8,128)S(1)}, f32[8,256]{1,0:T(8,128)S(1)}, u32[]{:S(2)}, u32[]{:S(2)}) collective-permute-start(f32[8,256]{1,0:T(8,128)S(1)} %get-tuple-element.18), channel_id=1, source_target_pairs={{0,2},{2,0},{4,6},{6,4},{8,10},{10,8},{12,14},{14,12},{16,18},{18,... | collective-permute-start | bytes 24584 | tf_op jit(solution)/shard_map/ppermute | solution.py:320

commit v11 on v8

--- a/solution.py
+++ b/solution.py
@@ -33,7 +33,7 @@
         kernel,
         out_shape=out_shape,
         in_specs=in_specs,
-        out_specs=jax.tree.map(lambda _: in_vmem(), out_shape),
+        out_specs=jax.tree.map(lambda _: in_vmem(), out_shape, is_leaf=lambda x: hasattr(x, 'shape')),
         scratch_shapes=list(scratch),
         compiler_params=pltpu.CompilerParams(vmem_limit_bytes=limit),
         cost_estimate=cost,
@@ -321,7 +321,7 @@
 
     mine, theirs = call(
         attend_kernel,
-        (half_rows, half_rows),
+        (pltpu.VMEM(half_rows.shape, half_rows.dtype), pltpu.VMEM(half_rows.shape, half_rows.dtype)),
         [smem] + [hbm] * 5,
         [
             pltpu.VMEM(cache_rows.shape, jnp.bfloat16),

time: 37.7 us -> 36.7 us (0.973)
  local copies, waits for them, and re-layouts: 0.73 us -> 0.02 us
  starting transfers between devices: 5.36 us -> 4.97 us
    unnamed x10 -> x8, local copies, waits for them, and re-layouts: 0.73 us -> 0.02 us
    ppermute x2, starting transfers between devices: 4.77 us -> 4.38 us  [swap(): return lax.ppermute(array, 'pair', [(0, 1), (1, 0)])]
where the time goes in v11:
time: 36.7 us; the launch traced here: 36.5 us
  blocking collectives  22.3 us (61%)
  starting transfers between devices  4.97 us (14%)
  Pallas kernels  4.79 us (13%)
  waiting for transfers between devices  3 us (8%)
  between operations  1.38 us (4%)
    all_to_all x1, blocking collectives, shards(): lax.all_to_all(spread, 'wide', 0, 0, axis_index_groups=same_core, tiled=T...  13.1 us
    all_to_all x1, blocking collectives, shards(): lax.all_to_all(stats, 'wide', 0, 0, tiled=True)  9.2 us
    ppermute x2, starting transfers between devices, swap(): return lax.ppermute(array, 'pair', [(0, 1), (1, 0)])  4.38 us
    pallas_call x1, Pallas kernels, shards(): call(attend_kernel, (pltpu.VMEM(half_rows.shape, half_rows.dtype), pltpu....  2.44 us
    ppermute x2, waiting for transfers between devices, swap(): return lax.ppermute(array, 'pair', [(0, 1), (1, 0)])  1.83 us
    ppermute x3, waiting for transfers between devices, other_core(): lax.ppermute(array, 'wide', [(source, source ^ 1) for source in range(wid...  1.17 us
    pallas_call x1, Pallas kernels, shards(): call(finish_kernel, (jax.ShapeDtypeStruct((steps, half_pairs, width), jnp...  0.82 us
  transfers between devices with their start and end apart: 5, of which 3 were waited for; matrix products, arithmetic and copies ran while one was open for 0% of the time, Pallas kernels for 8%

profile of v11, /device:TPU:0, one launch (start us, length us, event | category | flops | bytes accessed | tf_op | source)
XLA Modules:
  0.0 36.5 jit_solution(15984814367166374628)
XLA Ops:
  0.6 0.0 copy-start
  0.6 0.0 copy-start.3
  0.7 0.5 %collective-permute-start.1 = (bf16[4096,256]{1,0:T(8,128)(2,1)}, bf16[4096,256]{1,0:T(8,128)(2,1)S(1)}, u32[]{:S(2)}, u32[]{:S(2)}) collective-permute-start(bf16[4096,256]{1,0:T(8,128)(2,1)} %weight.1), channel_id=1, source_target_pairs={{0,2},{2,0},{4,6},{6,4},{8,10},{10,8},{12,14},{14,12},{16,18},{18,... | collective-permute-start | bytes 6291464 | tf_op jit(solution)/shard_map/ppermute | solution.py:317
  1.9 2.4 %shard_map.113 = (bf16[64,128]{1,0:T(8,128)(2,1)S(1)}, bf16[64,128]{1,0:T(8,128)(2,1)S(1)}) custom-call(s32[1,1]{1,0:T(1,128)S(6)} %copy.16.lengths, bf16[128,128]{1,0:T(8,128)(2,1)} %bitcast.22, bf16[8192,128]{1,0:T(8,128)(2,1)} %bitcast.21, bf16[32,128]{1,0:T(8,128)(2,1)} %bitcast.25, bf16[128,128]{1,0:T(8,128)(2,1)} %bitcast.23, f32[64,128]{1,0:T(8,128)} %bitcast.24), custom_call_target="tpu_custom_call" | custom-call | tf_op jit(solution)/shard_map/pallas_call | solution.py:322
  4.3 2.5 %collective-permute-start = (bf16[64,128]{1,0:T(8,128)(2,1)S(1)}, bf16[64,128]{1,0:T(8,128)(2,1)S(1)}, u32[]{:S(2)}, u32[]{:S(2)}) collective-permute-start(bf16[64,128]{1,0:T(8,128)(2,1)S(1)} %get-tuple-element.14), channel_id=1, source_target_pairs={{0,1},{1,0},{2,3},{3,2},{4,5},{5,4},{6,7},{7,6},{8,9},{9,8},{10,11... | collective-permute-start | bytes 49160 | tf_op jit(solution)/shard_map/ppermute | solution.py:320
  6.8 0.0 copy-done.3
  6.8 0.6 %shard_map.114 = (f32[64,128]{1,0:T(8,128)S(1)}, f32[8,128]{1,0:T(8,128)S(1)}) custom-call(f32[16]{0:T(128)S(1)} %copy-done.3, bf16[64,128]{1,0:T(8,128)(2,1)S(1)} %get-tuple-element.11.mine), custom_call_target="tpu_custom_call" | custom-call | tf_op jit(solution)/shard_map/pallas_call | solution.py:347
  7.4 1.1 %collective-permute-done.received = bf16[64,128]{1,0:T(8,128)(2,1)S(1)} collective-permute-done((bf16[64,128]{1,0:T(8,128)(2,1)S(1)}, bf16[64,128]{1,0:T(8,128)(2,1)S(1)}, u32[]{:S(2)}, u32[]{:S(2)}) %collective-permute-start) | collective-permute-done | bytes 16416 | tf_op jit(solution)/shard_map/ppermute | solution.py:320
  8.5 13.1 %all_to_all.10.rows = bf16[8,64,128]{2,1,0:T(8,128)(2,1)S(1)} all-to-all(bf16[8,64,128]{2,1,0:T(8,128)(2,1)S(1)} %shard_map.115), channel_id=1, replica_groups={{0,4,8,12,16,20,24,28},{2,6,10,14,18,22,26,30},{1,5,9,13,17,21,25,29},{..., dimensions={0} | all-to-all | bytes 262144 | tf_op jit(solution)/shard_map/all_to_all | solution.py:357
  21.6 0.0 copy-start.1
  21.7 0.0 collective-permute-done.1.other_weight
  21.7 0.0 copy-done
  21.7 0.7 %shard_map.116 = (f32[8,512]{1,0:T(8,128)S(1)}, f32[8,512]{1,0:T(8,128)S(1)}) custom-call(bf16[8,64,128]{2,1,0:T(8,128)(2,1)S(1)} %all_to_all.10.rows, bf16[4096,256]{1,0:T(8,128)(2,1)S(1)} %copy-done, bf16[4096,256]{1,0:T(8,128)(2,1)S(1)} %collective-permute-done.1.other_weight), custom_call_target="tpu_custom_call" | custom-call | tf_op jit(solution)/shard_map/pallas_call | solution.py:358
  22.3 1.9 %collective-permute-start.2 = (f32[8,512]{1,0:T(8,128)S(1)}, f32[8,512]{1,0:T(8,128)S(1)}, u32[]{:S(2)}, u32[]{:S(2)}) collective-permute-start(f32[8,512]{1,0:T(8,128)S(1)} %get-tuple-element.16), channel_id=1, source_target_pairs={{0,1},{1,0},{2,3},{3,2},{4,5},{5,4},{6,7},{7,6},{8,9},{9,8},{10,11... | collective-permute-start | bytes 49160 | tf_op jit(solution)/shard_map/ppermute | solution.py:320
  24.2 0.0 copy-done.1
  24.2 0.0 collective-permute-start.3
  24.2 1.2 %collective-permute-done.3.other_blocks = s32[2,8,8]{2,1,0:T(8,128)S(1)} collective-permute-done((s32[2,8,8]{2,1,0:T(8,128)S(1)}, s32[2,8,8]{2,1,0:T(8,128)S(1)}, u32[]{:S(2)}, u32[]{:S(2)}) %collective-permute-start.3) | collective-permute-done | bytes 544 | tf_op jit(solution)/shard_map/ppermute | solution.py:317
  25.4 0.7 %collective-permute-done.2.received = f32[8,512]{1,0:T(8,128)S(1)} collective-permute-done((f32[8,512]{1,0:T(8,128)S(1)}, f32[8,512]{1,0:T(8,128)S(1)}, u32[]{:S(2)}, u32[]{:S(2)}) %collective-permute-start.2) | collective-permute-done | bytes 16416 | tf_op jit(solution)/shard_map/ppermute | solution.py:320
  26.1 0.0 copy-done.2
  26.1 0.3 shard_map.117
  26.4 0.1 collective-permute-start.4
  26.5 9.2 %all_to_all.11.stats = f32[16,3,8]{2,1,0:T(4,128)S(1)} all-to-all(f32[16,3,8]{2,1,0:T(4,128)S(1)} %get-tuple-element.19), channel_id=1, replica_groups=mesh['wide'=16,'pair'=2] {'wide'}, dimensions={0} | all-to-all | bytes 3072 | tf_op jit(solution)/shard_map/all_to_all | solution.py:377
  35.7 0.0 collective-permute-done.4.received
  35.7 0.8 %shard_map.118 = (f32[2,8,256]{2,1,0:T(8,128)}, f32[2,8]{1,0:T(2,128)}) custom-call(f32[8,256]{1,0:T(8,128)S(1)} %get-tuple-element.17.guided, f32[8,256]{1,0:T(8,128)S(1)} %collective-permute-done.4.received, f32[16,3,8]{2,1,0:T(4,128)S(1)} %all_to_all.11.stats, s32[2,8,8]{2,1,0:T(8,128)S(1)} %copy-done.1), custom_call_target="tpu_custom_call" | custom-call | tf_op jit(solution)/shard_map/pallas_call | solution.py:370
  (2 shorter events, 0.0 us)
Async XLA Ops:
  0.6 21.0 %copy-start = (bf16[4096,256]{1,0:T(8,128)(2,1)S(1)}, bf16[4096,256]{1,0:T(8,128)(2,1)}, u32[]{:S(2)}) copy-start(bf16[4096,256]{1,0:T(8,128)(2,1)} %weight.1) | copy-start | bytes 6291460
  0.6 6.2 %copy-start.3 = (f32[16]{0:T(128)S(1)}, f32[16]{0:T(128)}, u32[]{:S(2)}) copy-start(f32[16]{0:T(128)} %scale.1) | copy-start | bytes 196
  0.7 21.0 %collective-permute-start.1 = (bf16[4096,256]{1,0:T(8,128)(2,1)}, bf16[4096,256]{1,0:T(8,128)(2,1)S(1)}, u32[]{:S(2)}, u32[]{:S(2)}) collective-permute-start(bf16[4096,256]{1,0:T(8,128)(2,1)} %weight.1), channel_id=1, source_target_pairs={{0,2},{2,0},{4,6},{6,4},{8,10},{10,8},{12,14},{14,12},{16,18},{18,... | collective-permute-start | bytes 6291464 | tf_op jit(solution)/shard_map/ppermute | solution.py:317
  4.3 4.2 %collective-permute-start = (bf16[64,128]{1,0:T(8,128)(2,1)S(1)}, bf16[64,128]{1,0:T(8,128)(2,1)S(1)}, u32[]{:S(2)}, u32[]{:S(2)}) collective-permute-start(bf16[64,128]{1,0:T(8,128)(2,1)S(1)} %get-tuple-element.14), channel_id=1, source_target_pairs={{0,1},{1,0},{2,3},{3,2},{4,5},{5,4},{6,7},{7,6},{8,9},{9,8},{10,11... | collective-permute-start | bytes 49160 | tf_op jit(solution)/shard_map/ppermute | solution.py:320
  21.6 2.6 %copy-start.1 = (s32[2,8,8]{2,1,0:T(8,128)S(1)}, s32[2,8,8]{2,1,0:T(8,128)}, u32[]{:S(2)}) copy-start(s32[2,8,8]{2,1,0:T(8,128)} %blocks.3) | copy-start | bytes 1540
  21.6 4.4 %copy-start.2 = (s32[2,8]{1,0:T(2,128)S(1)}, s32[2,8]{1,0:T(2,128)}, u32[]{:S(2)}) copy-start(s32[2,8]{1,0:T(2,128)} %sampled.1) | copy-start | bytes 196
  22.3 3.7 %collective-permute-start.2 = (f32[8,512]{1,0:T(8,128)S(1)}, f32[8,512]{1,0:T(8,128)S(1)}, u32[]{:S(2)}, u32[]{:S(2)}) collective-permute-start(f32[8,512]{1,0:T(8,128)S(1)} %get-tuple-element.16), channel_id=1, source_target_pairs={{0,1},{1,0},{2,3},{3,2},{4,5},{5,4},{6,7},{7,6},{8,9},{9,8},{10,11... | collective-permute-start | bytes 49160 | tf_op jit(solution)/shard_map/ppermute | solution.py:320
  24.2 1.2 %collective-permute-start.3 = (s32[2,8,8]{2,1,0:T(8,128)S(1)}, s32[2,8,8]{2,1,0:T(8,128)S(1)}, u32[]{:S(2)}, u32[]{:S(2)}) collective-permute-start(s32[2,8,8]{2,1,0:T(8,128)S(1)} %copy-done.1), channel_id=1, source_target_pairs={{0,2},{2,0},{4,6},{6,4},{8,10},{10,8},{12,14},{14,12},{16,18},{18,... | collective-permute-start | bytes 1544 | tf_op jit(solution)/shard_map/ppermute | solution.py:317
  26.4 9.3 %collective-permute-start.4 = (f32[8,256]{1,0:T(8,128)S(1)}, f32[8,256]{1,0:T(8,128)S(1)}, u32[]{:S(2)}, u32[]{:S(2)}) collective-permute-start(f32[8,256]{1,0:T(8,128)S(1)} %get-tuple-element.18), channel_id=1, source_target_pairs={{0,2},{2,0},{4,6},{6,4},{8,10},{10,8},{12,14},{14,12},{16,18},{18,... | collective-permute-start | bytes 24584 | tf_op jit(solution)/shard_map/ppermute | solution.py:317

commit v12 on v9

--- a/solution.py
+++ b/solution.py
@@ -127,7 +127,7 @@
         power = jnp.sum(jnp.where(step_of_row == step, row_power, 0.0), axis=0, keepdims=True)
         power = power / (QUERY_HEADS * HEAD_SIZE)
         scale = jnp.where(step_of_row == step, lax.rsqrt(power + 1e-05), scale)
-    normed = (hidden * scale * gain_rows[...]).astype(jnp.bfloat16)
+    normed = (hidden * scale * gain_rows[pl.ds(0, hidden.shape[0]), :]).astype(jnp.bfloat16)
     half = normed.shape[0] // 2
     first = lax.axis_index("pair") == 0
     mine[...] = jnp.where(first, normed[:half], normed[half:])
@@ -319,8 +319,8 @@
         [smem] + [hbm] * 5,
         [
             pltpu.VMEM(cache_rows.shape, jnp.bfloat16),
-            pltpu.VMEM((cache.shape[2] * SLOT_PITCH, HEAD_SIZE), jnp.float32),
-            pltpu.VMEM((rows, HEAD_SIZE), jnp.float32),
+            pltpu.VMEM(((cache.shape[2] + 8) * SLOT_PITCH, HEAD_SIZE), jnp.float32),
+            pltpu.VMEM((rows + 8, HEAD_SIZE), jnp.float32),
             pltpu.VMEM((rows, HEAD_SIZE), jnp.bfloat16),
             pltpu.VMEM((steps * SLOT_ROWS, HEAD_SIZE), jnp.bfloat16),
             pltpu.VMEM((rows, HEAD_SIZE), jnp.bfloat16),
@@ -352,7 +352,7 @@
         project_kernel,
         (flat_two, flat_two),
         [vmem] * 3,
-        [pltpu.VMEM((chips * (rows // 2 + 1), HEAD_SIZE), jnp.float32)],
+        [pltpu.VMEM(((chips + 8) * (rows // 2 + 1), HEAD_SIZE), jnp.float32)],
     )(gathered, vocab_weight, other_weight)
     guided, other_guided, stats = call(
         stats_kernel,

time: 36.8 us -> 36.7 us (level)
  starting transfers between devices: 4.43 us -> 4.82 us
    ppermute x2, starting transfers between devices: 3.84 us -> 4.23 us  [swap(): return lax.ppermute(array, 'pair', [(0, 1), (1, 0)])]
  transfers between devices with their start and end apart: 5 -> 5, of which waited for: 3 -> 3; matrix products, arithmetic and copies ran while one was open for 0% -> 0% of each run, Pallas kernels for 8% -> 7%
where the time goes in v12:
time: 36.7 us; the launch traced here: 36.5 us
  blocking collectives  22.5 us (61%)
  starting transfers between devices  4.82 us (13%)
  Pallas kernels  4.36 us (12%)
  waiting for transfers between devices  3.4 us (9%)
  between operations  1.38 us (4%)
    all_to_all x1, blocking collectives, shards(): lax.all_to_all(spread, 'wide', 0, 0, axis_index_groups=same_core, tiled=T...  13.3 us
    all_to_all x1, blocking collectives, shards(): lax.all_to_all(stats, 'wide', 0, 0, tiled=True)  9.2 us
    ppermute x2, starting transfers between devices, swap(): return lax.ppermute(array, 'pair', [(0, 1), (1, 0)])  4.23 us
    ppermute x2, waiting for transfers between devices, swap(): return lax.ppermute(array, 'pair', [(0, 1), (1, 0)])  2.22 us
    pallas_call x1, Pallas kernels, shards(): call(attend_kernel, (pltpu.VMEM(half_rows.shape, half_rows.dtype), pltpu....  2.01 us
    ppermute x3, waiting for transfers between devices, other_core(): lax.ppermute(array, 'wide', [(source, source ^ 1) for source in range(wid...  1.17 us
    pallas_call x1, Pallas kernels, shards(): call(finish_kernel, (jax.ShapeDtypeStruct((steps, half_pairs, width), jnp...  0.82 us
  transfers between devices with their start and end apart: 5, of which 3 were waited for; matrix products, arithmetic and copies ran while one was open for 0% of the time, Pallas kernels for 7%

profile of v12, /device:TPU:0, one launch (start us, length us, event | category | flops | bytes accessed | tf_op | source)
XLA Modules:
  0.0 36.5 jit_solution(7777612762651454855)
XLA Ops:
  0.6 0.0 copy-start
  0.6 0.0 copy-start.3
  0.7 0.5 %collective-permute-start.1 = (bf16[4096,256]{1,0:T(8,128)(2,1)}, bf16[4096,256]{1,0:T(8,128)(2,1)S(1)}, u32[]{:S(2)}, u32[]{:S(2)}) collective-permute-start(bf16[4096,256]{1,0:T(8,128)(2,1)} %weight.1), channel_id=1, source_target_pairs={{0,2},{2,0},{4,6},{6,4},{8,10},{10,8},{12,14},{14,12},{16,18},{18,... | collective-permute-start | bytes 6291464 | tf_op jit(solution)/shard_map/ppermute | solution.py:311
  1.9 2.0 %shard_map.113 = (bf16[64,128]{1,0:T(8,128)(2,1)S(1)}, bf16[64,128]{1,0:T(8,128)(2,1)S(1)}) custom-call(s32[1,1]{1,0:T(1,128)S(6)} %copy.16.lengths, bf16[128,128]{1,0:T(8,128)(2,1)} %bitcast.22, bf16[8192,128]{1,0:T(8,128)(2,1)} %bitcast.21, bf16[32,128]{1,0:T(8,128)(2,1)} %bitcast.25, bf16[128,128]{1,0:T(8,128)(2,1)} %bitcast.23, f32[64,128]{1,0:T(8,128)} %bitcast.24), custom_call_target="tpu_custom_call" | custom-call | tf_op jit(solution)/shard_map/pallas_call | solution.py:316
  3.9 2.7 %collective-permute-start = (bf16[64,128]{1,0:T(8,128)(2,1)S(1)}, bf16[64,128]{1,0:T(8,128)(2,1)S(1)}, u32[]{:S(2)}, u32[]{:S(2)}) collective-permute-start(bf16[64,128]{1,0:T(8,128)(2,1)S(1)} %get-tuple-element.14), channel_id=1, source_target_pairs={{0,1},{1,0},{2,3},{3,2},{4,5},{5,4},{6,7},{7,6},{8,9},{9,8},{10,11... | collective-permute-start | bytes 49160 | tf_op jit(solution)/shard_map/ppermute | solution.py:314
  6.6 0.0 copy-done.3
  6.6 0.6 %shard_map.114 = (f32[64,128]{1,0:T(8,128)S(1)}, f32[8,128]{1,0:T(8,128)S(1)}) custom-call(f32[16]{0:T(128)S(1)} %copy-done.3, bf16[64,128]{1,0:T(8,128)(2,1)S(1)} %get-tuple-element.11.mine), custom_call_target="tpu_custom_call" | custom-call | tf_op jit(solution)/shard_map/pallas_call | solution.py:340
  7.2 1.1 %collective-permute-done.received = bf16[64,128]{1,0:T(8,128)(2,1)S(1)} collective-permute-done((bf16[64,128]{1,0:T(8,128)(2,1)S(1)}, bf16[64,128]{1,0:T(8,128)(2,1)S(1)}, u32[]{:S(2)}, u32[]{:S(2)}) %collective-permute-start) | collective-permute-done | bytes 16416 | tf_op jit(solution)/shard_map/ppermute | solution.py:314
  8.3 13.3 %all_to_all.10.rows = bf16[8,64,128]{2,1,0:T(8,128)(2,1)S(1)} all-to-all(bf16[8,64,128]{2,1,0:T(8,128)(2,1)S(1)} %shard_map.115), channel_id=1, replica_groups={{0,4,8,12,16,20,24,28},{2,6,10,14,18,22,26,30},{1,5,9,13,17,21,25,29},{..., dimensions={0} | all-to-all | bytes 262144 | tf_op jit(solution)/shard_map/all_to_all | solution.py:350
  21.7 0.0 copy-start.1
  21.7 0.0 collective-permute-done.1.other_weight
  21.7 0.0 copy-done
  21.7 0.7 %shard_map.116 = (f32[8,512]{1,0:T(8,128)S(1)}, f32[8,512]{1,0:T(8,128)S(1)}) custom-call(bf16[8,64,128]{2,1,0:T(8,128)(2,1)S(1)} %all_to_all.10.rows, bf16[4096,256]{1,0:T(8,128)(2,1)S(1)} %copy-done, bf16[4096,256]{1,0:T(8,128)(2,1)S(1)} %collective-permute-done.1.other_weight), custom_call_target="tpu_custom_call" | custom-call | tf_op jit(solution)/shard_map/pallas_call | solution.py:351
  22.4 1.5 %collective-permute-start.2 = (f32[8,512]{1,0:T(8,128)S(1)}, f32[8,512]{1,0:T(8,128)S(1)}, u32[]{:S(2)}, u32[]{:S(2)}) collective-permute-start(f32[8,512]{1,0:T(8,128)S(1)} %get-tuple-element.16), channel_id=1, source_target_pairs={{0,1},{1,0},{2,3},{3,2},{4,5},{5,4},{6,7},{7,6},{8,9},{9,8},{10,11... | collective-permute-start | bytes 49160 | tf_op jit(solution)/shard_map/ppermute | solution.py:314
  23.9 0.0 copy-done.1
  23.9 0.0 collective-permute-start.3
  23.9 1.2 %collective-permute-done.3.other_blocks = s32[2,8,8]{2,1,0:T(8,128)S(1)} collective-permute-done((s32[2,8,8]{2,1,0:T(8,128)S(1)}, s32[2,8,8]{2,1,0:T(8,128)S(1)}, u32[]{:S(2)}, u32[]{:S(2)}) %collective-permute-start.3) | collective-permute-done | bytes 544 | tf_op jit(solution)/shard_map/ppermute | solution.py:311
  25.0 1.1 %collective-permute-done.2.received = f32[8,512]{1,0:T(8,128)S(1)} collective-permute-done((f32[8,512]{1,0:T(8,128)S(1)}, f32[8,512]{1,0:T(8,128)S(1)}, u32[]{:S(2)}, u32[]{:S(2)}) %collective-permute-start.2) | collective-permute-done | bytes 16416 | tf_op jit(solution)/shard_map/ppermute | solution.py:314
  26.1 0.0 copy-done.2
  26.1 0.3 shard_map.117
  26.4 0.1 collective-permute-start.4
  26.5 9.2 %all_to_all.11.stats = f32[16,3,8]{2,1,0:T(4,128)S(1)} all-to-all(f32[16,3,8]{2,1,0:T(4,128)S(1)} %get-tuple-element.19), channel_id=1, replica_groups=mesh['wide'=16,'pair'=2] {'wide'}, dimensions={0} | all-to-all | bytes 3072 | tf_op jit(solution)/shard_map/all_to_all | solution.py:370
  35.7 0.0 collective-permute-done.4.received
  35.7 0.8 %shard_map.118 = (f32[2,8,256]{2,1,0:T(8,128)}, f32[2,8]{1,0:T(2,128)}) custom-call(f32[8,256]{1,0:T(8,128)S(1)} %get-tuple-element.17.guided, f32[8,256]{1,0:T(8,128)S(1)} %collective-permute-done.4.received, f32[16,3,8]{2,1,0:T(4,128)S(1)} %all_to_all.11.stats, s32[2,8,8]{2,1,0:T(8,128)S(1)} %copy-done.1), custom_call_target="tpu_custom_call" | custom-call | tf_op jit(solution)/shard_map/pallas_call | solution.py:363
  (2 shorter events, 0.0 us)
Async XLA Ops:
  0.6 21.1 %copy-start = (bf16[4096,256]{1,0:T(8,128)(2,1)S(1)}, bf16[4096,256]{1,0:T(8,128)(2,1)}, u32[]{:S(2)}) copy-start(bf16[4096,256]{1,0:T(8,128)(2,1)} %weight.1) | copy-start | bytes 6291460
  0.6 6.0 %copy-start.3 = (f32[16]{0:T(128)S(1)}, f32[16]{0:T(128)}, u32[]{:S(2)}) copy-start(f32[16]{0:T(128)} %scale.1) | copy-start | bytes 196
  0.7 21.0 %collective-permute-start.1 = (bf16[4096,256]{1,0:T(8,128)(2,1)}, bf16[4096,256]{1,0:T(8,128)(2,1)S(1)}, u32[]{:S(2)}, u32[]{:S(2)}) collective-permute-start(bf16[4096,256]{1,0:T(8,128)(2,1)} %weight.1), channel_id=1, source_target_pairs={{0,2},{2,0},{4,6},{6,4},{8,10},{10,8},{12,14},{14,12},{16,18},{18,... | collective-permute-start | bytes 6291464 | tf_op jit(solution)/shard_map/ppermute | solution.py:311
  3.9 4.4 %collective-permute-start = (bf16[64,128]{1,0:T(8,128)(2,1)S(1)}, bf16[64,128]{1,0:T(8,128)(2,1)S(1)}, u32[]{:S(2)}, u32[]{:S(2)}) collective-permute-start(bf16[64,128]{1,0:T(8,128)(2,1)S(1)} %get-tuple-element.14), channel_id=1, source_target_pairs={{0,1},{1,0},{2,3},{3,2},{4,5},{5,4},{6,7},{7,6},{8,9},{9,8},{10,11... | collective-permute-start | bytes 49160 | tf_op jit(solution)/shard_map/ppermute | solution.py:314
  21.7 2.2 %copy-start.1 = (s32[2,8,8]{2,1,0:T(8,128)S(1)}, s32[2,8,8]{2,1,0:T(8,128)}, u32[]{:S(2)}) copy-start(s32[2,8,8]{2,1,0:T(8,128)} %blocks.3) | copy-start | bytes 1540
  21.7 4.4 %copy-start.2 = (s32[2,8]{1,0:T(2,128)S(1)}, s32[2,8]{1,0:T(2,128)}, u32[]{:S(2)}) copy-start(s32[2,8]{1,0:T(2,128)} %sampled.1) | copy-start | bytes 196
  22.4 3.7 %collective-permute-start.2 = (f32[8,512]{1,0:T(8,128)S(1)}, f32[8,512]{1,0:T(8,128)S(1)}, u32[]{:S(2)}, u32[]{:S(2)}) collective-permute-start(f32[8,512]{1,0:T(8,128)S(1)} %get-tuple-element.16), channel_id=1, source_target_pairs={{0,1},{1,0},{2,3},{3,2},{4,5},{5,4},{6,7},{7,6},{8,9},{9,8},{10,11... | collective-permute-start | bytes 49160 | tf_op jit(solution)/shard_map/ppermute | solution.py:314
  23.9 1.2 %collective-permute-start.3 = (s32[2,8,8]{2,1,0:T(8,128)S(1)}, s32[2,8,8]{2,1,0:T(8,128)S(1)}, u32[]{:S(2)}, u32[]{:S(2)}) collective-permute-start(s32[2,8,8]{2,1,0:T(8,128)S(1)} %copy-done.1), channel_id=1, source_target_pairs={{0,2},{2,0},{4,6},{6,4},{8,10},{10,8},{12,14},{14,12},{16,18},{18,... | collective-permute-start | bytes 1544 | tf_op jit(solution)/shard_map/ppermute | solution.py:311
  26.4 9.3 %collective-permute-start.4 = (f32[8,256]{1,0:T(8,128)S(1)}, f32[8,256]{1,0:T(8,128)S(1)}, u32[]{:S(2)}, u32[]{:S(2)}) collective-permute-start(f32[8,256]{1,0:T(8,128)S(1)} %get-tuple-element.18), channel_id=1, source_target_pairs={{0,2},{2,0},{4,6},{6,4},{8,10},{10,8},{12,14},{14,12},{16,18},{18,... | collective-permute-start | bytes 24584 | tf_op jit(solution)/shard_map/ppermute | solution.py:311
